TPU v7x, 512 devices: a whole 4x4x16 slice. The times are simulated.
512 devices in a mesh: member: 16 (over x, y_hi, core), grid: 32 (over y_lo, z).
Axes of the slice: x: 4, y: 4 (y_hi: 2, y_lo: 2; y = y_hi * 2 + y_lo), z: 16, core: 2. Of those that a mesh axis runs over, the one named last changes fastest.
Arguments:
- mesh_latent: bfloat16 [16, 8192, 1024], P('member', 'grid'), may hold values from -6 to 6
- grid_latent: bfloat16 [8192, 1024], P('grid'), may hold values from -6 to 6
- node_weight: bfloat16 [1024, 1024], replicated, may hold values from -0.1875 to 0.1875
- out_weight: bfloat16 [100, 1024], replicated, may hold values from -0.1875 to 0.1875
- target: float32 [100, 8192], P(None, 'grid'), may hold values from -6 to 6
- area_weight: float32 [8192], P('grid'), may hold values from 0.3 to 3
- var_weight: float32 [100], replicated, may hold values from 0.2 to 2
- edge_src: int32 [32, 3, 512], P('grid'), may hold values from 0 to 255
- edge_dst: int32 [32, 3, 512], P('grid'), may hold values from 0 to 255
- edge_count: int32 [32, 3], P('grid'), may hold values from 1 to 512, as said below
Outputs:
- grad_mesh: bfloat16 [16, 8192, 1024], P('member', 'grid')
- grad_grid: bfloat16 [8192, 1024], P('grid', 'member')
Inputs may be any that keep to these rules, and one draw needn't show every extreme that they name: Each destination shard takes edges only from its own shard and its two neighbours along the closed band of shards, as the offsets say; slots c with c >= edge_count[d, o] carry no edge; in every draw some destination shard has all 512 slots used for all three offsets.
All inputs are finite; a program needn't handle non-finite values.
Results may differ from a plain program's by a relative error of at most 0.0087.
Values may be sent and summed in bfloat16 or wider, within the bound.
No kernel may reach another device: no remote copies, remote signals or barrier semaphores. Data moves between devices by JAX's collectives and lax.ppermute only.
A program may use at most 64 MiB of HBM per device.

v0:
```python
import jax
import jax.numpy as jnp
from jax import lax
from jax.sharding import PartitionSpec as P

SMOOTH = 0.1
ALPHA = 0.95
EPS = 1e-05


def from_behind(value, axis, steps):
    count = lax.axis_size(axis)
    pairs = [(source, (source + steps) % count) for source in range(count)]
    return lax.ppermute(value, axis, pairs)


def smooth_slope(difference):
    return difference / jnp.sqrt(difference * difference + SMOOTH * SMOOTH)


def decode_forward(gathered, grid_latent, node_weight, out_weight):
    summed = gathered + grid_latent.astype(jnp.float32)
    centered = summed - jnp.mean(summed, axis=-1, keepdims=True)
    inverse = lax.rsqrt(jnp.mean(centered * centered, axis=-1, keepdims=True) + EPS)
    normed = centered * inverse
    pre_act = jnp.dot(normed.astype(jnp.bfloat16), node_weight, preferred_element_type=jnp.float32)
    hidden = jax.nn.silu(pre_act).astype(jnp.bfloat16)
    predicted = lax.dot_general(
        out_weight, hidden, (((1,), (1,)), ((), ())), preferred_element_type=jnp.float32
    )
    return (predicted, normed, inverse, pre_act)


def decode_backward(grad_pred, normed, inverse, pre_act, node_weight, out_weight):
    grad_hidden = lax.dot_general(
        grad_pred.astype(jnp.bfloat16),
        out_weight,
        (((0,), (0,)), ((), ())),
        preferred_element_type=jnp.float32,
    )
    gate_sig = jax.nn.sigmoid(pre_act)
    grad_pre = (grad_hidden * gate_sig * (1.0 + pre_act * (1.0 - gate_sig))).astype(jnp.bfloat16)
    grad_normed = lax.dot_general(
        grad_pre, node_weight, (((1,), (1,)), ((), ())), preferred_element_type=jnp.float32
    )
    return inverse * (
        grad_normed
        - jnp.mean(grad_normed, axis=-1, keepdims=True)
        - normed * jnp.mean(grad_normed * normed, axis=-1, keepdims=True)
    )


def one_hot_rows(picks, count):
    return (picks[:, None] == jnp.arange(count, dtype=jnp.int32)[None, :]).astype(jnp.bfloat16)


def select_rows(hot, rows):
    return jnp.dot(hot, rows, preferred_element_type=jnp.float32)


def spread_back(hot, grads):
    return lax.dot_general(hot, grads, (((0,), (0,)), ((), ())), preferred_element_type=jnp.float32)


def per_device(
    mesh_latent,
    grid_latent,
    node_weight,
    out_weight,
    target,
    area_weight,
    var_weight,
    edge_src,
    edge_dst,
    edge_count,
):
    members = lax.axis_size("member")
    latent = mesh_latent[0]
    mesh_rows = latent.shape[0]
    grid_rows = grid_latent.shape[0]
    width = latent.shape[1]
    capacity = edge_dst.shape[2]
    slot_live = (jnp.arange(capacity, dtype=jnp.int32)[None, :] < edge_count[0][:, None]).reshape(
        -1
    )
    target_pick = edge_dst[0].reshape(-1)
    target_hot = (
        (jnp.arange(grid_rows, dtype=jnp.int32)[:, None] == target_pick[None, :])
        & slot_live[None, :]
    ).astype(jnp.bfloat16)
    from_right_picks = from_behind(edge_src[0, 2], "grid", -1)
    from_left_picks = from_behind(edge_src[0, 0], "grid", 1)
    own_hot = one_hot_rows(edge_src[0, 1], mesh_rows)
    right_hot = one_hot_rows(from_right_picks, mesh_rows)
    left_hot = one_hot_rows(from_left_picks, mesh_rows)
    to_right = select_rows(right_hot, latent).astype(jnp.bfloat16)
    to_left = select_rows(left_hot, latent).astype(jnp.bfloat16)
    own_rows = select_rows(own_hot, latent).astype(jnp.bfloat16)
    arrive_left = from_behind(to_right, "grid", 1)
    arrive_right = from_behind(to_left, "grid", -1)
    incoming = jnp.concatenate([arrive_right, own_rows, arrive_left], axis=0)
    gathered = jnp.dot(target_hot, incoming, preferred_element_type=jnp.float32)
    predicted, normed, inverse, pre_act = decode_forward(
        gathered, grid_latent, node_weight, out_weight
    )
    pair_sum = jnp.sum(
        smooth_slope(
            predicted[None] - lax.all_gather(predicted[None], "member", axis=0, tiled=True)
        ),
        axis=0,
    )
    pair_scale = (1.0 - (1.0 - ALPHA) / members) / (members - 1)
    grad_pred = (
        area_weight[None, :]
        * var_weight[:, None]
        * (smooth_slope(predicted - target) - pair_scale * pair_sum)
    )
    grad_summed = decode_backward(grad_pred, normed, inverse, pre_act, node_weight, out_weight)
    slot_grads = (
        spread_back(target_hot, grad_summed.astype(jnp.bfloat16))
        .astype(jnp.bfloat16)
        .reshape(3, capacity, width)
    )
    back_left = from_behind(slot_grads[0], "grid", 1)
    back_right = from_behind(slot_grads[2], "grid", -1)
    grad_latent = (
        spread_back(own_hot, slot_grads[1])
        + spread_back(left_hot, back_left)
        + spread_back(right_hot, back_right)
    )
    grid_share = lax.psum_scatter(grad_summed, "member", scatter_dimension=1, tiled=True)
    return (grad_latent.astype(jnp.bfloat16)[None], grid_share.astype(jnp.bfloat16))


def solution(mesh):
    return jax.shard_map(
        per_device,
        mesh=mesh,
        in_specs=(
            P("member", "grid", None),
            P("grid", None),
            P(),
            P(),
            P(None, "grid"),
            P("grid"),
            P(),
            P("grid", None, None),
            P("grid", None, None),
            P("grid", None),
        ),
        out_specs=(P("member", "grid", None), P("grid", "member")),
        check_vma=False,
    )
```

profile of v0, /device:TPU:1, one launch (start us, length us, event | category | flops | bytes accessed | tf_op | source)
XLA Modules:
  0.0 231.7 jit_solution(17376738798907109342)
XLA Ops:
  8.1 4.4 %collective-permute-start = (s32[512]{0:T(512)S(1)}, s32[512]{0:T(512)S(1)}, u32[]{:S(2)}, u32[]{:S(2)}) collective-permute-start(s32[512]{0:T(512)S(1)} %bitcast.38), channel_id=1, source_target_pairs={{0,1},{1,2},{2,3},{3,4},{4,5},{5,6},{6,7},{7,8},{8,9},{9,10},{10,1... | collective-permute-start | bytes 6152 | tf_op jit(solution)/shard_map/ppermute | solution.py:14
  12.5 10.5 %collective-permute-start.2 = (s32[512]{0:T(512)S(1)}, s32[512]{0:T(512)S(1)}, u32[]{:S(2)}, u32[]{:S(2)}) collective-permute-start(s32[512]{0:T(512)S(1)} %bitcast.37), channel_id=1, source_target_pairs={{0,31},{1,0},{2,1},{3,2},{4,3},{5,4},{6,5},{7,6},{8,7},{9,8},{10,9... | collective-permute-start | bytes 6152 | tf_op jit(solution)/shard_map/ppermute | solution.py:14
  23.0 2.5 %convolution_convert_fusion.3 = bf16[512,1024]{1,0:T(8,128)(2,1)} fusion(bf16[1,256,1024]{2,1,0:T(8,128)(2,1)} %param.10, s32[512]{0:T(512)S(1)} %collective-permute-done), kind=kOutput, calls=%fused_computation.12 | convolution fusion | flops 269090816 | bytes 1574912 | tf_op jit(solution)/shard_map/dot_general | solution.py:58
  25.5 3.4 %collective-permute-start.1 = (bf16[512,1024]{1,0:T(8,128)(2,1)}, bf16[512,1024]{1,0:T(8,128)(2,1)}, u32[]{:S(2)}, u32[]{:S(2)}) collective-permute-start(bf16[512,1024]{1,0:T(8,128)(2,1)} %convolution_convert_fusion.3), channel_id=1, source_target_pairs={{0,31},{1,0},{2,1},{3,2},{4,3},{5,4},{6,5},{7,6},{8,7},{9,8},{10,9... | collective-permute-start | bytes 3145736 | tf_op jit(solution)/shard_map/ppermute | solution.py:14
  28.9 2.5 %convolution_convert_fusion.1 = bf16[512,1024]{1,0:T(8,128)(2,1)} fusion(bf16[1,256,1024]{2,1,0:T(8,128)(2,1)} %param.10, s32[512]{0:T(512)S(1)} %collective-permute-done.2), kind=kOutput, calls=%fused_computation.10 | convolution fusion | flops 269090816 | bytes 1574912 | tf_op jit(solution)/shard_map/dot_general | solution.py:58
  31.4 1.9 collective-permute-start.3
  34.0 17.5 %collective-permute-done.1 = bf16[512,1024]{1,0:T(8,128)(2,1)} collective-permute-done((bf16[512,1024]{1,0:T(8,128)(2,1)}, bf16[512,1024]{1,0:T(8,128)(2,1)}, u32[]{:S(2)}, u32[]{:S(2)}) %collective-permute-start.1) | collective-permute-done | bytes 1048608 | tf_op jit(solution)/shard_map/ppermute | solution.py:14
  51.5 7.4 %collective-permute-done.3 = bf16[512,1024]{1,0:T(8,128)(2,1)} collective-permute-done((bf16[512,1024]{1,0:T(8,128)(2,1)}, bf16[512,1024]{1,0:T(8,128)(2,1)}, u32[]{:S(2)}, u32[]{:S(2)}) %collective-permute-start.3) | collective-permute-done | bytes 1048608 | tf_op jit(solution)/shard_map/ppermute | solution.py:14
  58.9 2.8 %fusion.65 = (f32[256]{0:T(256)S(1)}, f32[256,1024]{1,0:T(8,128)S(1)}) fusion(bf16[256,1024]{1,0:T(8,128)(2,1)} %param.11, bf16[512,1024]{1,0:T(8,128)(2,1)} %collective-permute-done.3, bf16[512,1024]{1,0:T(8,128)(2,1)S(1)} %convolution_convert_fusion.2, bf16[512,1024]{1,0:T(8,128)(2,1)} %collective-permute-done.1, s32[1536]{0:T(1024)S(1)} %eq.61, ...), kind=kOutput, calls=%fused_computation.75 | convolution fusion | flops 816316160 | bytes 4727296 | tf_op jit(solution)/shard_map/dot_general | solution.py:102
  62.8 1.1 fusion.38
  64.0 59.5 %all-gather.4.cloned.1.call-done = f32[16,100,256]{2,1,0:T(8,128)} async-done(((f32[1,100,256]{2,1,0:T(8,128)}), f32[16,100,256]{2,1,0:T(8,128)}) %all-gather.4.cloned.1.call-update) | async-done | bytes 1638416 | tf_op jit(solution)/shard_map/all_gather | solution.py:108
  123.5 1.8 multiply_reduce_fusion
  125.3 3.5 %fusion.62 = (f32[256]{0:T(256)S(1)}, f32[256]{0:T(256)S(1)}, f32[256,1024]{1,0:T(8,128)}) fusion(f32[256]{0:T(256)S(1)} %add_rsqrt_fusion, f32[256,1024]{1,0:T(8,128)S(1)} %get-tuple-element.14, f32[256]{0:T(256)S(1)} %broadcast_multiply_fusion.2, bf16[1024,1024]{1,0:T(8,128)(2,1)S(1)} %copy-done, bf16[100,1024]{1,0:T(8,128)(2,1)S(1)} %copy-done.6, ...), kind=kOutput, calls=%fused_computation.72 | convolution fusion | flops 593199616 | bytes 5760400 | tf_op jit(solution)/shard_map/dot_general | solution.py:43
  128.8 2.6 %subtract_multiply_fusion = f32[256,1024]{1,0:T(8,128)} fusion(f32[256,1024]{1,0:T(8,128)} %get-tuple-element.15, f32[256,1024]{1,0:T(8,128)S(1)} %get-tuple-element.14, f32[256]{0:T(256)S(1)} %get-tuple-element.16, f32[256]{0:T(256)S(1)} %get-tuple-element.17, f32[256]{0:T(256)S(1)} %add_rsqrt_fusion, f32[256]{0:T(256)S(1)} %broadcast_multiply_fusion.2), kind=kLoop, calls=%fused_computation.24 | loop fusion | flops 1572864 | bytes 3149824 | tf_op jit(solution)/shard_map/mul | solution.py:46
  131.4 2.6 %copy.14 = f32[256,1024]{0,1:T(8,128)} copy(f32[256,1024]{1,0:T(8,128)} %subtract_multiply_fusion) | data formatting | bytes 2097152
  134.0 2.7 %convolution_convert_fusion = bf16[1536,1024]{1,0:T(8,128)(2,1)} fusion(s32[1536]{0:T(1024)S(1)} %eq.61, pred[1536]{0:T(1024)(128)(4,1)S(1)} %lt.26, f32[256,1024]{1,0:T(8,128)S(1)} %copy-done.1), kind=kOutput, calls=%fused_computation | convolution fusion | flops 807927808 | bytes 4201984 | tf_op jit(solution)/shard_map/dot_general | solution.py:62
  136.7 1.7 fusion.63
  138.5 3.2 %collective-permute-start.4 = (bf16[512,1024]{1,0:T(8,128)(2,1)S(1)}, bf16[512,1024]{1,0:T(8,128)(2,1)S(1)}, u32[]{:S(2)}, u32[]{:S(2)}) collective-permute-start(bf16[512,1024]{1,0:T(8,128)(2,1)S(1)} %get-tuple-element.9), channel_id=1, source_target_pairs={{0,1},{1,2},{2,3},{3,4},{4,5},{5,6},{6,7},{7,8},{8,9},{9,10},{10,1... | collective-permute-start | bytes 3145736 | tf_op jit(solution)/shard_map/ppermute | solution.py:14
  141.6 4.4 %collective-permute-start.5 = (bf16[512,1024]{1,0:T(8,128)(2,1)S(1)}, bf16[512,1024]{1,0:T(8,128)(2,1)S(1)}, u32[]{:S(2)}, u32[]{:S(2)}) collective-permute-start(bf16[512,1024]{1,0:T(8,128)(2,1)S(1)} %get-tuple-element.8), channel_id=1, source_target_pairs={{0,31},{1,0},{2,1},{3,2},{4,3},{5,4},{6,5},{7,6},{8,7},{9,8},{10,9... | collective-permute-start | bytes 3145736 | tf_op jit(solution)/shard_map/ppermute | solution.py:14
  146.1 1.8 fusion.19
  147.9 19.6 %collective-permute-done.4 = bf16[512,1024]{1,0:T(8,128)(2,1)S(1)} collective-permute-done((bf16[512,1024]{1,0:T(8,128)(2,1)S(1)}, bf16[512,1024]{1,0:T(8,128)(2,1)S(1)}, u32[]{:S(2)}, u32[]{:S(2)}) %collective-permute-start.4) | collective-permute-done | bytes 1048608 | tf_op jit(solution)/shard_map/ppermute | solution.py:14
  168.3 1.4 fusion.17
  169.7 53.5 %reduce-scatter.4.cloned.1.call-done = f32[64,256]{1,0:T(8,128)} async-done(((f32[1024,256]{1,0:T(8,128)}), f32[64,256]{1,0:T(8,128)}) %reduce-scatter.4.cloned.1.call-update) | async-done | bytes 65552
  223.2 0.9 copy.15
  (38 shorter events, 4.4 us)
Async XLA Ops:
  7.2 54.7 %copy-start = (bf16[1024,1024]{1,0:T(8,128)(2,1)S(1)}, bf16[1024,1024]{1,0:T(8,128)(2,1)}, u32[]{:S(2)}) copy-start(bf16[1024,1024]{1,0:T(8,128)(2,1)} %param.12) | copy-start | bytes 6291460
  7.2 26.3 %copy-start.2 = (bf16[1,256,1024]{2,1,0:T(8,128)(2,1)S(1)}, bf16[1,256,1024]{2,1,0:T(8,128)(2,1)}, u32[]{:S(2)}) copy-start(bf16[1,256,1024]{2,1,0:T(8,128)(2,1)} %param.10) | copy-start | bytes 1572868
  7.2 26.1 %copy-start.5 = (s32[1,3]{1,0:T(1,128)S(1)}, s32[1,3]{1,0:T(1,128)}, u32[]{:S(2)}) copy-start(s32[1,3]{1,0:T(1,128)} %param.19) | copy-start | bytes 40
  7.2 26.2 %copy-start.4 = (s32[1,3,512]{2,0,1:T(1,128)S(1)}, s32[1,3,512]{2,0,1:T(1,128)}, u32[]{:S(2)}) copy-start(s32[1,3,512]{2,0,1:T(1,128)} %param.18) | copy-start | bytes 18436
  7.2 116.3 %all-gather.4.cloned.1.call-start = ((), (), s32[]{:S(2)}) async-start(), calls=%async_computation.1 | async-start | bytes 1810432 | tf_op jit(solution)/shard_map/all_gather | solution.py:108
  8.1 14.9 %collective-permute-start = (s32[512]{0:T(512)S(1)}, s32[512]{0:T(512)S(1)}, u32[]{:S(2)}, u32[]{:S(2)}) collective-permute-start(s32[512]{0:T(512)S(1)} %bitcast.38), channel_id=1, source_target_pairs={{0,1},{1,2},{2,3},{3,4},{4,5},{5,6},{6,7},{7,8},{8,9},{9,10},{10,1... | collective-permute-start | bytes 6152 | tf_op jit(solution)/shard_map/ppermute | solution.py:14
  12.5 16.4 %collective-permute-start.2 = (s32[512]{0:T(512)S(1)}, s32[512]{0:T(512)S(1)}, u32[]{:S(2)}, u32[]{:S(2)}) collective-permute-start(s32[512]{0:T(512)S(1)} %bitcast.37), channel_id=1, source_target_pairs={{0,31},{1,0},{2,1},{3,2},{4,3},{5,4},{6,5},{7,6},{8,7},{9,8},{10,9... | collective-permute-start | bytes 6152 | tf_op jit(solution)/shard_map/ppermute | solution.py:14
  25.5 25.9 %collective-permute-start.1 = (bf16[512,1024]{1,0:T(8,128)(2,1)}, bf16[512,1024]{1,0:T(8,128)(2,1)}, u32[]{:S(2)}, u32[]{:S(2)}) collective-permute-start(bf16[512,1024]{1,0:T(8,128)(2,1)} %convolution_convert_fusion.3), channel_id=1, source_target_pairs={{0,31},{1,0},{2,1},{3,2},{4,3},{5,4},{6,5},{7,6},{8,7},{9,8},{10,9... | collective-permute-start | bytes 3145736 | tf_op jit(solution)/shard_map/ppermute | solution.py:14
  31.4 27.4 %collective-permute-start.3 = (bf16[512,1024]{1,0:T(8,128)(2,1)}, bf16[512,1024]{1,0:T(8,128)(2,1)}, u32[]{:S(2)}, u32[]{:S(2)}) collective-permute-start(bf16[512,1024]{1,0:T(8,128)(2,1)} %convolution_convert_fusion.1), channel_id=1, source_target_pairs={{0,1},{1,2},{2,3},{3,4},{4,5},{5,6},{6,7},{7,8},{8,9},{9,10},{10,1... | collective-permute-start | bytes 3145736 | tf_op jit(solution)/shard_map/ppermute | solution.py:14
  61.9 0.9 copy-start.6
  62.8 1.1 copy-start.3
  62.8 62.5 %copy-start.7 = (f32[256]{0:T(256)S(1)}, f32[256]{0:T(256)}, u32[]{:S(2)}) copy-start(f32[256]{0:T(256)} %param.15) | copy-start | bytes 3076
  62.8 62.5 %copy-start.8 = (f32[100]{0:T(128)S(1)}, f32[100]{0:T(128)}, u32[]{:S(2)}) copy-start(f32[100]{0:T(128)} %param.16) | copy-start | bytes 1204
  64.0 159.3 %reduce-scatter.4.cloned.1.call-start = ((), (), s32[]{:S(2)}) async-start(), calls=%async_computation.2 | async-start | bytes 1114112
  131.4 2.6 %copy-start.1 = (f32[256,1024]{1,0:T(8,128)S(1)}, f32[256,1024]{1,0:T(8,128)}, u32[]{:S(2)}) copy-start(f32[256,1024]{1,0:T(8,128)} %subtract_multiply_fusion) | copy-start | bytes 3145732
  138.5 29.0 %collective-permute-start.4 = (bf16[512,1024]{1,0:T(8,128)(2,1)S(1)}, bf16[512,1024]{1,0:T(8,128)(2,1)S(1)}, u32[]{:S(2)}, u32[]{:S(2)}) collective-permute-start(bf16[512,1024]{1,0:T(8,128)(2,1)S(1)} %get-tuple-element.9), channel_id=1, source_target_pairs={{0,1},{1,2},{2,3},{3,4},{4,5},{5,6},{6,7},{7,8},{8,9},{9,10},{10,1... | collective-permute-start | bytes 3145736 | tf_op jit(solution)/shard_map/ppermute | solution.py:14
  141.6 26.7 %collective-permute-start.5 = (bf16[512,1024]{1,0:T(8,128)(2,1)S(1)}, bf16[512,1024]{1,0:T(8,128)(2,1)S(1)}, u32[]{:S(2)}, u32[]{:S(2)}) collective-permute-start(bf16[512,1024]{1,0:T(8,128)(2,1)S(1)} %get-tuple-element.8), channel_id=1, source_target_pairs={{0,31},{1,0},{2,1},{3,2},{4,3},{5,4},{6,5},{7,6},{8,7},{9,8},{10,9... | collective-permute-start | bytes 3145736 | tf_op jit(solution)/shard_map/ppermute | solution.py:14
Sparse Core Ops, SparseCore 0:
  64.1 59.3 all-gather.3
  136.9 86.3 reduce-scatter.3
where the time goes:
time: 233 us; the launch traced here: 232 us
  waiting for transfers between devices  158 us (68%)
  starting transfers between devices  27.8 us (12%)
  matrix products  20.1 us (9%)
  between operations  14.2 us (6%)
  local copies, waits for them, and re-layouts  7.11 us (3%)
  other arithmetic  4.73 us (2%)
    all_gather x1, waiting for transfers between devices, per_device(): lax.all_gather(predicted[None], 'member', axis=0, tiled=True)  59.5 us
    unnamed x3, waiting for transfers between devices  53.5 us
    ppermute x6, waiting for transfers between devices, from_behind(): return lax.ppermute(value, axis, pairs)  44.7 us
    ppermute x6, starting transfers between devices, from_behind(): return lax.ppermute(value, axis, pairs)  27.7 us
    dot_general x4, matrix products, spread_back(): lax.dot_general(hot, grads, (((0,), (0,)), ((), ())), preferred_element_t...  6.49 us
    dot_general x3, matrix products, select_rows(): return jnp.dot(hot, rows, preferred_element_type=jnp.float32)  5.5 us
  transfers between devices with their start and end apart: 8, of which 6 were waited for; matrix products, arithmetic and copies ran while one was open for 5% of the time, Pallas kernels for 0%

commit v1 on v0

v1 whole, which is shorter than its diff:
```python
import jax
import jax.numpy as jnp
from jax import lax
from jax.sharding import PartitionSpec as P

SMOOTH = 0.1
ALPHA = 0.95
EPS = 1e-05


def from_behind(value, axis, steps):
    count = lax.axis_size(axis)
    pairs = [(source, (source + steps) % count) for source in range(count)]
    return lax.ppermute(value, axis, pairs)


def smooth_slope(difference):
    return difference * lax.rsqrt(difference * difference + SMOOTH * SMOOTH)


def counts_of(rows_pick, columns_pick, rows, columns):
    row_hot = (jnp.arange(rows, dtype=jnp.int32)[:, None] == rows_pick[None, :]).astype(jnp.bfloat16)
    column_hot = (columns_pick[:, None] == jnp.arange(columns, dtype=jnp.int32)[None, :]).astype(
        jnp.bfloat16
    )
    counts = jnp.dot(row_hot, column_hot, preferred_element_type=jnp.float32)
    high = counts.astype(jnp.bfloat16)
    return high, (counts - high.astype(jnp.float32)).astype(jnp.bfloat16)


def per_device(
    mesh_latent,
    grid_latent,
    node_weight,
    out_weight,
    target,
    area_weight,
    var_weight,
    edge_src,
    edge_dst,
    edge_count,
):
    members = lax.axis_size("member")
    latent = mesh_latent[0]
    mesh_rows = latent.shape[0]
    grid_rows, width = grid_latent.shape
    capacity = edge_dst.shape[2]
    live = jnp.arange(capacity, dtype=jnp.int32)[None, :] < edge_count[0][:, None]
    picks = jnp.where(live, edge_dst[0], -1)
    from_left = from_behind(latent, "grid", 1)
    from_right = from_behind(latent, "grid", -1)
    edges = jnp.stack([edge_src[0], picks], axis=1)
    edges_left = from_behind(edges[0], "grid", 1)
    edges_right = from_behind(edges[2], "grid", -1)

    parts = [counts_of(picks[o], edge_src[0, o], grid_rows, mesh_rows) for o in range(3)]
    spread = jnp.concatenate([p[0] for p in parts] + [p[1] for p in parts], axis=1)
    rows = jnp.concatenate([from_right, latent, from_left] * 2, axis=0)
    gathered = jnp.dot(spread, rows, preferred_element_type=jnp.float32)

    summed = gathered + grid_latent.astype(jnp.float32)
    centered = summed - jnp.mean(summed, axis=-1, keepdims=True)
    inverse = lax.rsqrt(jnp.mean(centered * centered, axis=-1, keepdims=True) + EPS)
    normed = centered * inverse
    pre_act = jnp.dot(normed.astype(jnp.bfloat16), node_weight, preferred_element_type=jnp.float32)
    hidden = jax.nn.silu(pre_act).astype(jnp.bfloat16)
    variables = out_weight.shape[0]
    out_padded = jnp.pad(out_weight, ((0, 128 - variables), (0, 0)))
    predicted = lax.dot_general(
        hidden, out_padded, (((1,), (1,)), ((), ())), preferred_element_type=jnp.float32
    )
    shared = jnp.broadcast_to(predicted.astype(jnp.bfloat16)[None], (members, grid_rows, 128))
    everyone = lax.all_to_all(shared, "member", 0, 0, tiled=True)
    own = lax.axis_index("member")
    others = jnp.where(
        jnp.arange(members)[:, None, None] == own, predicted[None], everyone.astype(jnp.float32)
    )
    pair_sum = jnp.sum(smooth_slope(predicted[None] - others), axis=0)
    pair_scale = (1.0 - (1.0 - ALPHA) / members) / (members - 1)
    target_padded = jnp.pad(target, ((0, 128 - variables), (0, 0))).T
    var_padded = jnp.pad(var_weight, (0, 128 - variables))
    grad_pred = (
        area_weight[:, None]
        * var_padded[None, :]
        * (smooth_slope(predicted - target_padded) - pair_scale * pair_sum)
    )
    grad_hidden = jnp.dot(
        grad_pred.astype(jnp.bfloat16), out_padded, preferred_element_type=jnp.float32
    )
    gate_sig = jax.nn.sigmoid(pre_act)
    grad_pre = (grad_hidden * gate_sig * (1.0 + pre_act * (1.0 - gate_sig))).astype(jnp.bfloat16)
    grad_normed = lax.dot_general(
        grad_pre, node_weight, (((1,), (1,)), ((), ())), preferred_element_type=jnp.float32
    )
    grad_summed = inverse * (
        grad_normed
        - jnp.mean(grad_normed, axis=-1, keepdims=True)
        - normed * jnp.mean(grad_normed * normed, axis=-1, keepdims=True)
    )
    grad_send = grad_summed.astype(jnp.bfloat16)
    back_left = from_behind(grad_send, "grid", 1)
    back_right = from_behind(grad_send, "grid", -1)
    share = width // members
    blocks = grad_send.reshape(2, grid_rows // 2, members, share).transpose(2, 1, 0, 3)
    blocks = blocks.reshape(members, grid_rows // 2, 2 * share)
    landed = lax.all_to_all(blocks, "member", 0, 0, tiled=True)
    grid_sum = jnp.sum(landed.astype(jnp.float32), axis=0).astype(jnp.bfloat16)
    grid_share = grid_sum.reshape(grid_rows // 2, 2, share).transpose(1, 0, 2)
    grid_share = grid_share.reshape(grid_rows, share)

    own_edges = (edge_src[0, 1], picks[1])
    back = [
        counts_of(dst, src, grid_rows, mesh_rows)
        for src, dst in (edges_left, own_edges, edges_right)
    ]
    collect = jnp.concatenate([p[0] for p in back] + [p[1] for p in back], axis=0)
    grads = jnp.concatenate([back_left, grad_send, back_right] * 2, axis=0)
    grad_latent = lax.dot_general(
        collect, grads, (((0,), (0,)), ((), ())), preferred_element_type=jnp.float32
    )
    return (grad_latent.astype(jnp.bfloat16)[None], grid_share)


def solution(mesh):
    return jax.shard_map(
        per_device,
        mesh=mesh,
        in_specs=(
            P("member", "grid", None),
            P("grid", None),
            P(),
            P(),
            P(None, "grid"),
            P("grid"),
            P(),
            P("grid", None, None),
            P("grid", None, None),
            P("grid", None),
        ),
        out_specs=(P("member", "grid", None), P("grid", "member")),
        check_vma=False,
    )
```

time: 233 us -> 108 us (0.46)
  waiting for transfers between devices: 158 us -> 30.4 us
  starting transfers between devices: 27.8 us -> 42.8 us
  between operations: 14.2 us -> 0.96 us
  matrix products: 20.1 us -> 9.47 us
  local copies, waits for them, and re-layouts: 7.11 us -> 15.5 us
  other arithmetic: 4.73 us -> 8.18 us
    all_gather x1 -> x0, waiting for transfers between devices: 59.5 us -> none  [per_device(): lax.all_gather(predicted[None], 'member', axis=0, tiled=True)]
    unnamed x3 -> x0, waiting for transfers between devices: 53.5 us -> none
    ppermute x6, waiting for transfers between devices: 44.7 us -> 8.46 us  [from_behind(): return lax.ppermute(value, axis, pairs)]
    all_to_all x0 -> x2, waiting for transfers between devices: none -> 22 us  [the longest x1 15.2 us: per_device(): everyone = lax.all_to_all(shared, 'member', 0, 0, tiled=True)]
    all_to_all x0 -> x2, starting transfers between devices: none -> 12.7 us  [the longest x1 8.51 us: per_device(): everyone = lax.all_to_all(shared, 'member', 0, 0, tiled=True)]
    dot_general x11 -> x10, matrix products: 20.1 us -> 9.47 us  [the longest x1 3.64 us: per_device(): lax.dot_general(grad_pre, node_weight, (((1,), (1,)), ((), ())), preferre...]
    unnamed x21 -> x27, local copies, waits for them, and re-layouts: 4.5 us -> 7.2 us
    mul x1 -> x0, other arithmetic: 2.55 us -> none  [decode_backward(): inverse * (grad_normed - jnp.mean(grad_normed, axis=-1, keepdims=True) -...]
  transfers between devices with their start and end apart: 8 -> 8, of which waited for: 6 -> 4; matrix products, arithmetic and copies ran while one was open for 5% -> 13% of each run, Pallas kernels for 0% -> 0%
where the time goes in v1:
time: 108 us; the launch traced here: 107 us
  starting transfers between devices  42.8 us (40%)
  waiting for transfers between devices  30.4 us (28%)
  local copies, waits for them, and re-layouts  15.5 us (14%)
  matrix products  9.47 us (9%)
  other arithmetic  8.18 us (8%)
    ppermute x6, starting transfers between devices, from_behind(): return lax.ppermute(value, axis, pairs)  30.1 us
    all_to_all x1, waiting for transfers between devices, per_device(): everyone = lax.all_to_all(shared, 'member', 0, 0, tiled=True)  15.2 us
    all_to_all x1, starting transfers between devices, per_device(): everyone = lax.all_to_all(shared, 'member', 0, 0, tiled=True)  8.51 us
    ppermute x6, waiting for transfers between devices, from_behind(): return lax.ppermute(value, axis, pairs)  8.46 us
    unnamed x27, local copies, waits for them, and re-layouts  7.2 us
    all_to_all x1, waiting for transfers between devices, per_device(): landed = lax.all_to_all(blocks, 'member', 0, 0, tiled=True)  6.8 us
    all_to_all x1, starting transfers between devices, per_device(): landed = lax.all_to_all(blocks, 'member', 0, 0, tiled=True)  4.23 us
    dot_general x1, matrix products, per_device(): lax.dot_general(grad_pre, node_weight, (((1,), (1,)), ((), ())), preferre...  3.64 us
  transfers between devices with their start and end apart: 8, of which 4 were waited for; matrix products, arithmetic and copies ran while one was open for 13% of the time, Pallas kernels for 0%

profile of v1, /device:TPU:1, one launch (start us, length us, event | category | flops | bytes accessed | tf_op | source)
XLA Modules:
  0.0 107.3 jit_solution(16618063186118045143)
XLA Ops:
  0.7 13.1 %collective-permute-start.2 = (bf16[256,1024]{1,0:T(8,128)(2,1)}, bf16[256,1024]{1,0:T(8,128)(2,1)S(1)}, u32[]{:S(2)}, u32[]{:S(2)}) collective-permute-start(bf16[256,1024]{1,0:T(8,128)(2,1)} %bitcast.50), channel_id=1, source_target_pairs={{0,31},{1,0},{2,1},{3,2},{4,3},{5,4},{6,5},{7,6},{8,7},{9,8},{10,9... | collective-permute-start | bytes 1572872 | tf_op jit(solution)/shard_map/ppermute | solution.py:14
  13.8 1.9 %collective-permute-start.3 = (bf16[256,1024]{1,0:T(8,128)(2,1)}, bf16[256,1024]{1,0:T(8,128)(2,1)S(1)}, u32[]{:S(2)}, u32[]{:S(2)}) collective-permute-start(bf16[256,1024]{1,0:T(8,128)(2,1)} %bitcast.51), channel_id=1, source_target_pairs={{0,1},{1,2},{2,3},{3,4},{4,5},{5,6},{6,7},{7,8},{8,9},{9,10},{10,1... | collective-permute-start | bytes 1572872 | tf_op jit(solution)/shard_map/ppermute | solution.py:14
  17.2 1.9 %collective-permute-start = (s32[2,512]{1,0:T(2,128)S(1)}, s32[2,512]{1,0:T(2,128)S(1)}, u32[]{:S(2)}, u32[]{:S(2)}) collective-permute-start(s32[2,512]{1,0:T(2,128)S(1)} %get-tuple-element.9), channel_id=1, source_target_pairs={{0,1},{1,2},{2,3},{3,4},{4,5},{5,6},{6,7},{7,8},{8,9},{9,10},{10,1... | collective-permute-start | bytes 12296 | tf_op jit(solution)/shard_map/ppermute | solution.py:14
  19.1 5.5 %collective-permute-start.1 = (s32[2,512]{1,0:T(2,128)S(1)}, s32[2,512]{1,0:T(2,128)S(1)}, u32[]{:S(2)}, u32[]{:S(2)}) collective-permute-start(s32[2,512]{1,0:T(2,128)S(1)} %get-tuple-element.8), channel_id=1, source_target_pairs={{0,31},{1,0},{2,1},{3,2},{4,3},{5,4},{6,5},{7,6},{8,7},{9,8},{10,9... | collective-permute-start | bytes 12296 | tf_op jit(solution)/shard_map/ppermute | solution.py:14
  26.4 4.1 %collective-permute-done = s32[2,512]{1,0:T(2,128)S(1)} collective-permute-done((s32[2,512]{1,0:T(2,128)S(1)}, s32[2,512]{1,0:T(2,128)S(1)}, u32[]{:S(2)}, u32[]{:S(2)}) %collective-permute-start) | collective-permute-done | bytes 4128 | tf_op jit(solution)/shard_map/ppermute | solution.py:14
  37.0 1.2 %broadcast_in_dim.21 = bf16[16,256,128]{2,1,0:T(8,128)(2,1)} broadcast(bf16[256,128]{1,0:T(8,128)(2,1)S(1)} %get-tuple-element.31), dimensions={1,2} | broadcast | bytes 1114112 | tf_op jit(solution)/shard_map/broadcast_in_dim | solution.py:72
  38.2 8.5 %all-to-all-start = ((bf16[16,256,128]{2,1,0:T(8,128)(2,1)}), bf16[16,256,128]{2,1,0:T(8,128)(2,1)}, u32[]{:S(2)}, u32[]{:S(2)}) async-start(bf16[16,256,128]{2,1,0:T(8,128)(2,1)} %broadcast_in_dim.21), calls=%async_computation | async-start | bytes 2097152 | tf_op jit(solution)/shard_map/all_to_all | solution.py:73
  46.7 1.6 %copy.36 = f32[100,256]{0,1:T(8,128)} copy(f32[100,256]{1,0:T(8,128)} %param.14) | data formatting | bytes 204800 | tf_op args[4]
  48.8 15.2 %all-to-all-done = bf16[16,256,128]{2,1,0:T(8,128)(2,1)} async-done(((bf16[16,256,128]{2,1,0:T(8,128)(2,1)}), bf16[16,256,128]{2,1,0:T(8,128)(2,1)}, u32[]{:S(2)}, u32[]{:S(2)}) %all-to-all-start) | async-done | bytes 1048608 | tf_op jit(solution)/shard_map/all_to_all | solution.py:73
  64.0 2.5 %multiply_reduce_fusion = f32[256,128]{1,0:T(8,128)} fusion(bf16[16,256,128]{2,1,0:T(8,128)(2,1)} %all-to-all-done, f32[256,128]{1,0:T(8,128)S(1)} %get-tuple-element.32, pred[16]{0:T(512)(128)(4,1)S(1)} %iota_compare_fusion.21), kind=kLoop, calls=%fused_computation | loop fusion | flops 3637248 | bytes 1310736 | tf_op jit(solution)/shard_map/reduce_sum | solution.py:78
  66.5 3.6 %fusion.56 = (f32[256]{0:T(256)S(1)}, f32[256]{0:T(256)S(1)}, f32[256,1024]{1,0:T(8,128)}) fusion(f32[256]{0:T(256)S(1)} %add_rsqrt_fusion, f32[256,1024]{1,0:T(8,128)S(1)} %get-tuple-element.30, f32[256]{0:T(256)S(1)} %broadcast_multiply_fusion.2, bf16[1024,1024]{1,0:T(8,128)(2,1)S(1)} %copy-done, f32[256,1024]{1,0:T(8,128)} %copy-done.2, ...), kind=kOutput, calls=%fused_computation.104 | convolution fusion | flops 607944192 | bytes 5817856 | tf_op jit(solution)/shard_map/dot_general | solution.py:92
  70.1 2.3 %multiply_convert_fusion = bf16[256,1024]{1,0:T(8,128)(2,1)} fusion(f32[256,1024]{1,0:T(8,128)} %get-tuple-element.33, f32[256,1024]{1,0:T(8,128)S(1)} %get-tuple-element.30, f32[256]{0:T(256)S(1)} %broadcast_multiply_fusion, f32[256]{0:T(256)S(1)} %broadcast_multiply_fusion.1, f32[256]{0:T(256)S(1)} %add_rsqrt_fusion, f32[256]{0:T(256)S(1)} %broadcast_multiply_fusion.2), kind=kLoop, calls=%fused_computation.8 | loop fusion | flops 1835008 | bytes 2625536 | tf_op jit(solution)/shard_map/convert_element_type | solution.py:100
  72.5 1.9 %collective-permute-start.4 = (bf16[256,1024]{1,0:T(8,128)(2,1)}, bf16[256,1024]{1,0:T(8,128)(2,1)S(1)}, u32[]{:S(2)}, u32[]{:S(2)}) collective-permute-start(bf16[256,1024]{1,0:T(8,128)(2,1)} %multiply_convert_fusion), channel_id=1, source_target_pairs={{0,1},{1,2},{2,3},{3,4},{4,5},{5,6},{6,7},{7,8},{8,9},{9,10},{10,1... | collective-permute-start | bytes 1572872 | tf_op jit(solution)/shard_map/ppermute | solution.py:14
  74.4 2.0 %copy.37 = bf16[256,1024]{0,1:T(8,128)(2,1)} copy(bf16[256,1024]{1,0:T(8,128)(2,1)} %multiply_convert_fusion) | data formatting | bytes 1048576 | tf_op jit(solution)/shard_map/convert_element_type | solution.py:100
  76.4 1.2 %reshape.98 = bf16[2,128,16,64]{1,0,3,2:T(2,128)(2,1)S(1)} reshape(bf16[256,1024]{0,1:T(8,128)(2,1)} %copy.37) | data formatting | bytes 1048576 | tf_op jit(solution)/shard_map/reshape | solution.py:104
  78.5 4.2 %all-to-all-start.1 = ((bf16[16,128,128]{1,2,0:T(8,128)(2,1)}), bf16[16,128,128]{1,2,0:T(8,128)(2,1)S(1)}, u32[]{:S(2)}, u32[]{:S(2)}) async-start(bf16[16,128,128]{1,2,0:T(8,128)(2,1)} %bitcast.52), calls=%async_computation.1 | async-start | bytes 1048576 | tf_op jit(solution)/shard_map/all_to_all | solution.py:106
  82.8 5.7 %collective-permute-start.5 = (bf16[256,1024]{1,0:T(8,128)(2,1)}, bf16[256,1024]{1,0:T(8,128)(2,1)}, u32[]{:S(2)}, u32[]{:S(2)}) collective-permute-start(bf16[256,1024]{1,0:T(8,128)(2,1)} %multiply_convert_fusion), channel_id=1, source_target_pairs={{0,31},{1,0},{2,1},{3,2},{4,3},{5,4},{6,5},{7,6},{8,7},{9,8},{10,9... | collective-permute-start | bytes 1572872 | tf_op jit(solution)/shard_map/ppermute | solution.py:14
  89.2 6.8 %all-to-all-done.1 = bf16[16,128,128]{1,2,0:T(8,128)(2,1)S(1)} async-done(((bf16[16,128,128]{1,2,0:T(8,128)(2,1)}), bf16[16,128,128]{1,2,0:T(8,128)(2,1)S(1)}, u32[]{:S(2)}, u32[]{:S(2)}) %all-to-all-start.1) | async-done | bytes 524320 | tf_op jit(solution)/shard_map/all_to_all | solution.py:106
  96.7 1.1 %constant_dynamic-update-slice_fusion.14 = bf16[1536,1024]{1,0:T(8,128)(2,1)S(1)} fusion(bf16[1536,1024]{1,0:T(8,128)(2,1)S(1)} %constant_dynamic-update-slice_fusion.15, bf16[256,1024]{1,0:T(8,128)(2,1)} %multiply_convert_fusion), kind=kLoop, calls=%fused_computation.83 | loop fusion | bytes 1048576
  97.9 4.3 %collective-permute-done.5 = bf16[256,1024]{1,0:T(8,128)(2,1)} collective-permute-done((bf16[256,1024]{1,0:T(8,128)(2,1)}, bf16[256,1024]{1,0:T(8,128)(2,1)}, u32[]{:S(2)}, u32[]{:S(2)}) %collective-permute-start.5) | collective-permute-done | bytes 524320 | tf_op jit(solution)/shard_map/ppermute | solution.py:14
  102.2 1.1 %constant_dynamic-update-slice_fusion.13 = bf16[1536,1024]{1,0:T(8,128)(2,1)S(1)} fusion(bf16[1536,1024]{1,0:T(8,128)(2,1)S(1)} %constant_dynamic-update-slice_fusion.14, bf16[256,1024]{1,0:T(8,128)(2,1)} %collective-permute-done.5), kind=kLoop, calls=%fused_computation.82 | loop fusion | bytes 1048576
  103.3 1.1 %constant_dynamic-update-slice_fusion.11 = bf16[1536,1024]{1,0:T(8,128)(2,1)S(1)} fusion(bf16[1536,1024]{1,0:T(8,128)(2,1)S(1)} %constant_dynamic-update-slice_fusion.12, bf16[256,1024]{1,0:T(8,128)(2,1)} %multiply_convert_fusion), kind=kLoop, calls=%fused_computation.80 | loop fusion | bytes 1048576
  104.4 1.1 %constant_dynamic-update-slice_fusion.10 = bf16[1536,1024]{1,0:T(8,128)(2,1)S(1)} fusion(bf16[1536,1024]{1,0:T(8,128)(2,1)S(1)} %constant_dynamic-update-slice_fusion.11, bf16[256,1024]{1,0:T(8,128)(2,1)} %collective-permute-done.5), kind=kLoop, calls=%fused_computation.79 | loop fusion | bytes 1048576 | tf_op jit(solution)/shard_map/concatenate | solution.py:117
  105.5 1.8 %fusion.2 = bf16[1,256,1024]{2,1,0:T(8,128)(2,1)} fusion(bf16[1536,256]{1,0:T(8,128)(2,1)S(1)} %copy-done.4, bf16[1536,1024]{1,0:T(8,128)(2,1)S(1)} %constant_dynamic-update-slice_fusion.10), kind=kOutput, calls=%fused_computation.6 | convolution fusion | flops 805568512 | bytes 4456448 | tf_op jit(solution)/shard_map/dot_general | solution.py:118
  (57 shorter events, 12.5 us)
Async XLA Ops:
  0.6 34.2 %copy-start = (bf16[1024,1024]{1,0:T(8,128)(2,1)S(1)}, bf16[1024,1024]{1,0:T(8,128)(2,1)}, u32[]{:S(2)}) copy-start(bf16[1024,1024]{1,0:T(8,128)(2,1)} %param.12) | copy-start | bytes 6291460
  0.6 31.6 %copy-start.1 = (bf16[1,256,1024]{2,1,0:T(8,128)(2,1)S(1)}, bf16[1,256,1024]{2,1,0:T(8,128)(2,1)}, u32[]{:S(2)}) copy-start(bf16[1,256,1024]{2,1,0:T(8,128)(2,1)} %param.10) | copy-start | bytes 1572868
  0.7 31.5 %collective-permute-start.2 = (bf16[256,1024]{1,0:T(8,128)(2,1)}, bf16[256,1024]{1,0:T(8,128)(2,1)S(1)}, u32[]{:S(2)}, u32[]{:S(2)}) collective-permute-start(bf16[256,1024]{1,0:T(8,128)(2,1)} %bitcast.50), channel_id=1, source_target_pairs={{0,31},{1,0},{2,1},{3,2},{4,3},{5,4},{6,5},{7,6},{8,7},{9,8},{10,9... | collective-permute-start | bytes 1572872 | tf_op jit(solution)/shard_map/ppermute | solution.py:14
  13.8 18.5 %collective-permute-start.3 = (bf16[256,1024]{1,0:T(8,128)(2,1)}, bf16[256,1024]{1,0:T(8,128)(2,1)S(1)}, u32[]{:S(2)}, u32[]{:S(2)}) collective-permute-start(bf16[256,1024]{1,0:T(8,128)(2,1)} %bitcast.51), channel_id=1, source_target_pairs={{0,1},{1,2},{2,3},{3,4},{4,5},{5,6},{6,7},{7,8},{8,9},{9,10},{10,1... | collective-permute-start | bytes 1572872 | tf_op jit(solution)/shard_map/ppermute | solution.py:14
  17.2 13.4 %collective-permute-start = (s32[2,512]{1,0:T(2,128)S(1)}, s32[2,512]{1,0:T(2,128)S(1)}, u32[]{:S(2)}, u32[]{:S(2)}) collective-permute-start(s32[2,512]{1,0:T(2,128)S(1)} %get-tuple-element.9), channel_id=1, source_target_pairs={{0,1},{1,2},{2,3},{3,4},{4,5},{5,6},{6,7},{7,8},{8,9},{9,10},{10,1... | collective-permute-start | bytes 12296 | tf_op jit(solution)/shard_map/ppermute | solution.py:14
  19.1 12.2 %collective-permute-start.1 = (s32[2,512]{1,0:T(2,128)S(1)}, s32[2,512]{1,0:T(2,128)S(1)}, u32[]{:S(2)}, u32[]{:S(2)}) collective-permute-start(s32[2,512]{1,0:T(2,128)S(1)} %get-tuple-element.8), channel_id=1, source_target_pairs={{0,31},{1,0},{2,1},{3,2},{4,3},{5,4},{6,5},{7,6},{8,7},{9,8},{10,9... | collective-permute-start | bytes 12296 | tf_op jit(solution)/shard_map/ppermute | solution.py:14
  32.1 0.9 copy-start.3
  32.1 1.3 %copy-start.5 = (bf16[256,1024]{1,0:T(8,128)(2,1)S(1)}, bf16[256,1024]{1,0:T(8,128)(2,1)}, u32[]{:S(2)}) copy-start(bf16[256,1024]{1,0:T(8,128)(2,1)} %param.11) | copy-start | bytes 1572868
  34.5 2.0 %copy-start.6 = (bf16[100,1024]{1,0:T(8,128)(2,1)S(1)}, bf16[100,1024]{1,0:T(8,128)(2,1)}, u32[]{:S(2)}) copy-start(bf16[100,1024]{1,0:T(8,128)(2,1)} %param.13) | copy-start | bytes 614404
  35.6 1.0 copy-start.2
  36.6 11.8 %copy-start.7 = (f32[100]{0:T(128)S(1)}, f32[100]{0:T(128)}, u32[]{:S(2)}) copy-start(f32[100]{0:T(128)} %param.16) | copy-start | bytes 1204
  38.2 25.8 %all-to-all-start = ((bf16[16,256,128]{2,1,0:T(8,128)(2,1)}), bf16[16,256,128]{2,1,0:T(8,128)(2,1)}, u32[]{:S(2)}, u32[]{:S(2)}) async-start(bf16[16,256,128]{2,1,0:T(8,128)(2,1)} %broadcast_in_dim.21), calls=%async_computation | async-start | bytes 2097152 | tf_op jit(solution)/shard_map/all_to_all | solution.py:73
  72.5 24.2 %collective-permute-start.4 = (bf16[256,1024]{1,0:T(8,128)(2,1)}, bf16[256,1024]{1,0:T(8,128)(2,1)S(1)}, u32[]{:S(2)}, u32[]{:S(2)}) collective-permute-start(bf16[256,1024]{1,0:T(8,128)(2,1)} %multiply_convert_fusion), channel_id=1, source_target_pairs={{0,1},{1,2},{2,3},{3,4},{4,5},{5,6},{6,7},{7,8},{8,9},{9,10},{10,1... | collective-permute-start | bytes 1572872 | tf_op jit(solution)/shard_map/ppermute | solution.py:14
  78.5 17.5 %all-to-all-start.1 = ((bf16[16,128,128]{1,2,0:T(8,128)(2,1)}), bf16[16,128,128]{1,2,0:T(8,128)(2,1)S(1)}, u32[]{:S(2)}, u32[]{:S(2)}) async-start(bf16[16,128,128]{1,2,0:T(8,128)(2,1)} %bitcast.52), calls=%async_computation.1 | async-start | bytes 1048576 | tf_op jit(solution)/shard_map/all_to_all | solution.py:106
  82.8 19.5 %collective-permute-start.5 = (bf16[256,1024]{1,0:T(8,128)(2,1)}, bf16[256,1024]{1,0:T(8,128)(2,1)}, u32[]{:S(2)}, u32[]{:S(2)}) collective-permute-start(bf16[256,1024]{1,0:T(8,128)(2,1)} %multiply_convert_fusion), channel_id=1, source_target_pairs={{0,31},{1,0},{2,1},{3,2},{4,3},{5,4},{6,5},{7,6},{8,7},{9,8},{10,9... | collective-permute-start | bytes 1572872 | tf_op jit(solution)/shard_map/ppermute | solution.py:14
  96.7 8.8 %copy-start.4 = (bf16[1536,256]{1,0:T(8,128)(2,1)S(1)}, bf16[1536,256]{1,0:T(8,128)(2,1)}, u32[]{:S(2)}) copy-start(bf16[1536,256]{1,0:T(8,128)(2,1)} %fusion.33) | copy-start | bytes 2359300

commit v2 on v1

v2 whole, which is shorter than its diff:
```python
import functools

import jax
import jax.numpy as jnp
from jax import lax
from jax.experimental import pallas as pl
from jax.experimental.pallas import tpu as pltpu
from jax.sharding import PartitionSpec as P

SMOOTH = 0.1
ALPHA = 0.95
EPS = 1e-05
LANES = 128
VARS = 100
MAIN = 208
FOLD = 25
FOLDS = 4
STEPS = 32767.0
CODE = 256.0
LOWEST = -20.0
VMEM_LIMIT = 28 * 1024 * 1024


def from_behind(value, axis, steps):
    count = lax.axis_size(axis)
    pairs = [(source, (source + steps) % count) for source in range(count)]
    return lax.ppermute(value, axis, pairs)


def smooth_slope(difference):
    return difference * lax.rsqrt(difference * difference + SMOOTH * SMOOTH)


def turn(values, shift):
    shift = shift % LANES
    return pltpu.roll(values, shift, 1) if shift else values


def lanes_of(values):
    return lax.broadcasted_iota(jnp.int32, values.shape, 1)


def one_hot(picks, rows):
    places = lax.broadcasted_iota(jnp.int32, (rows, picks.shape[1]), 0)
    return jnp.where(places == picks, 1.0, 0.0).astype(jnp.bfloat16)


def count_pairs(row_picks, column_picks, rows, columns):
    return lax.dot_general(
        one_hot(row_picks, rows),
        one_hot(column_picks, columns),
        (((1,), (1,)), ((), ())),
        preferred_element_type=jnp.float32,
    )


def store_counts(counts, at, high_ref, low_ref):
    high = counts.astype(jnp.bfloat16)
    high_ref[:, at] = high
    low_ref[:, at] = (counts - high.astype(jnp.float32)).astype(jnp.bfloat16)
    return jnp.max(counts)


def edges_kernel(count_ref, src_ref, dst_ref, out_ref, high_ref, low_ref, over_ref, first_ref, last_ref, pad_ref, turned_ref):
    grid_rows = high_ref.shape[0]
    mesh_rows = high_ref.shape[1] // 3
    slots = src_ref.shape[1]
    slot = lax.broadcasted_iota(jnp.int32, (1, slots), 1)
    most = 0.0
    for offset in range(3):
        picks = jnp.where(slot < count_ref[0, offset], dst_ref[offset : offset + 1, :], -1)
        sources = src_ref[offset : offset + 1, :]
        counts = count_pairs(picks, sources, grid_rows, mesh_rows)
        at = slice(offset * mesh_rows, (offset + 1) * mesh_rows)
        most = jnp.maximum(most, store_counts(counts, at, high_ref, low_ref))
        if offset != 1:
            ref = first_ref if offset == 0 else last_ref
            ref[0:1, :] = sources
            ref[1:2, :] = picks
    over_ref[0, 0] = (most > 256.0).astype(jnp.int32)
    variables, width = out_ref.shape
    padded = jnp.concatenate(
        [out_ref[...].astype(jnp.float32), jnp.zeros((LANES - variables, width), jnp.float32)], axis=0
    )
    pad_ref[...] = padded.astype(jnp.bfloat16)
    turned_ref[...] = padded.T.astype(jnp.bfloat16)


def back_edges_kernel(count_ref, src_ref, dst_ref, left_ref, right_ref, high_ref, low_ref, over_ref):
    mesh_rows = high_ref.shape[0]
    grid_rows = high_ref.shape[1] // 3
    slots = src_ref.shape[1]
    slot = lax.broadcasted_iota(jnp.int32, (1, slots), 1)
    own = jnp.where(slot < count_ref[0, 1], dst_ref[1:2, :], -1)
    triples = (
        (left_ref[0:1, :], left_ref[1:2, :]),
        (src_ref[1:2, :], own),
        (right_ref[0:1, :], right_ref[1:2, :]),
    )
    most = 0.0
    for place, (sources, picks) in enumerate(triples):
        counts = count_pairs(sources, picks, mesh_rows, grid_rows)
        at = slice(place * grid_rows, (place + 1) * grid_rows)
        most = jnp.maximum(most, store_counts(counts, at, high_ref, low_ref))
    over_ref[0, 0] = (most > 256.0).astype(jnp.int32)


def forward_kernel(
    over_ref, high_ref, low_ref, right_ref, own_ref, left_ref, grid_ref, node_ref, turned_ref,
    shared_ref, pred_ref, normed_ref, inverse_ref, pre_ref, sum_ref,
):
    mesh_rows = own_ref.shape[0]
    rows = (right_ref, own_ref, left_ref)

    def gather(counts_ref):
        return sum(
            jnp.dot(
                counts_ref[:, i * mesh_rows : (i + 1) * mesh_rows],
                rows[i][...],
                preferred_element_type=jnp.float32,
            )
            for i in range(3)
        )

    sum_ref[...] = gather(high_ref) + grid_ref[...].astype(jnp.float32)

    @pl.when(over_ref[0, 0] > 0)
    def _():
        sum_ref[...] += gather(low_ref)

    summed = sum_ref[...]
    centered = summed - jnp.mean(summed, axis=-1, keepdims=True)
    inverse = lax.rsqrt(jnp.mean(centered * centered, axis=-1, keepdims=True) + EPS)
    normed = centered * inverse
    normed_ref[...] = normed
    inverse_ref[...] = inverse
    pre_act = jnp.dot(normed.astype(jnp.bfloat16), node_ref[...], preferred_element_type=jnp.float32)
    pre_ref[...] = pre_act
    hidden = (pre_act * (0.5 + 0.5 * jnp.tanh(0.5 * pre_act))).astype(jnp.bfloat16)
    pred = jnp.dot(hidden, turned_ref[...], preferred_element_type=jnp.float32)
    pred_ref[...] = pred
    largest = jnp.max(jnp.abs(pred), axis=0, keepdims=True)
    code = jnp.ceil(jnp.log2(jnp.maximum(largest, 2.0**LOWEST)) * CODE)
    whole = jnp.round(pred * (jnp.exp2(code * (-1.0 / CODE)) * STEPS))
    packed = fold(whole, code).astype(jnp.int16)
    for member in range(shared_ref.shape[0]):
        shared_ref[member] = packed


def fold(values, code=None):
    rest = values[MAIN:, :]
    tail = jnp.zeros((MAIN - FOLDS * rest.shape[0], LANES), values.dtype)
    if code is not None:
        wide = jnp.broadcast_to(code, tail.shape)
        row = lax.broadcasted_iota(jnp.int32, tail.shape, 0)
        for k in range(FOLDS):
            tail = jnp.where(row == k, turn(wide, VARS - FOLD * k), tail)
    pieces = [turn(rest, VARS - FOLD * k) for k in range(FOLDS)] + [tail]
    spare = jnp.concatenate(pieces, axis=0)
    main = values[:MAIN, :]
    lane = lanes_of(main)
    return jnp.where(lane < VARS, main, jnp.where(lane < VARS + FOLD, spare, jnp.zeros_like(main)))


def unfold(values, rows):
    rest_rows = rows - MAIN
    lane = lax.broadcasted_iota(jnp.int32, (rest_rows, LANES), 1)
    rest = jnp.zeros((rest_rows, LANES), values.dtype)
    for k in range(FOLDS):
        piece = turn(values[k * rest_rows : (k + 1) * rest_rows, :], FOLD * k - VARS)
        rest = jnp.where((lane >= FOLD * k) & (lane < FOLD * (k + 1)), piece, rest)
    return jnp.concatenate([values, rest], axis=0)


def middle_kernel(
    pre_ref, pred_ref, target_ref, area_ref, var_ref, node_ref,
    gate_ref, lead_ref, weight_ref, fold_ref, turned_ref, *, pair_scale
):
    pre_act = pre_ref[...]
    gate_sig = 0.5 + 0.5 * jnp.tanh(0.5 * pre_act)
    gate_ref[...] = gate_sig * (1.0 + pre_act * (1.0 - gate_sig))
    variables, grid_rows = target_ref.shape
    padded = jnp.concatenate(
        [target_ref[...], jnp.zeros((LANES - variables, grid_rows), jnp.float32)], axis=0
    )
    weight = area_ref[...] * var_ref[...]
    lead_ref[...] = weight * smooth_slope(pred_ref[...] - padded.T)
    weight_ref[...] = weight * pair_scale
    fold_ref[...] = fold(pred_ref[...])
    turned_ref[...] = node_ref[...].T


def backward_kernel(
    me_ref, everyone_ref, fold_ref, lead_ref, weight_ref, gate_ref, normed_ref, inverse_ref, pad_ref, turned_ref,
    send_ref, blocks_ref, scale_ref,
):
    members = everyone_ref.shape[0]
    grid_rows, width = normed_ref.shape
    rest_rows = grid_rows - MAIN
    me = me_ref[0]
    first = FOLDS * rest_rows
    lane = lax.broadcasted_iota(jnp.int32, (members, LANES), 1)
    tails = everyone_ref[:, first:MAIN, :].astype(jnp.float32)
    code = jnp.zeros((members, LANES), jnp.float32)
    for k in range(FOLDS):
        piece = turn(tails[:, k, :], FOLD * k - VARS)
        code = jnp.where((lane >= FOLD * k) & (lane < FOLD * (k + 1)), piece, code)
    scale = jnp.exp2(code * (1.0 / CODE)) * (1.0 / STEPS)
    for k in range(FOLDS):
        scale_ref[k] = jnp.where(lane < VARS, scale, turn(scale, VARS - FOLD * k))

    bounds = [(k * rest_rows, (k + 1) * rest_rows) for k in range(FOLDS)] + [(first, MAIN)]
    parts = [jnp.zeros((high - low, LANES), jnp.float32) for low, high in bounds]
    for step in range(1, members):
        other = lax.rem(me + step, members)
        for i, (low, high) in enumerate(bounds):
            factor = scale_ref[min(i, FOLDS - 1), pl.ds(other, 1), :]
            theirs = everyone_ref[other, low:high, :].astype(jnp.float32) * factor
            parts[i] = parts[i] + smooth_slope(fold_ref[low:high, :] - theirs)
    pair_sum = unfold(jnp.concatenate(parts, axis=0), grid_rows)
    real = lanes_of(pair_sum) < VARS
    grad_pred = lead_ref[...] - weight_ref[...] * jnp.where(real, pair_sum, 0.0)
    grad_hidden = jnp.dot(
        grad_pred.astype(jnp.bfloat16), pad_ref[...], preferred_element_type=jnp.float32
    )
    grad_pre = (grad_hidden * gate_ref[...]).astype(jnp.bfloat16)
    grad_normed = jnp.dot(grad_pre, turned_ref[...], preferred_element_type=jnp.float32)
    normed = normed_ref[...]
    grad_summed = inverse_ref[...] * (
        grad_normed
        - jnp.mean(grad_normed, axis=-1, keepdims=True)
        - normed * jnp.mean(grad_normed * normed, axis=-1, keepdims=True)
    )
    send_ref[...] = grad_summed.astype(jnp.bfloat16)
    half = grid_rows // 2
    lower = lax.broadcasted_iota(jnp.int32, (half, LANES), 1) < LANES // 2
    for pair in range(width // LANES):
        at = slice(pair * LANES, (pair + 1) * LANES)
        top = grad_summed[:half, at]
        bottom = grad_summed[half:, at]
        blocks_ref[2 * pair] = jnp.where(lower, top, turn(bottom, LANES // 2)).astype(jnp.bfloat16)
        blocks_ref[2 * pair + 1] = jnp.where(lower, turn(top, LANES // 2), bottom).astype(jnp.bfloat16)


def member_sum_kernel(landed_ref, out_ref):
    total = landed_ref[0].astype(jnp.float32)
    for member in range(1, landed_ref.shape[0]):
        total = total + landed_ref[member].astype(jnp.float32)
    half = total.shape[0]
    share = out_ref.shape[1]
    out_ref[:half, :] = total[:, :share].astype(jnp.bfloat16)
    out_ref[half:, :] = turn(total, LANES // 2)[:, :share].astype(jnp.bfloat16)


def spread_kernel(over_ref, high_ref, low_ref, left_ref, own_ref, right_ref, out_ref, sum_ref):
    rows = left_ref.shape[0]
    grads = (left_ref, own_ref, right_ref)

    def spread(counts_ref):
        return sum(
            jnp.dot(
                counts_ref[:, i * rows : (i + 1) * rows], grads[i][...], preferred_element_type=jnp.float32
            )
            for i in range(3)
        )

    sum_ref[...] = spread(high_ref)

    @pl.when(over_ref[0, 0] > 0)
    def _():
        sum_ref[...] += spread(low_ref)

    out_ref[...] = sum_ref[...].astype(jnp.bfloat16)


def shape(dims, dtype):
    return jax.ShapeDtypeStruct(dims, dtype)


SMEM = pl.BlockSpec(memory_space=pltpu.SMEM)
VMEM = pl.BlockSpec(memory_space=pltpu.VMEM)


def call(kernel, outs, ins, scratch=(), cost=(0, 0), small=()):
    return pl.pallas_call(
        kernel,
        out_shape=[o for o in outs],
        in_specs=[SMEM if ("in", i) in small else VMEM for i in range(len(ins))],
        out_specs=[SMEM if ("out", i) in small else VMEM for i in range(len(outs))],
        scratch_shapes=list(scratch),
        compiler_params=pltpu.CompilerParams(vmem_limit_bytes=VMEM_LIMIT),
        cost_estimate=pl.CostEstimate(flops=cost[0], bytes_accessed=cost[1], transcendentals=0),
    )(*ins)


def per_device(
    mesh_latent, grid_latent, node_weight, out_weight, target, area_weight, var_weight, edge_src, edge_dst, edge_count
):
    f32, b16, i32 = jnp.float32, jnp.bfloat16, jnp.int32
    members = lax.axis_size("member")
    latent = mesh_latent[0]
    mesh_rows = latent.shape[0]
    grid_rows, width = grid_latent.shape
    slots = edge_dst.shape[2]
    variables = out_weight.shape[0]
    mega = 1 << 20

    from_left = from_behind(latent, "grid", 1)
    from_right = from_behind(latent, "grid", -1)
    src, dst = edge_src[0], edge_dst[0]
    high, low, over, first_edges, last_edges, out_pad, out_turned = call(
        edges_kernel,
        [
            shape((grid_rows, 3 * mesh_rows), b16),
            shape((grid_rows, 3 * mesh_rows), b16),
            shape((1, 1), i32),
            shape((2, slots), i32),
            shape((2, slots), i32),
            shape((LANES, width), b16),
            shape((width, LANES), b16),
        ],
        [edge_count, src, dst, out_weight],
        small=(("in", 0), ("out", 2)),
        cost=(300 * mega, 2 * mega),
    )
    left_edges = from_behind(first_edges, "grid", 1)
    right_edges = from_behind(last_edges, "grid", -1)

    shared, pred, normed, inverse, pre_act = call(
        forward_kernel,
        [
            shape((members, MAIN, LANES), jnp.int16),
            shape((grid_rows, LANES), f32),
            shape((grid_rows, width), f32),
            shape((grid_rows, 1), f32),
            shape((grid_rows, width), f32),
        ],
        [over, high, low, from_right, latent, from_left, grid_latent, node_weight, out_turned],
        scratch=[pltpu.VMEM((grid_rows, width), f32)],
        small=(("in", 0),),
        cost=(1000 * mega, 8 * mega),
    )
    everyone = lax.all_to_all(shared, "member", 0, 0, tiled=True)

    back_high, back_low, back_over = call(
        back_edges_kernel,
        [
            shape((mesh_rows, 3 * grid_rows), b16),
            shape((mesh_rows, 3 * grid_rows), b16),
            shape((1, 1), i32),
        ],
        [edge_count, src, dst, left_edges, right_edges],
        small=(("in", 0), ("out", 2)),
        cost=(300 * mega, 2 * mega),
    )
    pair_scale = (1.0 - (1.0 - ALPHA) / members) / (members - 1)
    gate, lead, weight, folded, node_turned = call(
        functools.partial(middle_kernel, pair_scale=pair_scale),
        [
            shape((grid_rows, width), f32),
            shape((grid_rows, LANES), f32),
            shape((grid_rows, LANES), f32),
            shape((MAIN, LANES), f32),
            shape((width, width), b16),
        ],
        [
            pre_act,
            pred,
            target,
            area_weight[:, None],
            jnp.pad(var_weight, (0, LANES - variables))[None, :],
            node_weight,
        ],
        cost=(10 * mega, 6 * mega),
    )
    me = lax.axis_index("member").astype(i32)[None]
    grad_send, blocks = call(
        backward_kernel,
        [
            shape((grid_rows, width), b16),
            shape((members, grid_rows // 2, LANES), b16),
        ],
        [me, everyone, folded, lead, weight, gate, normed, inverse, out_pad, node_turned],
        scratch=[pltpu.VMEM((FOLDS, members, LANES), f32)],
        small=(("in", 0),),
        cost=(700 * mega, 8 * mega),
    )
    back_left = from_behind(grad_send, "grid", 1)
    back_right = from_behind(grad_send, "grid", -1)
    landed = lax.all_to_all(blocks, "member", 0, 0, tiled=True)
    (grid_share,) = call(
        member_sum_kernel,
        [shape((grid_rows, width // members), b16)],
        [landed],
        cost=(mega, mega),
    )
    (grad_latent,) = call(
        spread_kernel,
        [shape((mesh_rows, width), b16)],
        [back_over, back_high, back_low, back_left, grad_send, back_right],
        scratch=[pltpu.VMEM((mesh_rows, width), f32)],
        small=(("in", 0),),
        cost=(400 * mega, 3 * mega),
    )
    return (grad_latent[None], grid_share)


def solution(mesh):
    return jax.shard_map(
        per_device,
        mesh=mesh,
        in_specs=(
            P("member", "grid", None),
            P("grid", None),
            P(),
            P(),
            P(None, "grid"),
            P("grid"),
            P(),
            P("grid", None, None),
            P("grid", None, None),
            P("grid", None),
        ),
        out_specs=(P("member", "grid", None), P("grid", "member")),
        check_vma=False,
    )
```

time: 108 us -> 99.8 us (0.924)
  Pallas kernels: 0 us -> 12.1 us
  waiting for transfers between devices: 30.4 us -> 19 us
  matrix products: 9.47 us -> 0 us
  local copies, waits for them, and re-layouts: 15.5 us -> 23.9 us
  other arithmetic: 8.18 us -> 0 us
    unnamed x27 -> x56, local copies, waits for them, and re-layouts: 7.2 us -> 23.7 us
    pallas_call x0 -> x7, Pallas kernels: none -> 12.1 us  [call(): pl.pallas_call(kernel, out_shape=[o for o in outs], in_specs=[SMEM if ('i...]
    dot_general x10 -> x0, matrix products: 9.47 us -> none  [the longest x1 3.64 us: per_device(): lax.dot_general(grad_pre, node_weight, (((1,), (1,)), ((), ())), preferre...]
    all_to_all x1, waiting for transfers between devices: 15.2 us -> 6.12 us  [per_device(): everyone = lax.all_to_all(shared, 'member', 0, 0, tiled=True)]
    all_to_all x1, waiting for transfers between devices: 6.8 us -> 1.06 us  [per_device(): landed = lax.all_to_all(blocks, 'member', 0, 0, tiled=True)]
    ppermute x6, waiting for transfers between devices: 8.46 us -> 11.8 us  [from_behind(): return lax.ppermute(value, axis, pairs)]
    reduce_sum x3 -> x0, other arithmetic: 2.83 us -> none  [the longest x1 2.5 us: per_device(): pair_sum = jnp.sum(smooth_slope(predicted[None] - others), axis=0)]
    convert_element_type x1 -> x0, other arithmetic: 2.33 us -> none  [per_device(): grad_send = grad_summed.astype(jnp.bfloat16)]
  transfers between devices with their start and end apart: 8 -> 8, of which waited for: 4 -> 5; matrix products, arithmetic and copies ran while one was open for 13% -> 2% of each run, Pallas kernels for 0% -> 5%
where the time goes in v2:
time: 99.8 us; the launch traced here: 98.9 us
  starting transfers between devices  43.2 us (43%)
  local copies, waits for them, and re-layouts  23.9 us (24%)
  waiting for transfers between devices  19 us (19%)
  Pallas kernels  12.1 us (12%)
    ppermute x6, starting transfers between devices, from_behind(): return lax.ppermute(value, axis, pairs)  29.6 us
    unnamed x56, local copies, waits for them, and re-layouts  23.7 us
    pallas_call x7, Pallas kernels, call(): pl.pallas_call(kernel, out_shape=[o for o in outs], in_specs=[SMEM if ('i...  12.1 us
    ppermute x6, waiting for transfers between devices, from_behind(): return lax.ppermute(value, axis, pairs)  11.8 us
    all_to_all x1, starting transfers between devices, per_device(): everyone = lax.all_to_all(shared, 'member', 0, 0, tiled=True)  8.51 us
    all_to_all x1, waiting for transfers between devices, per_device(): everyone = lax.all_to_all(shared, 'member', 0, 0, tiled=True)  6.12 us
    all_to_all x1, starting transfers between devices, per_device(): landed = lax.all_to_all(blocks, 'member', 0, 0, tiled=True)  5 us
  transfers between devices with their start and end apart: 8, of which 5 were waited for; matrix products, arithmetic and copies ran while one was open for 2% of the time, Pallas kernels for 5%

profile of v2, /device:TPU:1, one launch (start us, length us, event | category | flops | bytes accessed | tf_op | source)
XLA Modules:
  0.0 98.9 jit_solution(9070967761137823614)
XLA Ops:
  0.6 13.0 %collective-permute-start.2 = (bf16[256,1024]{1,0:T(8,128)(2,1)}, bf16[256,1024]{1,0:T(8,128)(2,1)S(1)}, u32[]{:S(2)}, u32[]{:S(2)}) collective-permute-start(bf16[256,1024]{1,0:T(8,128)(2,1)} %bitcast.10), channel_id=1, source_target_pairs={{0,31},{1,0},{2,1},{3,2},{4,3},{5,4},{6,5},{7,6},{8,7},{9,8},{10,9... | collective-permute-start | bytes 1572872 | tf_op jit(solution)/shard_map/ppermute | solution.py:27
  13.6 1.9 %collective-permute-start.3 = (bf16[256,1024]{1,0:T(8,128)(2,1)}, bf16[256,1024]{1,0:T(8,128)(2,1)S(1)}, u32[]{:S(2)}, u32[]{:S(2)}) collective-permute-start(bf16[256,1024]{1,0:T(8,128)(2,1)} %bitcast.11), channel_id=1, source_target_pairs={{0,1},{1,2},{2,3},{3,4},{4,5},{5,6},{6,7},{7,8},{8,9},{9,10},{10,1... | collective-permute-start | bytes 1572872 | tf_op jit(solution)/shard_map/ppermute | solution.py:27
  17.8 1.7 %shard_map.113 = (bf16[256,768]{1,0:T(8,128)(2,1)S(1)}, bf16[256,768]{1,0:T(8,128)(2,1)S(1)}, s32[1,1]{1,0:T(1,128)}, s32[2,512]{1,0:T(2,128)S(1)}, s32[2,512]{1...) custom-call(s32[1,3]{1,0:T(1,128)S(1)} %copy-done.23, ...), custom_call_target="tpu_custom_call" | custom-call | flops 314572800 | bytes 2097152 | tf_op jit(solution)/shard_map/pallas_call | solution.py:285
  19.5 5.0 %collective-permute-done.2.right_ref = bf16[256,1024]{1,0:T(8,128)(2,1)S(1)} collective-permute-done((bf16[256,1024]{1,0:T(8,128)(2,1)}, bf16[256,1024]{1,0:T(8,128)(2,1)S(1)}, u32[]{:S(2)}, u32[]{:S(2)}) %collective-permute-start.2) | collective-permute-done | bytes 524320 | tf_op jit(solution)/shard_map/ppermute | solution.py:27
  24.5 5.8 %collective-permute-done.3.left_ref = bf16[256,1024]{1,0:T(8,128)(2,1)S(1)} collective-permute-done((bf16[256,1024]{1,0:T(8,128)(2,1)}, bf16[256,1024]{1,0:T(8,128)(2,1)S(1)}, u32[]{:S(2)}, u32[]{:S(2)}) %collective-permute-start.3) | collective-permute-done | bytes 524320 | tf_op jit(solution)/shard_map/ppermute | solution.py:27
  30.3 1.6 %copy-done = bf16[1024,1024]{1,0:T(8,128)(2,1)S(1)} copy-done((bf16[1024,1024]{1,0:T(8,128)(2,1)S(1)}, bf16[1024,1024]{1,0:T(8,128)(2,1)}, u32[]{:S(2)}) %copy-start) | copy-done | bytes 2097176
  34.0 2.8 %shard_map.115 = (s16[16,208,128]{2,1,0:T(8,128)(2,1)S(1)}, f32[256,128]{1,0:T(8,128)S(1)}, f32[256,1024]{1,0:T(8,128)S(1)}, f32[256,1]{1,0:T(8,128)S(1)}, f32[256,1024]{1,0:T(8,128)S(1)}) custom-call(s32[1,1]{1,0:T(1,128)} %get-tuple-element.29.over_ref, bf16[256,768]{1,0:T(8,128)(2,1)S(1)} %get-tuple-element.30.high_ref, ...), custom_call_target="tpu_custom_call" | custom-call | flops 1048576000 | bytes 8388608 | tf_op jit(solution)/shard_map/pallas_call | solution.py:285
  39.7 8.5 %all-to-all-start = ((s16[16,208,128]{2,1,0:T(8,128)(2,1)}), s16[16,208,128]{2,1,0:T(8,128)(2,1)S(1)}, u32[]{:S(2)}, u32[]{:S(2)}) async-start(s16[16,208,128]{2,1,0:T(8,128)(2,1)} %copy-done.10), calls=%async_computation | async-start | bytes 1703936 | tf_op jit(solution)/shard_map/all_to_all | solution.py:343
  48.4 1.2 %copy-done.5 = f32[256,1024]{1,0:T(8,128)S(1)} copy-done((f32[256,1024]{1,0:T(8,128)S(1)}, f32[256,1024]{1,0:T(8,128)}, u32[]{:S(2)}) %copy-start.5) | copy-done | bytes 1048600
  51.4 1.2 %shard_map.116 = (f32[256,1024]{1,0:T(8,128)S(1)}, f32[256,128]{1,0:T(8,128)S(1)}, f32[256,128]{1,0:T(8,128)S(1)}, f32[208,128]{1,0:T(8,128)S(1)}, bf16[1024,1024]{1,0:T(8,128)(2,1)S(1)}) custom-call(f32[256,1024]{1,0:T(8,128)S(1)} %copy-done.5, f32[256,128]{1,0:T(8,128)S(1)} %copy-done.14, f32[100,256]{1,0:T(8,128)S(1)} %copy-done.19, ...), custom_call_target="tpu_custom_call" | custom-call | flops 10485760 | bytes 6291456 | tf_op jit(solution)/shard_map/pallas_call | solution.py:285
  52.6 1.4 %copy-done.2 = bf16[1024,1024]{1,0:T(8,128)(2,1)} copy-done((bf16[1024,1024]{1,0:T(8,128)(2,1)}, bf16[1024,1024]{1,0:T(8,128)(2,1)S(1)}, u32[]{:S(2)}) %copy-start.2) | copy-done | bytes 2097176
  57.0 6.1 %all-to-all-done.everyone_ref = s16[16,208,128]{2,1,0:T(8,128)(2,1)S(1)} async-done(((s16[16,208,128]{2,1,0:T(8,128)(2,1)}), s16[16,208,128]{2,1,0:T(8,128)(2,1)S(1)}, u32[]{:S(2)}, u32[]{:S(2)}) %all-to-all-start) | async-done | bytes 852000 | tf_op jit(solution)/shard_map/all_to_all | solution.py:343
  63.1 1.6 %copy-done.3 = bf16[1024,1024]{1,0:T(8,128)(2,1)S(1)} copy-done((bf16[1024,1024]{1,0:T(8,128)(2,1)S(1)}, bf16[1024,1024]{1,0:T(8,128)(2,1)}, u32[]{:S(2)}) %copy-start.3) | copy-done | bytes 2097176
  64.7 1.2 %copy-done.7 = f32[256,1024]{1,0:T(8,128)S(1)} copy-done((f32[256,1024]{1,0:T(8,128)S(1)}, f32[256,1024]{1,0:T(8,128)}, u32[]{:S(2)}) %copy-start.7) | copy-done | bytes 1048600
  65.9 1.2 %copy-done.9 = f32[256,1024]{1,0:T(8,128)S(1)} copy-done((f32[256,1024]{1,0:T(8,128)S(1)}, f32[256,1024]{1,0:T(8,128)}, u32[]{:S(2)}) %copy-start.9) | copy-done | bytes 1048600
  69.8 2.6 %shard_map.117 = (bf16[256,1024]{1,0:T(8,128)(2,1)S(1)}, bf16[16,128,128]{2,1,0:T(8,128)(2,1)}) custom-call(s32[1]{0:T(128)} %bitcast.me_ref, s16[16,208,128]{2,1,0:T(8,128)(2,1)S(1)} %all-to-all-done.everyone_ref, f32[208,128]{1,0:T(8,128)S(1)} %copy-done.21, f32[256,128]{1,0:T(8,128)S(1)} %copy-done.16, f32[256,128]{1,0:T(8,128)S(1)} %copy-done.18, ...), custom_call_target="tpu_custom_call" | custom-call | flops 734003200 | bytes 8388608 | tf_op jit(solution)/shard_map/pallas_call | solution.py:285
  72.5 1.9 %collective-permute-start.4 = (bf16[256,1024]{1,0:T(8,128)(2,1)S(1)}, bf16[256,1024]{1,0:T(8,128)(2,1)S(1)}, u32[]{:S(2)}, u32[]{:S(2)}) collective-permute-start(bf16[256,1024]{1,0:T(8,128)(2,1)S(1)} %get-tuple-element.44.own_ref), channel_id=1, source_target_pairs={{0,1},{1,2},{2,3},{3,4},{4,5},{5,6},{6,7},{7,8},{8,9},{9,10},{10,1... | collective-permute-start | bytes 1572872 | tf_op jit(solution)/shard_map/ppermute | solution.py:27
  74.4 5.5 %collective-permute-start.5 = (bf16[256,1024]{1,0:T(8,128)(2,1)S(1)}, bf16[256,1024]{1,0:T(8,128)(2,1)S(1)}, u32[]{:S(2)}, u32[]{:S(2)}) collective-permute-start(bf16[256,1024]{1,0:T(8,128)(2,1)S(1)} %get-tuple-element.44.own_ref), channel_id=1, source_target_pairs={{0,31},{1,0},{2,1},{3,2},{4,3},{5,4},{6,5},{7,6},{8,7},{9,8},{10,9... | collective-permute-start | bytes 1572872 | tf_op jit(solution)/shard_map/ppermute | solution.py:27
  79.9 5.0 %all-to-all-start.1 = ((bf16[16,128,128]{2,1,0:T(8,128)(2,1)}), bf16[16,128,128]{2,1,0:T(8,128)(2,1)S(1)}, u32[]{:S(2)}, u32[]{:S(2)}) async-start(bf16[16,128,128]{2,1,0:T(8,128)(2,1)} %get-tuple-element.45), calls=%async_computation.1 | async-start | bytes 1048576 | tf_op jit(solution)/shard_map/all_to_all | solution.py:390
  84.9 1.9 %collective-permute-start = (s32[2,512]{1,0:T(2,128)S(1)}, s32[2,512]{1,0:T(2,128)S(1)}, u32[]{:S(2)}, u32[]{:S(2)}) collective-permute-start(s32[2,512]{1,0:T(2,128)S(1)} %get-tuple-element.24), channel_id=1, source_target_pairs={{0,1},{1,2},{2,3},{3,4},{4,5},{5,6},{6,7},{7,8},{8,9},{9,10},{10,1... | collective-permute-start | bytes 12296 | tf_op jit(solution)/shard_map/ppermute | solution.py:27
  86.8 5.5 %collective-permute-start.1 = (s32[2,512]{1,0:T(2,128)S(1)}, s32[2,512]{1,0:T(2,128)S(1)}, u32[]{:S(2)}, u32[]{:S(2)}) collective-permute-start(s32[2,512]{1,0:T(2,128)S(1)} %get-tuple-element.25), channel_id=1, source_target_pairs={{0,31},{1,0},{2,1},{3,2},{4,3},{5,4},{6,5},{7,6},{8,7},{9,8},{10,9... | collective-permute-start | bytes 12296 | tf_op jit(solution)/shard_map/ppermute | solution.py:27
  92.3 1.1 %collective-permute-done.1.right_ref = s32[2,512]{1,0:T(2,128)S(1)} collective-permute-done((s32[2,512]{1,0:T(2,128)S(1)}, s32[2,512]{1,0:T(2,128)S(1)}, u32[]{:S(2)}, u32[]{:S(2)}) %collective-permute-start.1) | collective-permute-done | bytes 4128 | tf_op jit(solution)/shard_map/ppermute | solution.py:27
  93.3 1.6 %shard_map.114 = (bf16[256,768]{1,0:T(8,128)(2,1)S(1)}, bf16[256,768]{1,0:T(8,128)(2,1)S(1)}, s32[1,1]{1,0:T(1,128)}) custom-call(s32[1,3]{1,0:T(1,128)S(1)} %copy-done.24, s32[3,512]{1,0:T(4,128)S(1)} %get-tuple-element.51.src_ref, s32[3,512]{1,0:T(4,128)S(1)} %get-tuple-element.50.dst_ref, s32[2,512]{1,0:T(2,128)S(1)} %collective-permute-done.left_ref, ...), custom_call_target="tpu_custom_call" | custom-call | flops 314572800 | bytes 2097152 | tf_op jit(solution)/shard_map/pallas_call | solution.py:285
  96.9 2.0 %shard_map.118 = bf16[256,1024]{1,0:T(8,128)(2,1)} custom-call(s32[1,1]{1,0:T(1,128)} %get-tuple-element.26.over_ref, bf16[256,768]{1,0:T(8,128)(2,1)S(1)} %get-tuple-element.27.high_ref, bf16[256,768]{1,0:T(8,128)(2,1)S(1)} %get-tuple-element.28.low_ref, bf16[256,1024]{1,0:T(8,128)(2,1)S(1)} %collective-permute-done.4.left_ref, ...), custom_call_target="tpu_custom_call" | custom-call | flops 419430400 | bytes 3145728 | tf_op jit(solution)/shard_map/pallas_call | solution.py:285
  (57 shorter events, 16.9 us)
Async XLA Ops:
  0.6 23.9 %collective-permute-start.2 = (bf16[256,1024]{1,0:T(8,128)(2,1)}, bf16[256,1024]{1,0:T(8,128)(2,1)S(1)}, u32[]{:S(2)}, u32[]{:S(2)}) collective-permute-start(bf16[256,1024]{1,0:T(8,128)(2,1)} %bitcast.10), channel_id=1, source_target_pairs={{0,31},{1,0},{2,1},{3,2},{4,3},{5,4},{6,5},{7,6},{8,7},{9,8},{10,9... | collective-permute-start | bytes 1572872 | tf_op jit(solution)/shard_map/ppermute | solution.py:27
  13.6 16.7 %collective-permute-start.3 = (bf16[256,1024]{1,0:T(8,128)(2,1)}, bf16[256,1024]{1,0:T(8,128)(2,1)S(1)}, u32[]{:S(2)}, u32[]{:S(2)}) collective-permute-start(bf16[256,1024]{1,0:T(8,128)(2,1)} %bitcast.11), channel_id=1, source_target_pairs={{0,1},{1,2},{2,3},{3,4},{4,5},{5,6},{6,7},{7,8},{8,9},{9,10},{10,1... | collective-permute-start | bytes 1572872 | tf_op jit(solution)/shard_map/ppermute | solution.py:27
  30.3 1.6 %copy-start = (bf16[1024,1024]{1,0:T(8,128)(2,1)S(1)}, bf16[1024,1024]{1,0:T(8,128)(2,1)}, u32[]{:S(2)}) copy-start(bf16[1024,1024]{1,0:T(8,128)(2,1)} %node_ref.3) | copy-start | bytes 6291460
  31.9 1.0 %copy-start.11 = (bf16[1,256,1024]{2,1,0:T(8,128)(2,1)S(1)}, bf16[1,256,1024]{2,1,0:T(8,128)(2,1)}, u32[]{:S(2)}) copy-start(bf16[1,256,1024]{2,1,0:T(8,128)(2,1)} %param.10) | copy-start | bytes 1572868
  32.9 1.0 %copy-start.12 = (bf16[256,1024]{1,0:T(8,128)(2,1)S(1)}, bf16[256,1024]{1,0:T(8,128)(2,1)}, u32[]{:S(2)}) copy-start(bf16[256,1024]{1,0:T(8,128)(2,1)} %grid_ref.1) | copy-start | bytes 1572868
  34.0 14.2 %copy-start.25 = (f32[256]{0:T(256)S(1)}, f32[256]{0:T(256)}, u32[]{:S(2)}) copy-start(f32[256]{0:T(256)} %param.15) | copy-start | bytes 3076
  34.0 14.4 %copy-start.26 = (f32[100]{0:T(128)S(1)}, f32[100]{0:T(128)}, u32[]{:S(2)}) copy-start(f32[100]{0:T(128)} %param.16) | copy-start | bytes 1204
  34.0 14.4 %copy-start.1 = (bf16[1024,1024]{1,0:T(8,128)(2,1)S(1)}, bf16[1024,1024]{1,0:T(8,128)(2,1)}, u32[]{:S(2)}) copy-start(bf16[1024,1024]{1,0:T(8,128)(2,1)} %node_ref.3) | copy-start | bytes 6291460
  36.7 1.0 %copy-start.4 = (f32[256,1024]{1,0:T(8,128)}, f32[256,1024]{1,0:T(8,128)S(1)}, u32[]{:S(2)}) copy-start(f32[256,1024]{1,0:T(8,128)S(1)} %get-tuple-element.34.pre_ref) | copy-start | bytes 3145732
  37.7 1.0 %copy-start.6 = (f32[256,1024]{1,0:T(8,128)}, f32[256,1024]{1,0:T(8,128)S(1)}, u32[]{:S(2)}) copy-start(f32[256,1024]{1,0:T(8,128)S(1)} %get-tuple-element.40.normed_ref) | copy-start | bytes 3145732
  39.7 8.5 %copy-start.13 = (f32[256,128]{1,0:T(8,128)}, f32[256,128]{1,0:T(8,128)S(1)}, u32[]{:S(2)}) copy-start(f32[256,128]{1,0:T(8,128)S(1)} %get-tuple-element.35.pred_ref) | copy-start | bytes 393220
  39.7 23.4 %all-to-all-start = ((s16[16,208,128]{2,1,0:T(8,128)(2,1)}), s16[16,208,128]{2,1,0:T(8,128)(2,1)S(1)}, u32[]{:S(2)}, u32[]{:S(2)}) async-start(s16[16,208,128]{2,1,0:T(8,128)(2,1)} %copy-done.10), calls=%async_computation | async-start | bytes 1703936 | tf_op jit(solution)/shard_map/all_to_all | solution.py:343
  48.4 1.2 %copy-start.5 = (f32[256,1024]{1,0:T(8,128)S(1)}, f32[256,1024]{1,0:T(8,128)}, u32[]{:S(2)}) copy-start(f32[256,1024]{1,0:T(8,128)} %copy-done.4) | copy-start | bytes 3145732
  52.6 1.4 %copy-start.2 = (bf16[1024,1024]{1,0:T(8,128)(2,1)}, bf16[1024,1024]{1,0:T(8,128)(2,1)S(1)}, u32[]{:S(2)}) copy-start(bf16[1024,1024]{1,0:T(8,128)(2,1)S(1)} %get-tuple-element.43.turned_ref) | copy-start | bytes 6291460
  54.0 1.0 %copy-start.8 = (f32[256,1024]{1,0:T(8,128)}, f32[256,1024]{1,0:T(8,128)S(1)}, u32[]{:S(2)}) copy-start(f32[256,1024]{1,0:T(8,128)S(1)} %get-tuple-element.39.gate_ref) | copy-start | bytes 3145732
  63.1 1.6 %copy-start.3 = (bf16[1024,1024]{1,0:T(8,128)(2,1)S(1)}, bf16[1024,1024]{1,0:T(8,128)(2,1)}, u32[]{:S(2)}) copy-start(bf16[1024,1024]{1,0:T(8,128)(2,1)} %copy-done.2) | copy-start | bytes 6291460
  64.7 1.2 %copy-start.7 = (f32[256,1024]{1,0:T(8,128)S(1)}, f32[256,1024]{1,0:T(8,128)}, u32[]{:S(2)}) copy-start(f32[256,1024]{1,0:T(8,128)} %copy-done.6) | copy-start | bytes 3145732
  65.9 1.2 %copy-start.9 = (f32[256,1024]{1,0:T(8,128)S(1)}, f32[256,1024]{1,0:T(8,128)}, u32[]{:S(2)}) copy-start(f32[256,1024]{1,0:T(8,128)} %copy-done.8) | copy-start | bytes 3145732
  69.8 23.5 %copy-start.24 = (s32[1,3]{1,0:T(1,128)S(1)}, s32[1,3]{1,0:T(1,128)}, u32[]{:S(2)}) copy-start(s32[1,3]{1,0:T(1,128)} %count_ref.3) | copy-start | bytes 40
  72.5 24.4 %collective-permute-start.4 = (bf16[256,1024]{1,0:T(8,128)(2,1)S(1)}, bf16[256,1024]{1,0:T(8,128)(2,1)S(1)}, u32[]{:S(2)}, u32[]{:S(2)}) collective-permute-start(bf16[256,1024]{1,0:T(8,128)(2,1)S(1)} %get-tuple-element.44.own_ref), channel_id=1, source_target_pairs={{0,1},{1,2},{2,3},{3,4},{4,5},{5,6},{6,7},{7,8},{8,9},{9,10},{10,1... | collective-permute-start | bytes 1572872 | tf_op jit(solution)/shard_map/ppermute | solution.py:27
  74.4 22.5 %collective-permute-start.5 = (bf16[256,1024]{1,0:T(8,128)(2,1)S(1)}, bf16[256,1024]{1,0:T(8,128)(2,1)S(1)}, u32[]{:S(2)}, u32[]{:S(2)}) collective-permute-start(bf16[256,1024]{1,0:T(8,128)(2,1)S(1)} %get-tuple-element.44.own_ref), channel_id=1, source_target_pairs={{0,31},{1,0},{2,1},{3,2},{4,3},{5,4},{6,5},{7,6},{8,7},{9,8},{10,9... | collective-permute-start | bytes 1572872 | tf_op jit(solution)/shard_map/ppermute | solution.py:27
  79.9 16.2 %all-to-all-start.1 = ((bf16[16,128,128]{2,1,0:T(8,128)(2,1)}), bf16[16,128,128]{2,1,0:T(8,128)(2,1)S(1)}, u32[]{:S(2)}, u32[]{:S(2)}) async-start(bf16[16,128,128]{2,1,0:T(8,128)(2,1)} %get-tuple-element.45), calls=%async_computation.1 | async-start | bytes 1048576 | tf_op jit(solution)/shard_map/all_to_all | solution.py:390
  84.9 7.4 %collective-permute-start = (s32[2,512]{1,0:T(2,128)S(1)}, s32[2,512]{1,0:T(2,128)S(1)}, u32[]{:S(2)}, u32[]{:S(2)}) collective-permute-start(s32[2,512]{1,0:T(2,128)S(1)} %get-tuple-element.24), channel_id=1, source_target_pairs={{0,1},{1,2},{2,3},{3,4},{4,5},{5,6},{6,7},{7,8},{8,9},{9,10},{10,1... | collective-permute-start | bytes 12296 | tf_op jit(solution)/shard_map/ppermute | solution.py:27
  86.8 6.6 %collective-permute-start.1 = (s32[2,512]{1,0:T(2,128)S(1)}, s32[2,512]{1,0:T(2,128)S(1)}, u32[]{:S(2)}, u32[]{:S(2)}) collective-permute-start(s32[2,512]{1,0:T(2,128)S(1)} %get-tuple-element.25), channel_id=1, source_target_pairs={{0,31},{1,0},{2,1},{3,2},{4,3},{5,4},{6,5},{7,6},{8,7},{9,8},{10,9... | collective-permute-start | bytes 12296 | tf_op jit(solution)/shard_map/ppermute | solution.py:27
  (11 other events, 9.0 us)

commit v3 on v2

v3 whole, which is shorter than its diff:
```python
import functools

import jax
import jax.numpy as jnp
from jax import lax
from jax.experimental import pallas as pl
from jax.experimental.pallas import tpu as pltpu
from jax.sharding import PartitionSpec as P

SMOOTH = 0.1
ALPHA = 0.95
EPS = 1e-05
LANES = 128
VARS = 100
MAIN = 208
FOLD = 25
FOLDS = 4
STEPS = 32767.0
CODE = 256.0
LOWEST = -20.0
VMEM_LIMIT = 48 * 1024 * 1024


def to_neighbours(value, side):
    members, shards = lax.axis_size("member"), lax.axis_size("grid")
    pairs = [
        (member * shards + shard, member * shards + (shard + (1 if member % 2 == side else -1)) % shards)
        for member in range(members)
        for shard in range(shards)
    ]
    return lax.ppermute(value, ("member", "grid"), pairs)


def smooth_slope(difference):
    return difference * lax.rsqrt(difference * difference + SMOOTH * SMOOTH)


def turn(values, shift):
    shift = shift % LANES
    return pltpu.roll(values, shift, 1) if shift else values


def lanes_of(values):
    return lax.broadcasted_iota(jnp.int32, values.shape, 1)


def one_hot(picks, rows):
    places = lax.broadcasted_iota(jnp.int32, (rows, picks.shape[1]), 0)
    return jnp.where(places == picks, 1.0, 0.0).astype(jnp.bfloat16)


def count_pairs(row_hot, column_hot):
    return lax.dot_general(
        row_hot, column_hot, (((1,), (1,)), ((), ())), preferred_element_type=jnp.float32
    )


def store_counts(counts, at, high_ref, low_ref):
    high = counts.astype(jnp.bfloat16)
    high_ref[:, at] = high
    low_ref[:, at] = (counts - high.astype(jnp.float32)).astype(jnp.bfloat16)
    return jnp.max(counts)


def edges_kernel(
    me_ref, count_ref, src_ref, dst_ref, out_ref,
    high_ref, low_ref, back_high_ref, back_low_ref, over_ref, pad_ref, turned_ref,
):
    size = high_ref.shape[0]
    slots = src_ref.shape[1]
    slot = lax.broadcasted_iota(jnp.int32, (1, slots), 1)
    odd = lax.rem(me_ref[0], 2)
    most = 0.0
    for place, offset in enumerate((2 - 2 * odd, 1, 2 * odd)):
        live = slot < count_ref[0, offset]
        targets = one_hot(jnp.where(live, dst_ref[pl.ds(offset, 1), :], -1), size)
        sources = one_hot(src_ref[pl.ds(offset, 1), :], size)
        counts = count_pairs(targets, sources)
        most = jnp.maximum(
            most, store_counts(counts, slice(place * size, (place + 1) * size), high_ref, low_ref)
        )
        back = 2 - place
        store_counts(
            count_pairs(sources, targets), slice(back * size, (back + 1) * size), back_high_ref, back_low_ref
        )
    over_ref[0] = (most > 256.0).astype(jnp.int32)
    variables, width = out_ref.shape
    padded = jnp.concatenate(
        [out_ref[...].astype(jnp.float32), jnp.zeros((LANES - variables, width), jnp.float32)], axis=0
    )
    pad_ref[...] = padded.astype(jnp.bfloat16)
    turned_ref[...] = padded.T.astype(jnp.bfloat16)


def start_all(sources, targets, sems):
    copies = [pltpu.make_async_copy(s, t, sems.at[i]) for i, (s, t) in enumerate(zip(sources, targets))]
    for copy in copies:
        copy.start()
    return copies


def dot(left, right):
    return jnp.dot(left, right, preferred_element_type=jnp.float32)


def forward_kernel(
    over_ref, high_hbm, own_hbm, first_hbm, second_hbm, grid_hbm, node_hbm, turned_hbm, low_hbm,
    shared_hbm, pred_hbm, normed_hbm, inverse_hbm, pre_hbm,
    high_ref, own_ref, first_ref, second_ref, grid_ref, node_ref, turned_ref, low_ref,
    packed_ref, pred_ref, normed_ref, inverse_ref, pre_ref, sum_ref,
    in_sems, low_sem, out_sems, share_sems,
):
    size = own_ref.shape[0]
    loads = start_all(
        (high_hbm, own_hbm, first_hbm, second_hbm, grid_hbm, node_hbm, turned_hbm),
        (high_ref, own_ref, first_ref, second_ref, grid_ref, node_ref, turned_ref),
        in_sems,
    )
    outs = [
        pltpu.make_async_copy(s, t, out_sems.at[i])
        for i, (s, t) in enumerate(
            ((normed_ref, normed_hbm), (inverse_ref, inverse_hbm), (pre_ref, pre_hbm), (pred_ref, pred_hbm))
        )
    ]
    for load in loads[:5]:
        load.wait()

    def gather(counts_ref):
        return (
            dot(counts_ref[:, :size], first_ref[...])
            + dot(counts_ref[:, size : 2 * size], own_ref[...])
            + dot(counts_ref[:, 2 * size :], second_ref[...])
        )

    sum_ref[...] = gather(high_ref) + grid_ref[...].astype(jnp.float32)

    @pl.when(over_ref[0] > 0)
    def _():
        copy = pltpu.make_async_copy(low_hbm, low_ref, low_sem)
        copy.start()
        copy.wait()
        sum_ref[...] += gather(low_ref)

    summed = sum_ref[...]
    centered = summed - jnp.mean(summed, axis=-1, keepdims=True)
    inverse = lax.rsqrt(jnp.mean(centered * centered, axis=-1, keepdims=True) + EPS)
    normed = centered * inverse
    normed_ref[...] = normed
    inverse_ref[...] = inverse
    outs[0].start()
    outs[1].start()
    loads[5].wait()
    pre_act = dot(normed.astype(jnp.bfloat16), node_ref[...])
    pre_ref[...] = pre_act
    outs[2].start()
    hidden = (pre_act * (0.5 + 0.5 * jnp.tanh(0.5 * pre_act))).astype(jnp.bfloat16)
    loads[6].wait()
    pred = dot(hidden, turned_ref[...])
    pred_ref[...] = pred
    outs[3].start()
    largest = jnp.max(jnp.abs(pred), axis=0, keepdims=True)
    code = jnp.ceil(jnp.log2(jnp.maximum(largest, 2.0**LOWEST)) * CODE)
    whole = jnp.round(pred * (jnp.exp2(code * (-1.0 / CODE)) * STEPS))
    packed_ref[...] = fold(whole, code).astype(jnp.int16)
    members = shared_hbm.shape[0]
    shares = start_all([packed_ref] * members, [shared_hbm.at[m] for m in range(members)], share_sems)
    for copy in outs + shares:
        copy.wait()


def fold(values, code=None):
    rest = values[MAIN:, :]
    tail = jnp.zeros((MAIN - FOLDS * rest.shape[0], LANES), values.dtype)
    if code is not None:
        wide = jnp.broadcast_to(code, tail.shape)
        row = lax.broadcasted_iota(jnp.int32, tail.shape, 0)
        for k in range(FOLDS):
            tail = jnp.where(row == k, turn(wide, VARS - FOLD * k), tail)
    pieces = [turn(rest, VARS - FOLD * k) for k in range(FOLDS)] + [tail]
    spare = jnp.concatenate(pieces, axis=0)
    main = values[:MAIN, :]
    lane = lanes_of(main)
    return jnp.where(lane < VARS, main, jnp.where(lane < VARS + FOLD, spare, jnp.zeros_like(main)))


def unfold(values, rows):
    rest_rows = rows - MAIN
    lane = lax.broadcasted_iota(jnp.int32, (rest_rows, LANES), 1)
    rest = jnp.zeros((rest_rows, LANES), values.dtype)
    for k in range(FOLDS):
        piece = turn(values[k * rest_rows : (k + 1) * rest_rows, :], FOLD * k - VARS)
        rest = jnp.where((lane >= FOLD * k) & (lane < FOLD * (k + 1)), piece, rest)
    return jnp.concatenate([values, rest], axis=0)


def middle_kernel(
    pre_ref, pred_ref, target_ref, area_ref, var_ref, node_ref,
    gate_ref, lead_ref, weight_ref, fold_ref, turned_ref, *, pair_scale
):
    pre_act = pre_ref[...]
    gate_sig = 0.5 + 0.5 * jnp.tanh(0.5 * pre_act)
    gate_ref[...] = gate_sig * (1.0 + pre_act * (1.0 - gate_sig))
    variables, grid_rows = target_ref.shape
    padded = jnp.concatenate(
        [target_ref[...], jnp.zeros((LANES - variables, grid_rows), jnp.float32)], axis=0
    )
    weight = area_ref[...] * var_ref[...]
    lead_ref[...] = weight * smooth_slope(pred_ref[...] - padded.T)
    weight_ref[...] = weight * pair_scale
    fold_ref[...] = fold(pred_ref[...])
    turned_ref[...] = node_ref[...].T


def backward_kernel(
    me_ref, over_ref,
    everyone_hbm, fold_hbm, lead_hbm, weight_hbm, pad_hbm, gate_hbm, turned_hbm, normed_hbm, inverse_hbm, counts_hbm, low_hbm,
    first_hbm, second_hbm, blocks_hbm, send_hbm,
    everyone_ref, fold_ref, lead_ref, weight_ref, pad_ref, gate_ref, turned_ref, normed_ref, inverse_ref, counts_ref, low_ref,
    first_ref, second_ref, blocks_ref, send_ref, scale_ref,
    in_sems, low_sem, out_sems,
):
    loads = start_all(
        (everyone_hbm, fold_hbm, lead_hbm, weight_hbm, pad_hbm, gate_hbm, turned_hbm, normed_hbm, inverse_hbm, counts_hbm),
        (everyone_ref, fold_ref, lead_ref, weight_ref, pad_ref, gate_ref, turned_ref, normed_ref, inverse_ref, counts_ref),
        in_sems,
    )
    outs = [
        pltpu.make_async_copy(s, t, out_sems.at[i])
        for i, (s, t) in enumerate(
            ((send_ref, send_hbm), (first_ref, first_hbm), (second_ref, second_hbm), (blocks_ref, blocks_hbm))
        )
    ]
    members = everyone_ref.shape[0]
    grid_rows, width = normed_ref.shape
    rest_rows = grid_rows - MAIN
    me = me_ref[0]
    first = FOLDS * rest_rows
    lane = lax.broadcasted_iota(jnp.int32, (members, LANES), 1)
    loads[0].wait()
    loads[1].wait()
    tails = everyone_ref[:, first:MAIN, :].astype(jnp.float32)
    code = jnp.zeros((members, LANES), jnp.float32)
    for k in range(FOLDS):
        piece = turn(tails[:, k, :], FOLD * k - VARS)
        code = jnp.where((lane >= FOLD * k) & (lane < FOLD * (k + 1)), piece, code)
    scale = jnp.exp2(code * (1.0 / CODE)) * (1.0 / STEPS)
    for k in range(FOLDS):
        scale_ref[k] = jnp.where(lane < VARS, scale, turn(scale, VARS - FOLD * k))

    bounds = [(k * rest_rows, (k + 1) * rest_rows) for k in range(FOLDS)] + [(first, MAIN)]
    parts = [jnp.zeros((high - low, LANES), jnp.float32) for low, high in bounds]
    for step in range(1, members):
        other = lax.rem(me + step, members)
        for i, (low, high) in enumerate(bounds):
            factor = scale_ref[min(i, FOLDS - 1), pl.ds(other, 1), :]
            theirs = everyone_ref[other, low:high, :].astype(jnp.float32) * factor
            parts[i] = parts[i] + smooth_slope(fold_ref[low:high, :] - theirs)
    pair_sum = unfold(jnp.concatenate(parts, axis=0), grid_rows)
    real = lanes_of(pair_sum) < VARS
    for load in loads[2:6]:
        load.wait()
    grad_pred = lead_ref[...] - weight_ref[...] * jnp.where(real, pair_sum, 0.0)
    grad_hidden = dot(grad_pred.astype(jnp.bfloat16), pad_ref[...])
    grad_pre = (grad_hidden * gate_ref[...]).astype(jnp.bfloat16)
    for load in loads[6:]:
        load.wait()
    grad_normed = dot(grad_pre, turned_ref[...])
    normed = normed_ref[...]
    grad_summed = inverse_ref[...] * (
        grad_normed
        - jnp.mean(grad_normed, axis=-1, keepdims=True)
        - normed * jnp.mean(grad_normed * normed, axis=-1, keepdims=True)
    )
    send_ref[...] = grad_summed.astype(jnp.bfloat16)
    outs[0].start()
    half = grid_rows // 2
    lower = lax.broadcasted_iota(jnp.int32, (half, LANES), 1) < LANES // 2
    for pair in range(width // LANES):
        at = slice(pair * LANES, (pair + 1) * LANES)
        top = grad_summed[:half, at]
        bottom = grad_summed[half:, at]
        blocks_ref[2 * pair] = jnp.where(lower, top, turn(bottom, LANES // 2)).astype(jnp.bfloat16)
        blocks_ref[2 * pair + 1] = jnp.where(lower, turn(top, LANES // 2), bottom).astype(jnp.bfloat16)
    outs[3].start()
    size = first_ref.shape[0]
    first_ref[...] = dot(counts_ref[:, :grid_rows], send_ref[...]).astype(jnp.bfloat16)
    second_ref[...] = dot(counts_ref[:, 2 * grid_rows :], send_ref[...]).astype(jnp.bfloat16)

    @pl.when(over_ref[0] > 0)
    def _():
        copy = pltpu.make_async_copy(low_hbm, low_ref, low_sem)
        copy.start()
        copy.wait()
        for ref, at in ((first_ref, slice(0, grid_rows)), (second_ref, slice(2 * grid_rows, 3 * grid_rows))):
            total = dot(counts_ref[:, at], send_ref[...]) + dot(low_ref[:, at], send_ref[...])
            ref[...] = total.astype(jnp.bfloat16)

    outs[1].start()
    outs[2].start()
    for copy in outs:
        copy.wait()


def own_kernel(over_ref, high_ref, low_ref, send_ref, out_ref):
    rows = send_ref.shape[0]
    out_ref[...] = dot(high_ref[:, rows : 2 * rows], send_ref[...])

    @pl.when(over_ref[0] > 0)
    def _():
        out_ref[...] += dot(low_ref[:, rows : 2 * rows], send_ref[...])


def member_sum_kernel(landed_ref, out_ref):
    total = landed_ref[0].astype(jnp.float32)
    for member in range(1, landed_ref.shape[0]):
        total = total + landed_ref[member].astype(jnp.float32)
    half = total.shape[0]
    share = out_ref.shape[0]
    flipped = total.T
    out_ref[:, :half] = flipped[:share, :].astype(jnp.bfloat16)
    out_ref[:, half:] = flipped[share:, :].astype(jnp.bfloat16)


def shape(dims, dtype):
    return jax.ShapeDtypeStruct(dims, dtype)


def whole(value):
    dims = value.shape
    return pl.BlockSpec(dims, lambda step: (0,) * len(dims))


SMEM = pl.BlockSpec(memory_space=pltpu.SMEM)
HBM = pl.BlockSpec(memory_space=pltpu.HBM)


def cost_of(mega_flops, mega_bytes):
    return pl.CostEstimate(
        flops=mega_flops << 20, bytes_accessed=mega_bytes << 20, transcendentals=0
    )


PARAMS = pltpu.CompilerParams(vmem_limit_bytes=VMEM_LIMIT)


def staged(kernel, outs, ins, scalars_in=(), scalars_out=(), cost=(0, 0)):
    return pl.pallas_call(
        kernel,
        grid=(1,),
        out_shape=list(outs),
        in_specs=[SMEM if i in scalars_in else whole(v) for i, v in enumerate(ins)],
        out_specs=[SMEM if i in scalars_out else whole(v) for i, v in enumerate(outs)],
        compiler_params=PARAMS,
        cost_estimate=cost_of(*cost),
    )(*ins)


def held(value):
    return pltpu.VMEM(value.shape, value.dtype)


def per_device(
    mesh_latent, grid_latent, node_weight, out_weight, target, area_weight, var_weight, edge_src, edge_dst, edge_count
):
    f32, b16, i32 = jnp.float32, jnp.bfloat16, jnp.int32
    members = lax.axis_size("member")
    me = lax.axis_index("member").astype(i32)[None]
    latent = mesh_latent[0]
    mesh_rows = latent.shape[0]
    grid_rows, width = grid_latent.shape
    variables = out_weight.shape[0]
    dma = pltpu.SemaphoreType.DMA

    first = to_neighbours(latent, 0)
    second = to_neighbours(latent, 1)
    high, low, back_high, back_low, over, out_pad, out_turned = staged(
        edges_kernel,
        [
            shape((grid_rows, 3 * mesh_rows), b16),
            shape((grid_rows, 3 * mesh_rows), b16),
            shape((mesh_rows, 3 * grid_rows), b16),
            shape((mesh_rows, 3 * grid_rows), b16),
            shape((1,), i32),
            shape((LANES, width), b16),
            shape((width, LANES), b16),
        ],
        [me, edge_count, edge_src[0], edge_dst[0], out_weight],
        scalars_in=(0, 1),
        scalars_out=(4,),
        cost=(400, 3),
    )

    ins = [high, latent, first, second, grid_latent, node_weight, out_turned, low]
    outs = [
        shape((members, MAIN, LANES), jnp.int16),
        shape((grid_rows, LANES), f32),
        shape((grid_rows, width), f32),
        shape((grid_rows, 1), f32),
        shape((grid_rows, width), f32),
    ]
    shared, pred, normed, inverse, pre_act = pl.pallas_call(
        forward_kernel,
        out_shape=outs,
        in_specs=[SMEM] + [HBM] * len(ins),
        out_specs=[HBM] * len(outs),
        scratch_shapes=[held(v) for v in ins]
        + [pltpu.VMEM((MAIN, LANES), jnp.int16)]
        + [held(v) for v in outs[1:]]
        + [pltpu.VMEM((grid_rows, width), f32), dma((len(ins) - 1,)), dma, dma((len(outs) - 1,)), dma((members,))],
        compiler_params=PARAMS,
        cost_estimate=cost_of(1000, 8),
    )(over, *ins)
    everyone = lax.all_to_all(shared, "member", 0, 0, tiled=True)

    pair_scale = (1.0 - (1.0 - ALPHA) / members) / (members - 1)
    gate, lead, weight, folded, node_turned = staged(
        functools.partial(middle_kernel, pair_scale=pair_scale),
        [
            shape((grid_rows, width), f32),
            shape((grid_rows, LANES), f32),
            shape((grid_rows, LANES), f32),
            shape((MAIN, LANES), f32),
            shape((width, width), b16),
        ],
        [
            pre_act,
            pred,
            target,
            area_weight[:, None],
            jnp.pad(var_weight, (0, LANES - variables))[None, :],
            node_weight,
        ],
        cost=(10, 8),
    )

    ins = [everyone, folded, lead, weight, out_pad, gate, node_turned, normed, inverse, back_high, back_low]
    outs = [
        shape((mesh_rows, width), b16),
        shape((mesh_rows, width), b16),
        shape((members, grid_rows // 2, LANES), b16),
        shape((grid_rows, width), b16),
    ]
    first_part, second_part, blocks, grad_send = pl.pallas_call(
        backward_kernel,
        out_shape=outs,
        in_specs=[SMEM] * 2 + [HBM] * len(ins),
        out_specs=[HBM] * len(outs),
        scratch_shapes=[held(v) for v in ins + outs]
        + [pltpu.VMEM((FOLDS, members, LANES), f32), dma((len(ins) - 1,)), dma, dma((len(outs),))],
        compiler_params=PARAMS,
        cost_estimate=cost_of(1000, 8),
    )(me, over, *ins)
    first_back = to_neighbours(first_part, 0)
    second_back = to_neighbours(second_part, 1)
    landed = lax.all_to_all(blocks, "member", 0, 0, tiled=True)
    (own_part,) = staged(
        own_kernel,
        [shape((mesh_rows, width), f32)],
        [over, back_high, back_low, grad_send],
        scalars_in=(0,),
        cost=(130, 2),
    )
    (grid_share,) = staged(
        member_sum_kernel, [shape((width // members, grid_rows), b16)], [landed], cost=(1, 1)
    )
    grad_latent = own_part + first_back.astype(f32) + second_back.astype(f32)
    return (grad_latent.astype(b16)[None], grid_share.T)


def solution(mesh):
    return jax.shard_map(
        per_device,
        mesh=mesh,
        in_specs=(
            P("member", "grid", None),
            P("grid", None),
            P(),
            P(),
            P(None, "grid"),
            P("grid"),
            P(),
            P("grid", None, None),
            P("grid", None, None),
            P("grid", None),
        ),
        out_specs=(P("member", "grid", None), P("grid", "member")),
        check_vma=False,
    )
```

time: 99.8 us -> 94.6 us (0.948)
  local copies, waits for them, and re-layouts: 23.9 us -> 13 us
  starting transfers between devices: 43.2 us -> 35.2 us
  waiting for transfers between devices: 19 us -> 25.1 us
  Pallas kernels: 12.1 us -> 17.6 us
  other arithmetic: 0 us -> 2.08 us
    unnamed x56 -> x33, local copies, waits for them, and re-layouts: 23.7 us -> 12.9 us
    all_to_all x1, waiting for transfers between devices: 1.06 us -> 11 us  [per_device(): landed = lax.all_to_all(blocks, 'member', 0, 0, tiled=True)]
    ppermute x6 -> x4, starting transfers between devices: 29.6 us -> 21 us  [to_neighbours(): return lax.ppermute(value, ('member', 'grid'), pairs)]
    pallas_call x7 -> x6, Pallas kernels: 12.1 us -> 17.6 us  [the longest x4 6.49 us: staged(): pl.pallas_call(kernel, grid=(1,), out_shape=list(outs), in_specs=[SMEM if...]
    ppermute x6 -> x4, waiting for transfers between devices: 11.8 us -> 6.95 us  [to_neighbours(): return lax.ppermute(value, ('member', 'grid'), pairs)]
    broadcast_in_dim x0 -> x1, other arithmetic: none -> 2.08 us  [per_device(): return (grad_latent.astype(b16)[None], grid_share.T)]
    all_to_all x1, starting transfers between devices: 5 us -> 6.32 us  [per_device(): landed = lax.all_to_all(blocks, 'member', 0, 0, tiled=True)]
    all_to_all x1, waiting for transfers between devices: 6.12 us -> 7.18 us  [per_device(): everyone = lax.all_to_all(shared, 'member', 0, 0, tiled=True)]
  transfers between devices with their start and end apart: 8 -> 6, of which waited for: 5 -> 4; matrix products, arithmetic and copies ran while one was open for 2% -> 1% of each run, Pallas kernels for 5% -> 7%
where the time goes in v3:
time: 94.6 us; the launch traced here: 93.8 us
  starting transfers between devices  35.2 us (37%)
  waiting for transfers between devices  25.1 us (27%)
  Pallas kernels  17.6 us (19%)
  local copies, waits for them, and re-layouts  13 us (14%)
  other arithmetic  2.08 us (2%)
    ppermute x4, starting transfers between devices, to_neighbours(): return lax.ppermute(value, ('member', 'grid'), pairs)  21 us
    unnamed x33, local copies, waits for them, and re-layouts  12.9 us
    all_to_all x1, waiting for transfers between devices, per_device(): landed = lax.all_to_all(blocks, 'member', 0, 0, tiled=True)  11 us
    all_to_all x1, starting transfers between devices, per_device(): everyone = lax.all_to_all(shared, 'member', 0, 0, tiled=True)  7.96 us
    all_to_all x1, waiting for transfers between devices, per_device(): everyone = lax.all_to_all(shared, 'member', 0, 0, tiled=True)  7.18 us
    ppermute x4, waiting for transfers between devices, to_neighbours(): return lax.ppermute(value, ('member', 'grid'), pairs)  6.95 us
    pallas_call x4, Pallas kernels, staged(): pl.pallas_call(kernel, grid=(1,), out_shape=list(outs), in_specs=[SMEM if...  6.49 us
    all_to_all x1, starting transfers between devices, per_device(): landed = lax.all_to_all(blocks, 'member', 0, 0, tiled=True)  6.32 us
  transfers between devices with their start and end apart: 6, of which 4 were waited for; matrix products, arithmetic and copies ran while one was open for 1% of the time, Pallas kernels for 7%

profile of v3, /device:TPU:1, one launch (start us, length us, event | category | flops | bytes accessed | tf_op | source)
XLA Modules:
  0.0 93.8 jit_solution(8759809294008751095)
XLA Ops:
  0.6 4.4 %collective-permute-start.1 = (bf16[256,1024]{1,0:T(8,128)(2,1)}, bf16[256,1024]{1,0:T(8,128)(2,1)S(1)}, u32[]{:S(2)}, u32[]{:S(2)}) collective-permute-start(bf16[256,1024]{1,0:T(8,128)(2,1)} %bitcast.12), channel_id=1, source_target_pairs={{0,31},{1,0},{2,1},{3,2},{4,3},{5,4},{6,5},{7,6},{8,7},{9,8},{10,9... | collective-permute-start | bytes 1572872 | tf_op jit(solution)/shard_map/ppermute | solution.py:31
  5.0 10.5 %collective-permute-start = (bf16[256,1024]{1,0:T(8,128)(2,1)}, bf16[256,1024]{1,0:T(8,128)(2,1)S(1)}, u32[]{:S(2)}, u32[]{:S(2)}) collective-permute-start(bf16[256,1024]{1,0:T(8,128)(2,1)} %bitcast.13), channel_id=1, source_target_pairs={{0,1},{1,2},{2,3},{3,4},{4,5},{5,6},{6,7},{7,8},{8,9},{9,10},{10,1... | collective-permute-start | bytes 1572872 | tf_op jit(solution)/shard_map/ppermute | solution.py:31
  16.3 0.9 copy-done.12
  17.8 2.0 %shard_map.113 = (bf16[256,768]{1,0:T(8,128)(2,1)S(1)}, bf16[256,768]{1,0:T(8,128)(2,1)S(1)}, bf16[256,768]{1,0:T(8,128)(2,1)S(1)}, bf16[256,768]{1,0:T(8,128)(2...) custom-call(s32[1]{0:T(128)} %bitcast.me_ref, s32[1,3]{1,0:T(1,128)S(1)} %copy-done.13, ...), custom_call_target="tpu_custom_call" | custom-call | flops 419430400 | bytes 3145728 | tf_op jit(solution)/shard_map/pallas_call | solution.py:347
  20.4 6.4 %collective-permute-done.first_hbm = bf16[256,1024]{1,0:T(8,128)(2,1)S(1)} collective-permute-done((bf16[256,1024]{1,0:T(8,128)(2,1)}, bf16[256,1024]{1,0:T(8,128)(2,1)S(1)}, u32[]{:S(2)}, u32[]{:S(2)}) %collective-permute-start) | collective-permute-done | bytes 524320 | tf_op jit(solution)/shard_map/ppermute | solution.py:31
  26.8 1.0 %copy-done.5 = bf16[1,256,1024]{2,1,0:T(8,128)(2,1)S(1)} copy-done((bf16[1,256,1024]{2,1,0:T(8,128)(2,1)S(1)}, bf16[1,256,1024]{2,1,0:T(8,128)(2,1)}, u32[]{:S(2)}) %copy-start.5) | copy-done | bytes 524312
  27.8 1.0 %copy-done.6 = bf16[256,1024]{1,0:T(8,128)(2,1)S(1)} copy-done((bf16[256,1024]{1,0:T(8,128)(2,1)S(1)}, bf16[256,1024]{1,0:T(8,128)(2,1)}, u32[]{:S(2)}) %copy-start.6) | copy-done | bytes 524312
  28.9 5.2 %shard_map.114 = (s16[16,208,128]{2,1,0:T(8,128)(2,1)}, f32[256,128]{1,0:T(8,128)S(1)}, f32[256,1024]{1,0:T(8,128)S(1)}, f32[256,1]{1,0:T(8,128)S(1)}, f32[256,1024]{1,0:T(8,128)}) custom-call(s32[1]{0:T(128)} %get-tuple-element.23.over_ref, bf16[256,768]{1,0:T(8,128)(2,1)S(1)} %get-tuple-element.26.high_hbm, bf16[256,1024]{1,0:T(8,128)(2,1)S(1)} %bitcast.14, ...), custom_call_target="tpu_custom_call" | custom-call | flops 1048576000 | bytes 8388608 | tf_op jit(solution)/shard_map/pallas_call | solution.py:401
  34.0 1.0 %copy-done.2 = f32[256,1024]{1,0:T(8,128)} copy-done((f32[256,1024]{1,0:T(8,128)}, f32[256,1024]{1,0:T(8,128)S(1)}, u32[]{:S(2)}) %copy-start.2) | copy-done | bytes 1048600
  35.7 8.0 %all-to-all-start = ((s16[16,208,128]{2,1,0:T(8,128)(2,1)}), s16[16,208,128]{2,1,0:T(8,128)(2,1)S(1)}, u32[]{:S(2)}, u32[]{:S(2)}) async-start(s16[16,208,128]{2,1,0:T(8,128)(2,1)} %get-tuple-element.29), calls=%async_computation | async-start | bytes 1703936 | tf_op jit(solution)/shard_map/all_to_all | solution.py:413
  43.8 0.9 copy-done.8
  44.7 0.9 copy-done.9
  45.6 2.8 %shard_map.115 = (f32[256,1024]{1,0:T(8,128)S(1)}, f32[256,128]{1,0:T(8,128)S(1)}, f32[256,128]{1,0:T(8,128)S(1)}, f32[208,128]{1,0:T(8,128)S(1)}, bf16[1024,1024]{1,0:T(8,128)(2,1)S(1)}) custom-call(f32[256,1024]{1,0:T(8,128)S(1)} %copy-done.1, f32[256,128]{1,0:T(8,128)S(1)} %copy-done.8, f32[100,256]{1,0:T(8,128)S(1)} %copy-done.9, ...), custom_call_target="tpu_custom_call" | custom-call | flops 10485760 | bytes 8388608 | tf_op jit(solution)/shard_map/pallas_call | solution.py:347
  48.4 1.3 %copy-done = bf16[1024,1024]{1,0:T(8,128)(2,1)} copy-done((bf16[1024,1024]{1,0:T(8,128)(2,1)}, bf16[1024,1024]{1,0:T(8,128)(2,1)S(1)}, u32[]{:S(2)}) %copy-start) | copy-done | bytes 2097176
  49.8 1.0 %copy-done.3 = f32[256,1024]{1,0:T(8,128)} copy-done((f32[256,1024]{1,0:T(8,128)}, f32[256,1024]{1,0:T(8,128)S(1)}, u32[]{:S(2)}) %copy-start.3) | copy-done | bytes 1048600
  51.4 7.2 %all-to-all-done.everyone_hbm = s16[16,208,128]{2,1,0:T(8,128)(2,1)S(1)} async-done(((s16[16,208,128]{2,1,0:T(8,128)(2,1)}), s16[16,208,128]{2,1,0:T(8,128)(2,1)S(1)}, u32[]{:S(2)}, u32[]{:S(2)}) %all-to-all-start) | async-done | bytes 852000 | tf_op jit(solution)/shard_map/all_to_all | solution.py:413
  58.5 1.2 %copy-done.4 = f32[256,1024]{1,0:T(8,128)S(1)} copy-done((f32[256,1024]{1,0:T(8,128)S(1)}, f32[256,1024]{1,0:T(8,128)}, u32[]{:S(2)}) %copy-start.4) | copy-done | bytes 1048600
  60.7 5.9 %shard_map.116 = (bf16[256,1024]{1,0:T(8,128)(2,1)}, bf16[256,1024]{1,0:T(8,128)(2,1)}, bf16[16,128,128]{2,1,0:T(8,128)(2,1)}, bf16[256,1024]{1,0:T(8,128)(2,1)S(1)}) custom-call(s32[1]{0:T(128)} %bitcast.me_ref, s32[1]{0:T(128)} %get-tuple-element.23.over_ref, s16[16,208,128]{2,1,0:T(8,128)(2,1)S(1)} %all-to-all-done.everyone_hbm, ...), custom_call_target="tpu_custom_call" | custom-call | flops 1048576000 | bytes 8388608 | tf_op jit(solution)/shard_map/pallas_call | solution.py:443
  66.6 4.1 %collective-permute-start.2 = (bf16[256,1024]{1,0:T(8,128)(2,1)}, bf16[256,1024]{1,0:T(8,128)(2,1)S(1)}, u32[]{:S(2)}, u32[]{:S(2)}) collective-permute-start(bf16[256,1024]{1,0:T(8,128)(2,1)} %get-tuple-element.41), channel_id=1, source_target_pairs={{0,1},{1,2},{2,3},{3,4},{4,5},{5,6},{6,7},{7,8},{8,9},{9,10},{10,1... | collective-permute-start | bytes 1572872 | tf_op jit(solution)/shard_map/ppermute | solution.py:31
  70.8 1.9 %collective-permute-start.3 = (bf16[256,1024]{1,0:T(8,128)(2,1)}, bf16[256,1024]{1,0:T(8,128)(2,1)}, u32[]{:S(2)}, u32[]{:S(2)}) collective-permute-start(bf16[256,1024]{1,0:T(8,128)(2,1)} %get-tuple-element.42), channel_id=1, source_target_pairs={{0,31},{1,0},{2,1},{3,2},{4,3},{5,4},{6,5},{7,6},{8,7},{9,8},{10,9... | collective-permute-start | bytes 1572872 | tf_op jit(solution)/shard_map/ppermute | solution.py:31
  72.7 6.3 %all-to-all-start.1 = ((bf16[16,128,128]{2,1,0:T(8,128)(2,1)}), bf16[16,128,128]{2,1,0:T(8,128)(2,1)S(1)}, u32[]{:S(2)}, u32[]{:S(2)}) async-start(bf16[16,128,128]{2,1,0:T(8,128)(2,1)} %get-tuple-element.43), calls=%async_computation.1 | async-start | bytes 1048576 | tf_op jit(solution)/shard_map/all_to_all | solution.py:455
  79.0 1.0 %shard_map.117 = f32[256,1024]{1,0:T(8,128)S(1)} custom-call(s32[1]{0:T(128)} %get-tuple-element.23.over_ref, bf16[256,768]{1,0:T(8,128)(2,1)S(1)} %get-tuple-element.24.counts_hbm.high_ref, bf16[256,768]{1,0:T(8,128)(2,1)S(1)} %get-tuple-element.25.low_hbm.low_ref, bf16[256,1024]{1,0:T(8,128)(2,1)S(1)} %get-tuple-element.40.send_ref), custom_call_target="tpu_custom_call" | custom-call | flops 136314880 | bytes 2097152 | tf_op jit(solution)/shard_map/pallas_call | solution.py:347
  80.0 11.0 %all-to-all-done.1.landed_ref = bf16[16,128,128]{2,1,0:T(8,128)(2,1)S(1)} async-done(((bf16[16,128,128]{2,1,0:T(8,128)(2,1)}), bf16[16,128,128]{2,1,0:T(8,128)(2,1)S(1)}, u32[]{:S(2)}, u32[]{:S(2)}) %all-to-all-start.1) | async-done | bytes 524320 | tf_op jit(solution)/shard_map/all_to_all | solution.py:455
  91.7 2.1 %fusion = bf16[1,256,1024]{2,1,0:T(8,128)(2,1)} fusion(bf16[256,1024]{1,0:T(8,128)(2,1)} %collective-permute-done.3, f32[256,1024]{1,0:T(8,128)S(1)} %shard_map.117, bf16[256,1024]{1,0:T(8,128)(2,1)S(1)} %collective-permute-done.2), kind=kLoop, calls=%fused_computation.1 | loop fusion | flops 1310720 | bytes 2621440 | tf_op jit(solution)/shard_map/broadcast_in_dim | solution.py:467
  (30 shorter events, 5.0 us)
Async XLA Ops:
  0.6 19.7 %collective-permute-start.1 = (bf16[256,1024]{1,0:T(8,128)(2,1)}, bf16[256,1024]{1,0:T(8,128)(2,1)S(1)}, u32[]{:S(2)}, u32[]{:S(2)}) collective-permute-start(bf16[256,1024]{1,0:T(8,128)(2,1)} %bitcast.12), channel_id=1, source_target_pairs={{0,31},{1,0},{2,1},{3,2},{4,3},{5,4},{6,5},{7,6},{8,7},{9,8},{10,9... | collective-permute-start | bytes 1572872 | tf_op jit(solution)/shard_map/ppermute | solution.py:31
  5.0 21.8 %collective-permute-start = (bf16[256,1024]{1,0:T(8,128)(2,1)}, bf16[256,1024]{1,0:T(8,128)(2,1)S(1)}, u32[]{:S(2)}, u32[]{:S(2)}) collective-permute-start(bf16[256,1024]{1,0:T(8,128)(2,1)} %bitcast.13), channel_id=1, source_target_pairs={{0,1},{1,2},{2,3},{3,4},{4,5},{5,6},{6,7},{7,8},{8,9},{9,10},{10,1... | collective-permute-start | bytes 1572872 | tf_op jit(solution)/shard_map/ppermute | solution.py:31
  16.3 0.9 copy-start.12
  17.2 0.7 copy-start.13
  26.8 1.0 %copy-start.5 = (bf16[1,256,1024]{2,1,0:T(8,128)(2,1)S(1)}, bf16[1,256,1024]{2,1,0:T(8,128)(2,1)}, u32[]{:S(2)}) copy-start(bf16[1,256,1024]{2,1,0:T(8,128)(2,1)} %param.10) | copy-start | bytes 1572868
  27.8 1.0 %copy-start.6 = (bf16[256,1024]{1,0:T(8,128)(2,1)S(1)}, bf16[256,1024]{1,0:T(8,128)(2,1)}, u32[]{:S(2)}) copy-start(bf16[256,1024]{1,0:T(8,128)(2,1)} %grid_hbm.1) | copy-start | bytes 1572868
  28.9 14.8 %copy-start.14 = (f32[256]{0:T(256)S(1)}, f32[256]{0:T(256)}, u32[]{:S(2)}) copy-start(f32[256]{0:T(256)} %param.15) | copy-start | bytes 3076
  28.9 14.9 %copy-start.15 = (f32[100]{0:T(128)S(1)}, f32[100]{0:T(128)}, u32[]{:S(2)}) copy-start(f32[100]{0:T(128)} %param.16) | copy-start | bytes 1204
  34.0 1.0 %copy-start.2 = (f32[256,1024]{1,0:T(8,128)}, f32[256,1024]{1,0:T(8,128)S(1)}, u32[]{:S(2)}) copy-start(f32[256,1024]{1,0:T(8,128)S(1)} %get-tuple-element.38.normed_hbm) | copy-start | bytes 3145732
  35.0 0.7 copy-start.7
  35.7 8.1 %copy-start.1 = (f32[256,1024]{1,0:T(8,128)S(1)}, f32[256,1024]{1,0:T(8,128)}, u32[]{:S(2)}) copy-start(f32[256,1024]{1,0:T(8,128)} %get-tuple-element.30.pre_ref) | copy-start | bytes 3145732
  35.7 22.9 %all-to-all-start = ((s16[16,208,128]{2,1,0:T(8,128)(2,1)}), s16[16,208,128]{2,1,0:T(8,128)(2,1)S(1)}, u32[]{:S(2)}, u32[]{:S(2)}) async-start(s16[16,208,128]{2,1,0:T(8,128)(2,1)} %get-tuple-element.29), calls=%async_computation | async-start | bytes 1703936 | tf_op jit(solution)/shard_map/all_to_all | solution.py:413
  43.8 0.9 copy-start.8
  44.7 0.9 copy-start.9
  48.4 1.3 %copy-start = (bf16[1024,1024]{1,0:T(8,128)(2,1)}, bf16[1024,1024]{1,0:T(8,128)(2,1)S(1)}, u32[]{:S(2)}) copy-start(bf16[1024,1024]{1,0:T(8,128)(2,1)S(1)} %get-tuple-element.37.turned_hbm) | copy-start | bytes 6291460
  49.8 1.0 %copy-start.3 = (f32[256,1024]{1,0:T(8,128)}, f32[256,1024]{1,0:T(8,128)S(1)}, u32[]{:S(2)}) copy-start(f32[256,1024]{1,0:T(8,128)S(1)} %get-tuple-element.36.gate_hbm) | copy-start | bytes 3145732
  50.7 0.6 copy-start.10
  58.5 1.2 %copy-start.4 = (f32[256,1024]{1,0:T(8,128)S(1)}, f32[256,1024]{1,0:T(8,128)}, u32[]{:S(2)}) copy-start(f32[256,1024]{1,0:T(8,128)} %copy-done.3) | copy-start | bytes 3145732
  59.8 0.9 copy-start.11
  66.6 25.1 %collective-permute-start.2 = (bf16[256,1024]{1,0:T(8,128)(2,1)}, bf16[256,1024]{1,0:T(8,128)(2,1)S(1)}, u32[]{:S(2)}, u32[]{:S(2)}) collective-permute-start(bf16[256,1024]{1,0:T(8,128)(2,1)} %get-tuple-element.41), channel_id=1, source_target_pairs={{0,1},{1,2},{2,3},{3,4},{4,5},{5,6},{6,7},{7,8},{8,9},{9,10},{10,1... | collective-permute-start | bytes 1572872 | tf_op jit(solution)/shard_map/ppermute | solution.py:31
  70.8 21.0 %collective-permute-start.3 = (bf16[256,1024]{1,0:T(8,128)(2,1)}, bf16[256,1024]{1,0:T(8,128)(2,1)}, u32[]{:S(2)}, u32[]{:S(2)}) collective-permute-start(bf16[256,1024]{1,0:T(8,128)(2,1)} %get-tuple-element.42), channel_id=1, source_target_pairs={{0,31},{1,0},{2,1},{3,2},{4,3},{5,4},{6,5},{7,6},{8,7},{9,8},{10,9... | collective-permute-start | bytes 1572872 | tf_op jit(solution)/shard_map/ppermute | solution.py:31
  72.7 18.3 %all-to-all-start.1 = ((bf16[16,128,128]{2,1,0:T(8,128)(2,1)}), bf16[16,128,128]{2,1,0:T(8,128)(2,1)S(1)}, u32[]{:S(2)}, u32[]{:S(2)}) async-start(bf16[16,128,128]{2,1,0:T(8,128)(2,1)} %get-tuple-element.43), calls=%async_computation.1 | async-start | bytes 1048576 | tf_op jit(solution)/shard_map/all_to_all | solution.py:455

commit v4 on v3

v4 whole, which is shorter than its diff:
```python
import functools

import jax
import jax.numpy as jnp
from jax import lax
from jax.experimental import pallas as pl
from jax.experimental.pallas import tpu as pltpu
from jax.sharding import PartitionSpec as P

SMOOTH = 0.1
ALPHA = 0.95
EPS = 1e-05
LANES = 128
VARS = 100
MAIN = 208
FOLD = 25
FOLDS = 4
STEPS = 32767.0
CODE = 256.0
LOWEST = -20.0
VMEM_LIMIT = 20 * 1024 * 1024


def to_neighbours(value, side):
    members, shards = lax.axis_size("member"), lax.axis_size("grid")
    pairs = [
        (member * shards + shard, member * shards + (shard + (1 if member % 2 == side else -1)) % shards)
        for member in range(members)
        for shard in range(shards)
    ]
    return lax.ppermute(value, ("member", "grid"), pairs)


def smooth_slope(difference):
    return difference * lax.rsqrt(difference * difference + SMOOTH * SMOOTH)


def turn(values, shift):
    shift = shift % LANES
    return pltpu.roll(values, shift, 1) if shift else values


def lanes_of(values):
    return lax.broadcasted_iota(jnp.int32, values.shape, 1)


def one_hot(picks, rows):
    places = lax.broadcasted_iota(jnp.int32, (rows, picks.shape[1]), 0)
    return jnp.where(places == picks, 1.0, 0.0).astype(jnp.bfloat16)


def count_pairs(row_hot, column_hot):
    return lax.dot_general(
        row_hot, column_hot, (((1,), (1,)), ((), ())), preferred_element_type=jnp.float32
    )


def store_counts(counts, at, high_ref, low_ref):
    high = counts.astype(jnp.bfloat16)
    high_ref[:, at] = high
    low_ref[:, at] = (counts - high.astype(jnp.float32)).astype(jnp.bfloat16)
    return jnp.max(counts)


def edges_kernel(
    me_ref, count_ref, src_ref, dst_ref, out_ref, target_ref, area_ref, var_ref, latent_hbm, grid_hbm, node_hbm,
    over_ref, low_hbm, back_low_hbm,
    high_ref, back_high_ref, base_ref, node_ref, node_turned_ref, pad_ref, turned_ref, target_turned_ref, weight_ref,
    latent_ref, grid_ref, low_ref, back_low_ref, in_sems, out_sems,
):
    loads = start_all((latent_hbm, grid_hbm, node_hbm), (latent_ref, grid_ref, node_ref), in_sems)
    size = high_ref.shape[0]
    slots = src_ref.shape[1]
    slot = lax.broadcasted_iota(jnp.int32, (1, slots), 1)
    odd = lax.rem(me_ref[0], 2)
    most = 0.0
    for place, offset in enumerate((2 - 2 * odd, 1, 2 * odd)):
        live = slot < count_ref[0, offset]
        targets = one_hot(jnp.where(live, dst_ref[pl.ds(offset, 1), :], -1), size)
        sources = one_hot(src_ref[pl.ds(offset, 1), :], size)
        counts = count_pairs(targets, sources)
        most = jnp.maximum(
            most, store_counts(counts, slice(place * size, (place + 1) * size), high_ref, low_ref)
        )
        back = 2 - place
        store_counts(
            count_pairs(sources, targets), slice(back * size, (back + 1) * size), back_high_ref, back_low_ref
        )
    over_ref[0] = (most > 256.0).astype(jnp.int32)
    stores = start_all((low_ref, back_low_ref), (low_hbm, back_low_hbm), out_sems)
    variables, width = out_ref.shape
    padded = jnp.concatenate(
        [out_ref[...].astype(jnp.float32), jnp.zeros((LANES - variables, width), jnp.float32)], axis=0
    )
    pad_ref[...] = padded.astype(jnp.bfloat16)
    turned_ref[...] = padded.T.astype(jnp.bfloat16)
    target = jnp.concatenate(
        [target_ref[...], jnp.zeros((LANES - variables, target_ref.shape[1]), jnp.float32)], axis=0
    )
    target_turned_ref[...] = target.T
    weight_ref[...] = area_ref[...] * var_ref[...]
    for load in loads:
        load.wait()
    node_turned_ref[...] = node_ref[...].T
    own = slice(size, 2 * size)
    base_ref[...] = dot(high_ref[:, own], latent_ref[...]) + grid_ref[...].astype(jnp.float32)

    @pl.when(over_ref[0] > 0)
    def _():
        base_ref[...] += dot(low_ref[:, own], latent_ref[...])

    for store in stores:
        store.wait()


def start_all(sources, targets, sems):
    copies = [pltpu.make_async_copy(s, t, sems.at[i]) for i, (s, t) in enumerate(zip(sources, targets))]
    for copy in copies:
        copy.start()
    return copies


def dot(left, right):
    return jnp.dot(left, right, preferred_element_type=jnp.float32)


def forward_kernel(
    over_ref, high_ref, base_ref, first_ref, second_ref, node_ref, turned_ref, target_ref, weight_ref, low_hbm,
    shared_ref, fold_ref, lead_ref, gate_ref, normed_ref, inverse_ref,
    low_ref, sum_ref, low_sem,
):
    size = first_ref.shape[0]

    def gather(counts_ref):
        return dot(counts_ref[:, :size], first_ref[...]) + dot(counts_ref[:, 2 * size :], second_ref[...])

    sum_ref[...] = gather(high_ref) + base_ref[...]

    @pl.when(over_ref[0] > 0)
    def _():
        copy = pltpu.make_async_copy(low_hbm, low_ref, low_sem)
        copy.start()
        copy.wait()
        sum_ref[...] += gather(low_ref)

    summed = sum_ref[...]
    centered = summed - jnp.mean(summed, axis=-1, keepdims=True)
    inverse = lax.rsqrt(jnp.mean(centered * centered, axis=-1, keepdims=True) + EPS)
    normed = centered * inverse
    normed_ref[...] = normed
    inverse_ref[...] = inverse
    pre_act = dot(normed.astype(jnp.bfloat16), node_ref[...])
    gate_sig = 0.5 + 0.5 * jnp.tanh(0.5 * pre_act)
    gate_ref[...] = gate_sig * (1.0 + pre_act * (1.0 - gate_sig))
    hidden = (pre_act * gate_sig).astype(jnp.bfloat16)
    pred = dot(hidden, turned_ref[...])
    largest = jnp.max(jnp.abs(pred), axis=0, keepdims=True)
    code = jnp.ceil(jnp.log2(jnp.maximum(largest, 2.0**LOWEST)) * CODE)
    whole = jnp.round(pred * (jnp.exp2(code * (-1.0 / CODE)) * STEPS))
    packed = fold(whole, code).astype(jnp.int16)
    for member in range(shared_ref.shape[0]):
        shared_ref[member] = packed
    lead_ref[...] = weight_ref[...] * smooth_slope(pred - target_ref[...])
    fold_ref[...] = fold(pred)


def fold(values, code=None):
    rest = values[MAIN:, :]
    tail = jnp.zeros((MAIN - FOLDS * rest.shape[0], LANES), values.dtype)
    if code is not None:
        wide = jnp.broadcast_to(code, tail.shape)
        row = lax.broadcasted_iota(jnp.int32, tail.shape, 0)
        for k in range(FOLDS):
            tail = jnp.where(row == k, turn(wide, VARS - FOLD * k), tail)
    pieces = [turn(rest, VARS - FOLD * k) for k in range(FOLDS)] + [tail]
    spare = jnp.concatenate(pieces, axis=0)
    main = values[:MAIN, :]
    lane = lanes_of(main)
    return jnp.where(lane < VARS, main, jnp.where(lane < VARS + FOLD, spare, jnp.zeros_like(main)))


def unfold(values, rows):
    rest_rows = rows - MAIN
    lane = lax.broadcasted_iota(jnp.int32, (rest_rows, LANES), 1)
    rest = jnp.zeros((rest_rows, LANES), values.dtype)
    for k in range(FOLDS):
        piece = turn(values[k * rest_rows : (k + 1) * rest_rows, :], FOLD * k - VARS)
        rest = jnp.where((lane >= FOLD * k) & (lane < FOLD * (k + 1)), piece, rest)
    return jnp.concatenate([values, rest], axis=0)


def backward_kernel(
    me_ref, over_ref, everyone_ref, fold_ref, lead_ref, weight_ref, gate_ref,
    pad_ref, turned_ref, normed_ref, inverse_ref, high_ref, low_hbm,
    blocks_ref, first_ref, second_ref, send_ref,
    low_ref, scale_ref, low_sem, *, pair_scale
):
    members = everyone_ref.shape[0]
    grid_rows, width = normed_ref.shape
    rest_rows = grid_rows - MAIN
    me = me_ref[0]
    first = FOLDS * rest_rows
    lane = lax.broadcasted_iota(jnp.int32, (members, LANES), 1)
    tails = everyone_ref[:, first:MAIN, :].astype(jnp.float32)
    code = jnp.zeros((members, LANES), jnp.float32)
    for k in range(FOLDS):
        piece = turn(tails[:, k, :], FOLD * k - VARS)
        code = jnp.where((lane >= FOLD * k) & (lane < FOLD * (k + 1)), piece, code)
    scale = jnp.exp2(code * (1.0 / CODE)) * (1.0 / STEPS)
    for k in range(FOLDS):
        scale_ref[k] = jnp.where(lane < VARS, scale, turn(scale, VARS - FOLD * k))

    bounds = [(k * rest_rows, (k + 1) * rest_rows) for k in range(FOLDS)] + [(first, MAIN)]
    parts = [jnp.zeros((high - low, LANES), jnp.float32) for low, high in bounds]
    for step in range(1, members):
        other = lax.rem(me + step, members)
        for i, (low, high) in enumerate(bounds):
            factor = scale_ref[min(i, FOLDS - 1), pl.ds(other, 1), :]
            theirs = everyone_ref[other, low:high, :].astype(jnp.float32) * factor
            parts[i] = parts[i] + smooth_slope(fold_ref[low:high, :] - theirs)
    pair_sum = unfold(jnp.concatenate(parts, axis=0), grid_rows)
    real = lanes_of(pair_sum) < VARS
    grad_pred = lead_ref[...] - pair_scale * weight_ref[...] * jnp.where(real, pair_sum, 0.0)
    grad_hidden = dot(grad_pred.astype(jnp.bfloat16), pad_ref[...])
    grad_pre = (grad_hidden * gate_ref[...]).astype(jnp.bfloat16)
    grad_normed = dot(grad_pre, turned_ref[...])
    normed = normed_ref[...]
    grad_summed = inverse_ref[...] * (
        grad_normed
        - jnp.mean(grad_normed, axis=-1, keepdims=True)
        - normed * jnp.mean(grad_normed * normed, axis=-1, keepdims=True)
    )
    send_ref[...] = grad_summed.astype(jnp.bfloat16)
    half = grid_rows // 2
    lower = lax.broadcasted_iota(jnp.int32, (half, LANES), 1) < LANES // 2
    for pair in range(width // LANES):
        at = slice(pair * LANES, (pair + 1) * LANES)
        top = grad_summed[:half, at]
        bottom = grad_summed[half:, at]
        blocks_ref[2 * pair] = jnp.where(lower, top, turn(bottom, LANES // 2)).astype(jnp.bfloat16)
        blocks_ref[2 * pair + 1] = jnp.where(lower, turn(top, LANES // 2), bottom).astype(jnp.bfloat16)
    places = ((first_ref, slice(0, grid_rows)), (second_ref, slice(2 * grid_rows, 3 * grid_rows)))
    for ref, at in places:
        ref[...] = dot(high_ref[:, at], send_ref[...]).astype(jnp.bfloat16)

    @pl.when(over_ref[0] > 0)
    def _():
        copy = pltpu.make_async_copy(low_hbm, low_ref, low_sem)
        copy.start()
        copy.wait()
        for ref, at in places:
            total = dot(high_ref[:, at], send_ref[...]) + dot(low_ref[:, at], send_ref[...])
            ref[...] = total.astype(jnp.bfloat16)


def tail_kernel(
    over_ref, high_ref, send_ref, first_ref, second_ref, landed_ref, low_hbm, out_hbm, share_ref,
    low_ref, sum_ref, out_ref, low_sem, out_sems
):
    rows = send_ref.shape[0]
    own = slice(rows, 2 * rows)
    sum_ref[...] = dot(high_ref[:, own], send_ref[...])

    @pl.when(over_ref[0] > 0)
    def _():
        copy = pltpu.make_async_copy(low_hbm, low_ref, low_sem)
        copy.start()
        copy.wait()
        sum_ref[...] += dot(low_ref[:, own], send_ref[...])

    parts = out_sems.shape[0]
    stores = []
    for part in range(parts):
        at = slice(part * rows // parts, (part + 1) * rows // parts)
        total = sum_ref[at, :] + first_ref[at, :].astype(jnp.float32) + second_ref[at, :].astype(jnp.float32)
        out_ref[at, :] = total.astype(jnp.bfloat16)
        stores.append(pltpu.make_async_copy(out_ref.at[at, :], out_hbm.at[at, :], out_sems.at[part]))
        stores[-1].start()
    total = landed_ref[0].astype(jnp.float32)
    for member in range(1, landed_ref.shape[0]):
        total = total + landed_ref[member].astype(jnp.float32)
    half = total.shape[0]
    share = share_ref.shape[0]
    flipped = total.T
    share_ref[:, :half] = flipped[:share, :].astype(jnp.bfloat16)
    share_ref[:, half:] = flipped[share:, :].astype(jnp.bfloat16)
    for store in stores:
        store.wait()


def shape(dims, dtype):
    return jax.ShapeDtypeStruct(dims, dtype)


SMEM = pl.BlockSpec(memory_space=pltpu.SMEM)
VMEM = pl.BlockSpec(memory_space=pltpu.VMEM)
HBM = pl.BlockSpec(memory_space=pltpu.HBM)


def in_hbm(*values):
    return [pltpu.with_memory_space_constraint(v, pltpu.HBM) for v in values]


def cost_of(mega_flops, mega_bytes):
    return pl.CostEstimate(
        flops=mega_flops << 20, bytes_accessed=mega_bytes << 20, transcendentals=0
    )


PARAMS = pltpu.CompilerParams(vmem_limit_bytes=VMEM_LIMIT)


def held(value):
    return pltpu.VMEM(value.shape, value.dtype)


def per_device(
    mesh_latent, grid_latent, node_weight, out_weight, target, area_weight, var_weight, edge_src, edge_dst, edge_count
):
    f32, b16, i32 = jnp.float32, jnp.bfloat16, jnp.int32
    members = lax.axis_size("member")
    me = lax.axis_index("member").astype(i32)[None]
    latent = mesh_latent[0]
    mesh_rows = latent.shape[0]
    grid_rows, width = grid_latent.shape
    variables = out_weight.shape[0]
    dma = pltpu.SemaphoreType.DMA

    first = to_neighbours(latent, 0)
    second = to_neighbours(latent, 1)
    outs = [
        shape((1,), i32),
        pltpu.HBM((grid_rows, 3 * mesh_rows), b16),
        pltpu.HBM((mesh_rows, 3 * grid_rows), b16),
        pltpu.VMEM((grid_rows, 3 * mesh_rows), b16),
        pltpu.VMEM((mesh_rows, 3 * grid_rows), b16),
        pltpu.VMEM((grid_rows, width), f32),
        pltpu.VMEM((width, width), b16),
        pltpu.VMEM((width, width), b16),
        pltpu.VMEM((LANES, width), b16),
        pltpu.VMEM((width, LANES), b16),
        pltpu.VMEM((grid_rows, LANES), f32),
        pltpu.VMEM((grid_rows, LANES), f32),
    ]
    (
        over, low, back_low, high, back_high, base, node, node_turned, out_pad, out_turned, target_turned, weight
    ) = pl.pallas_call(
        edges_kernel,
        out_shape=outs,
        in_specs=[SMEM] * 2 + [VMEM] * 6 + [HBM] * 3,
        out_specs=[SMEM] + [HBM] * 2 + [VMEM] * 9,
        scratch_shapes=[held(v) for v in (latent, grid_latent, *outs[1:3])] + [dma((3,)), dma((2,))],
        compiler_params=PARAMS,
        cost_estimate=cost_of(500, 8),
    )(
        me,
        edge_count,
        edge_src[0],
        edge_dst[0],
        out_weight,
        target,
        area_weight[:, None],
        jnp.pad(var_weight, (0, LANES - variables))[None, :],
        *in_hbm(latent, grid_latent, node_weight),
    )

    outs = [
        pltpu.VMEM((members, MAIN, LANES), jnp.int16),
        pltpu.VMEM((MAIN, LANES), f32),
        pltpu.VMEM((grid_rows, LANES), f32),
        pltpu.VMEM((grid_rows, width), f32),
        pltpu.VMEM((grid_rows, width), f32),
        pltpu.VMEM((grid_rows, 1), f32),
    ]
    shared, folded, lead, gate, normed, inverse = pl.pallas_call(
        forward_kernel,
        out_shape=outs,
        in_specs=[SMEM] + [VMEM] * 8 + [HBM],
        out_specs=[VMEM] * len(outs),
        scratch_shapes=[held(low), pltpu.VMEM((grid_rows, width), f32), dma],
        compiler_params=PARAMS,
        cost_estimate=cost_of(1000, 8),
    )(over, high, base, first, second, node, out_turned, target_turned, weight, *in_hbm(low))
    everyone = lax.all_to_all(shared, "member", 0, 0, tiled=True)

    pair_scale = (1.0 - (1.0 - ALPHA) / members) / (members - 1)
    outs = [
        pltpu.VMEM((members, grid_rows // 2, LANES), b16),
        pltpu.VMEM((mesh_rows, width), b16),
        pltpu.VMEM((mesh_rows, width), b16),
        pltpu.VMEM((grid_rows, width), b16),
    ]
    blocks, first_part, second_part, grad_send = pl.pallas_call(
        functools.partial(backward_kernel, pair_scale=pair_scale),
        out_shape=outs,
        in_specs=[SMEM] * 2 + [VMEM] * 10 + [HBM],
        out_specs=[VMEM] * 4,
        scratch_shapes=[held(back_low), pltpu.VMEM((FOLDS, members, LANES), f32), dma],
        compiler_params=PARAMS,
        cost_estimate=cost_of(1000, 8),
    )(
        me, over, everyone, folded, lead, weight, gate, out_pad, node_turned, normed, inverse, back_high,
        *in_hbm(back_low),
    )
    landed = lax.all_to_all(blocks, "member", 0, 0, tiled=True)
    first_back = to_neighbours(first_part, 0)
    second_back = to_neighbours(second_part, 1)
    grad_latent, grid_share = pl.pallas_call(
        tail_kernel,
        out_shape=[pltpu.HBM((mesh_rows, width), b16), shape((width // members, grid_rows), b16)],
        in_specs=[SMEM] + [VMEM] * 5 + [HBM],
        out_specs=[HBM, VMEM],
        scratch_shapes=[
            held(back_low),
            pltpu.VMEM((mesh_rows, width), f32),
            pltpu.VMEM((mesh_rows, width), b16),
            dma,
            dma((4,)),
        ],
        compiler_params=PARAMS,
        cost_estimate=cost_of(130, 3),
    )(over, back_high, grad_send, first_back, second_back, landed, *in_hbm(back_low))
    return (grad_latent[None], grid_share.T)


def solution(mesh):
    return jax.shard_map(
        per_device,
        mesh=mesh,
        in_specs=(
            P("member", "grid", None),
            P("grid", None),
            P(),
            P(),
            P(None, "grid"),
            P("grid"),
            P(),
            P("grid", None, None),
            P("grid", None, None),
            P("grid", None),
        ),
        out_specs=(P("member", "grid", None), P("grid", "member")),
        check_vma=False,
    )
```

time: 94.6 us -> 81.7 us (0.86)
  blocking collectives: 0 us -> 40.6 us
  waiting for transfers between devices: 25.1 us -> 1.7 us
  starting transfers between devices: 35.2 us -> 21 us
  local copies, waits for them, and re-layouts: 13 us -> 4.66 us
  Pallas kernels: 17.6 us -> 12.6 us
  other arithmetic: 2.08 us -> 0 us
    all_to_all x0 -> x2, blocking collectives: none -> 40.6 us  [the longest x1 22.8 us: per_device(): everyone = lax.all_to_all(shared, 'member', 0, 0, tiled=True)]
    all_to_all x2 -> x0, waiting for transfers between devices: 18.2 us -> none  [the longest x1 11 us: per_device(): landed = lax.all_to_all(blocks, 'member', 0, 0, tiled=True)]
    all_to_all x2 -> x0, starting transfers between devices: 14.3 us -> none  [the longest x1 7.96 us: per_device(): everyone = lax.all_to_all(shared, 'member', 0, 0, tiled=True)]
    unnamed x33 -> x7, local copies, waits for them, and re-layouts: 12.9 us -> 3.19 us
    ppermute x4, waiting for transfers between devices: 6.95 us -> 1.7 us  [to_neighbours(): return lax.ppermute(value, ('member', 'grid'), pairs)]
    pallas_call x6 -> x4, Pallas kernels: 17.6 us -> 12.6 us  [the longest x1 4.85 us: per_device(): pl.pallas_call(edges_kernel, out_shape=outs, in_specs=[SMEM] * 2 + [VMEM]...]
    broadcast_in_dim x1 -> x0, other arithmetic: 2.08 us -> none  [per_device(): return (grad_latent.astype(b16)[None], grid_share.T)]
  transfers between devices with their start and end apart: 6 -> 4, of which waited for: 4 -> 1; matrix products, arithmetic and copies ran while one was open for 1% -> 3% of each run, Pallas kernels for 7% -> 6%
where the time goes in v4:
time: 81.7 us; the launch traced here: 81.3 us
  blocking collectives  40.6 us (50%)
  starting transfers between devices  21 us (26%)
  Pallas kernels  12.6 us (15%)
  local copies, waits for them, and re-layouts  4.66 us (6%)
  waiting for transfers between devices  1.7 us (2%)
    all_to_all x1, blocking collectives, per_device(): everyone = lax.all_to_all(shared, 'member', 0, 0, tiled=True)  22.8 us
    ppermute x4, starting transfers between devices, to_neighbours(): return lax.ppermute(value, ('member', 'grid'), pairs)  21 us
    all_to_all x1, blocking collectives, per_device(): landed = lax.all_to_all(blocks, 'member', 0, 0, tiled=True)  17.8 us
    pallas_call x1, Pallas kernels, per_device(): pl.pallas_call(edges_kernel, out_shape=outs, in_specs=[SMEM] * 2 + [VMEM]...  4.85 us
    unnamed x7, local copies, waits for them, and re-layouts  3.19 us
    pallas_call x1, Pallas kernels, per_device(): pl.pallas_call(functools.partial(backward_kernel, pair_scale=pair_scale),...  2.75 us
    pallas_call x1, Pallas kernels, per_device(): pl.pallas_call(forward_kernel, out_shape=outs, in_specs=[SMEM] + [VMEM] *...  2.58 us
    pallas_call x1, Pallas kernels, per_device(): pl.pallas_call(tail_kernel, out_shape=[pltpu.HBM((mesh_rows, width), b16)...  2.46 us
  transfers between devices with their start and end apart: 4, of which 1 were waited for; matrix products, arithmetic and copies ran while one was open for 3% of the time, Pallas kernels for 6%

profile of v4, /device:TPU:1, one launch (start us, length us, event | category | flops | bytes accessed | tf_op | source)
XLA Modules:
  0.0 81.3 jit_solution(3086960002357845454)
XLA Ops:
  0.6 4.4 %collective-permute-start.1 = (bf16[256,1024]{1,0:T(8,128)(2,1)}, bf16[256,1024]{1,0:T(8,128)(2,1)S(1)}, u32[]{:S(2)}, u32[]{:S(2)}) collective-permute-start(bf16[256,1024]{1,0:T(8,128)(2,1)} %bitcast.11), channel_id=1, source_target_pairs={{0,31},{1,0},{2,1},{3,2},{4,3},{5,4},{6,5},{7,6},{8,7},{9,8},{10,9... | collective-permute-start | bytes 1572872 | tf_op jit(solution)/shard_map/ppermute | solution.py:31
  5.0 10.5 %collective-permute-start = (bf16[256,1024]{1,0:T(8,128)(2,1)}, bf16[256,1024]{1,0:T(8,128)(2,1)S(1)}, u32[]{:S(2)}, u32[]{:S(2)}) collective-permute-start(bf16[256,1024]{1,0:T(8,128)(2,1)} %bitcast.12), channel_id=1, source_target_pairs={{0,1},{1,2},{2,3},{3,4},{4,5},{5,6},{6,7},{7,8},{8,9},{9,10},{10,1... | collective-permute-start | bytes 1572872 | tf_op jit(solution)/shard_map/ppermute | solution.py:31
  15.5 0.8 copy.12.area_ref
  16.4 0.7 pad_bitcast_fusion.var_ref
  17.0 0.7 copy_bitcast_fusion
  17.7 0.0 copy-start
  17.7 0.9 %copy-done = bf16[100,1024]{1,0:T(8,128)(2,1)S(1)} copy-done((bf16[100,1024]{1,0:T(8,128)(2,1)S(1)}, bf16[100,1024]{1,0:T(8,128)(2,1)}, u32[]{:S(2)}) %copy-start) | copy-done | bytes 204824
  18.7 0.0 copy-start.1
  18.7 0.9 %copy-done.1 = f32[100,256]{1,0:T(8,128)S(1)} copy-done((f32[100,256]{1,0:T(8,128)S(1)}, f32[100,256]{1,0:T(8,128)}, u32[]{:S(2)}) %copy-start.1) | copy-done | bytes 102424
  19.6 0.0 copy-start.2
  19.6 0.7 copy-done.2
  20.2 4.8 %shard_map.113 = (s32[1]{0:T(128)}, bf16[256,768]{1,0:T(8,128)(2,1)}, bf16[256,768]{1,0:T(8,128)(2,1)}, bf16[256,768]{1,0:T(8,128)(2,1)S(1)}, bf16[256,768]{1,0:...) custom-call(s32[1]{0:T(128)} %bitcast.me_ref, ...), custom_call_target="tpu_custom_call" | custom-call | flops 524288000 | bytes 8388608 | tf_op jit(solution)/shard_map/pallas_call | solution.py:347
  25.1 0.0 collective-permute-done.1.second_ref
  25.1 1.7 %collective-permute-done.first_ref = bf16[256,1024]{1,0:T(8,128)(2,1)S(1)} collective-permute-done((bf16[256,1024]{1,0:T(8,128)(2,1)}, bf16[256,1024]{1,0:T(8,128)(2,1)S(1)}, u32[]{:S(2)}, u32[]{:S(2)}) %collective-permute-start) | collective-permute-done | bytes 524320 | tf_op jit(solution)/shard_map/ppermute | solution.py:31
  26.8 2.6 %shard_map.114 = (s16[16,208,128]{2,1,0:T(8,128)(2,1)S(1)}, f32[208,128]{1,0:T(8,128)S(1)}, f32[256,128]{1,0:T(8,128)S(1)}, f32[256,1024]{1,0:T(8,128)S(1)}, f32...) custom-call(s32[1]{0:T(128)} %get-tuple-element.26.over_ref, bf16[256,768]{1,0:T(8,128)(2,1)S(1)} %get-tuple-element.28.high_ref, ...), custom_call_target="tpu_custom_call" | custom-call | flops 1048576000 | bytes 8388608 | tf_op jit(solution)/shard_map/pallas_call | solution.py:375
  29.4 22.8 %all_to_all.10.everyone_ref = s16[16,208,128]{2,1,0:T(8,128)(2,1)S(1)} all-to-all(s16[16,208,128]{2,1,0:T(8,128)(2,1)S(1)} %get-tuple-element.35), channel_id=1, replica_groups=mesh['member'=16,'grid'=32] {'member'}, dimensions={0} | all-to-all | bytes 1703936 | tf_op jit(solution)/shard_map/all_to_all | solution.py:384
  52.1 2.8 %shard_map.115 = (bf16[16,128,128]{2,1,0:T(8,128)(2,1)S(1)}, bf16[256,1024]{1,0:T(8,128)(2,1)S(1)}, bf16[256,1024]{1,0:T(8,128)(2,1)S(1)}, bf16[256,1024]{1,0:T(8,128)(2,1)S(1)}) custom-call(s32[1]{0:T(128)} %bitcast.me_ref, s32[1]{0:T(128)} %get-tuple-element.26.over_ref, s16[16,208,128]{2,1,0:T(8,128)(2,1)S(1)} %all_to_all.10.everyone_ref, ...), custom_call_target="tpu_custom_call" | custom-call | flops 1048576000 | bytes 8388608 | tf_op jit(solution)/shard_map/pallas_call | solution.py:393
  54.9 4.1 %collective-permute-start.2 = (bf16[256,1024]{1,0:T(8,128)(2,1)S(1)}, bf16[256,1024]{1,0:T(8,128)(2,1)S(1)}, u32[]{:S(2)}, u32[]{:S(2)}) collective-permute-start(bf16[256,1024]{1,0:T(8,128)(2,1)S(1)} %get-tuple-element.45), channel_id=1, source_target_pairs={{0,1},{1,2},{2,3},{3,4},{4,5},{5,6},{6,7},{7,8},{8,9},{9,10},{10,1... | collective-permute-start | bytes 1572872 | tf_op jit(solution)/shard_map/ppermute | solution.py:31
  59.0 1.9 %collective-permute-start.3 = (bf16[256,1024]{1,0:T(8,128)(2,1)S(1)}, bf16[256,1024]{1,0:T(8,128)(2,1)S(1)}, u32[]{:S(2)}, u32[]{:S(2)}) collective-permute-start(bf16[256,1024]{1,0:T(8,128)(2,1)S(1)} %get-tuple-element.46), channel_id=1, source_target_pairs={{0,31},{1,0},{2,1},{3,2},{4,3},{5,4},{6,5},{7,6},{8,7},{9,8},{10,9... | collective-permute-start | bytes 1572872 | tf_op jit(solution)/shard_map/ppermute | solution.py:31
  61.0 17.8 %all_to_all.11.landed_ref = bf16[16,128,128]{2,1,0:T(8,128)(2,1)S(1)} all-to-all(bf16[16,128,128]{2,1,0:T(8,128)(2,1)S(1)} %get-tuple-element.47), channel_id=1, replica_groups=mesh['member'=16,'grid'=32] {'member'}, dimensions={0} | all-to-all | bytes 1048576 | tf_op jit(solution)/shard_map/all_to_all | solution.py:405
  78.8 0.0 collective-permute-done.2.first_ref
  78.8 0.0 collective-permute-done.3.second_ref
  78.8 2.5 %shard_map.116 = (bf16[256,1024]{1,0:T(8,128)(2,1)}, bf16[64,256]{1,0:T(8,128)(2,1)}) custom-call(s32[1]{0:T(128)} %get-tuple-element.26.over_ref, bf16[256,768]{1,0:T(8,128)(2,1)S(1)} %get-tuple-element.27.high_ref, bf16[256,1024]{1,0:T(8,128)(2,1)S(1)} %get-tuple-element.44.send_ref, bf16[256,1024]{1,0:T(8,128)(2,1)S(1)} %collective-permute-done.2.first_ref, ...), custom_call_target="tpu_custom_call" | custom-call | flops 136314880 | bytes 3145728 | tf_op jit(solution)/shard_map/pallas_call | solution.py:408
Async XLA Ops:
  0.6 24.4 %collective-permute-start.1 = (bf16[256,1024]{1,0:T(8,128)(2,1)}, bf16[256,1024]{1,0:T(8,128)(2,1)S(1)}, u32[]{:S(2)}, u32[]{:S(2)}) collective-permute-start(bf16[256,1024]{1,0:T(8,128)(2,1)} %bitcast.11), channel_id=1, source_target_pairs={{0,31},{1,0},{2,1},{3,2},{4,3},{5,4},{6,5},{7,6},{8,7},{9,8},{10,9... | collective-permute-start | bytes 1572872 | tf_op jit(solution)/shard_map/ppermute | solution.py:31
  5.0 21.8 %collective-permute-start = (bf16[256,1024]{1,0:T(8,128)(2,1)}, bf16[256,1024]{1,0:T(8,128)(2,1)S(1)}, u32[]{:S(2)}, u32[]{:S(2)}) collective-permute-start(bf16[256,1024]{1,0:T(8,128)(2,1)} %bitcast.12), channel_id=1, source_target_pairs={{0,1},{1,2},{2,3},{3,4},{4,5},{5,6},{6,7},{7,8},{8,9},{9,10},{10,1... | collective-permute-start | bytes 1572872 | tf_op jit(solution)/shard_map/ppermute | solution.py:31
  17.7 0.9 %copy-start = (bf16[100,1024]{1,0:T(8,128)(2,1)S(1)}, bf16[100,1024]{1,0:T(8,128)(2,1)}, u32[]{:S(2)}) copy-start(bf16[100,1024]{1,0:T(8,128)(2,1)} %out_ref.1) | copy-start | bytes 614404
  18.7 0.9 %copy-start.1 = (f32[100,256]{1,0:T(8,128)S(1)}, f32[100,256]{1,0:T(8,128)}, u32[]{:S(2)}) copy-start(f32[100,256]{1,0:T(8,128)} %target_ref.1) | copy-start | bytes 307204
  19.6 0.7 copy-start.2
  54.9 23.9 %collective-permute-start.2 = (bf16[256,1024]{1,0:T(8,128)(2,1)S(1)}, bf16[256,1024]{1,0:T(8,128)(2,1)S(1)}, u32[]{:S(2)}, u32[]{:S(2)}) collective-permute-start(bf16[256,1024]{1,0:T(8,128)(2,1)S(1)} %get-tuple-element.45), channel_id=1, source_target_pairs={{0,1},{1,2},{2,3},{3,4},{4,5},{5,6},{6,7},{7,8},{8,9},{9,10},{10,1... | collective-permute-start | bytes 1572872 | tf_op jit(solution)/shard_map/ppermute | solution.py:31
  59.0 19.8 %collective-permute-start.3 = (bf16[256,1024]{1,0:T(8,128)(2,1)S(1)}, bf16[256,1024]{1,0:T(8,128)(2,1)S(1)}, u32[]{:S(2)}, u32[]{:S(2)}) collective-permute-start(bf16[256,1024]{1,0:T(8,128)(2,1)S(1)} %get-tuple-element.46), channel_id=1, source_target_pairs={{0,31},{1,0},{2,1},{3,2},{4,3},{5,4},{6,5},{7,6},{8,7},{9,8},{10,9... | collective-permute-start | bytes 1572872 | tf_op jit(solution)/shard_map/ppermute | solution.py:31

commit v5 on v4

--- a/solution.py
+++ b/solution.py
@@ -63,21 +63,29 @@
 
 
 def edges_kernel(
-    me_ref, count_ref, src_ref, dst_ref, out_ref, target_ref, area_ref, var_ref, latent_hbm, grid_hbm, node_hbm,
-    over_ref, low_hbm, back_low_hbm,
+    me_hbm, count_hbm, src_hbm, dst_hbm, area_hbm, var_hbm, out_hbm, target_hbm, node_hbm, latent_hbm, grid_hbm,
+    flags_ref, low_hbm, back_low_hbm,
     high_ref, back_high_ref, base_ref, node_ref, node_turned_ref, pad_ref, turned_ref, target_turned_ref, weight_ref,
-    latent_ref, grid_ref, low_ref, back_low_ref, in_sems, out_sems,
+    me_ref, count_ref, src_ref, dst_ref, area_ref, var_ref, out_ref, target_ref, latent_ref, grid_ref,
+    low_ref, back_low_ref, in_sems, out_sems,
 ):
-    loads = start_all((latent_hbm, grid_hbm, node_hbm), (latent_ref, grid_ref, node_ref), in_sems)
+    loads = start_all(
+        (me_hbm, count_hbm, src_hbm, dst_hbm, area_hbm, var_hbm, out_hbm, target_hbm, node_hbm, latent_hbm, grid_hbm),
+        (me_ref, count_ref, src_ref, dst_ref, area_ref, var_ref, out_ref, target_ref, node_ref, latent_ref, grid_ref),
+        in_sems,
+    )
     size = high_ref.shape[0]
-    slots = src_ref.shape[1]
+    slots = src_ref.shape[1] // 3
     slot = lax.broadcasted_iota(jnp.int32, (1, slots), 1)
+    for load in loads[:4]:
+        load.wait()
     odd = lax.rem(me_ref[0], 2)
     most = 0.0
     for place, offset in enumerate((2 - 2 * odd, 1, 2 * odd)):
+        at = pl.ds(pl.multiple_of(offset * slots, LANES), slots)
         live = slot < count_ref[0, offset]
-        targets = one_hot(jnp.where(live, dst_ref[pl.ds(offset, 1), :], -1), size)
-        sources = one_hot(src_ref[pl.ds(offset, 1), :], size)
+        targets = one_hot(jnp.where(live, dst_ref[:, at], -1), size)
+        sources = one_hot(src_ref[:, at], size)
         counts = count_pairs(targets, sources)
         most = jnp.maximum(
             most, store_counts(counts, slice(place * size, (place + 1) * size), high_ref, low_ref)
@@ -86,8 +94,11 @@
         store_counts(
             count_pairs(sources, targets), slice(back * size, (back + 1) * size), back_high_ref, back_low_ref
         )
-    over_ref[0] = (most > 256.0).astype(jnp.int32)
+    flags_ref[0] = (most > 256.0).astype(jnp.int32)
+    flags_ref[1] = me_ref[0]
     stores = start_all((low_ref, back_low_ref), (low_hbm, back_low_hbm), out_sems)
+    for load in loads[4:8]:
+        load.wait()
     variables, width = out_ref.shape
     padded = jnp.concatenate(
         [out_ref[...].astype(jnp.float32), jnp.zeros((LANES - variables, width), jnp.float32)], axis=0
@@ -98,14 +109,16 @@
         [target_ref[...], jnp.zeros((LANES - variables, target_ref.shape[1]), jnp.float32)], axis=0
     )
     target_turned_ref[...] = target.T
-    weight_ref[...] = area_ref[...] * var_ref[...]
-    for load in loads:
+    area = jnp.broadcast_to(area_ref[...], (LANES, area_ref.shape[1])).T
+    scales = jnp.concatenate([var_ref[...], jnp.zeros((1, LANES - variables), jnp.float32)], axis=1)
+    weight_ref[...] = area * scales
+    for load in loads[8:]:
         load.wait()
     node_turned_ref[...] = node_ref[...].T
     own = slice(size, 2 * size)
     base_ref[...] = dot(high_ref[:, own], latent_ref[...]) + grid_ref[...].astype(jnp.float32)
 
-    @pl.when(over_ref[0] > 0)
+    @pl.when(flags_ref[0] > 0)
     def _():
         base_ref[...] += dot(low_ref[:, own], latent_ref[...])
 
@@ -125,7 +138,7 @@
 
 
 def forward_kernel(
-    over_ref, high_ref, base_ref, first_ref, second_ref, node_ref, turned_ref, target_ref, weight_ref, low_hbm,
+    flags_ref, high_ref, base_ref, first_ref, second_ref, node_ref, turned_ref, target_ref, weight_ref, low_hbm,
     shared_ref, fold_ref, lead_ref, gate_ref, normed_ref, inverse_ref,
     low_ref, sum_ref, low_sem,
 ):
@@ -136,7 +149,7 @@
 
     sum_ref[...] = gather(high_ref) + base_ref[...]
 
-    @pl.when(over_ref[0] > 0)
+    @pl.when(flags_ref[0] > 0)
     def _():
         copy = pltpu.make_async_copy(low_hbm, low_ref, low_sem)
         copy.start()
@@ -190,7 +203,7 @@
 
 
 def backward_kernel(
-    me_ref, over_ref, everyone_ref, fold_ref, lead_ref, weight_ref, gate_ref,
+    flags_ref, everyone_ref, fold_ref, lead_ref, weight_ref, gate_ref,
     pad_ref, turned_ref, normed_ref, inverse_ref, high_ref, low_hbm,
     blocks_ref, first_ref, second_ref, send_ref,
     low_ref, scale_ref, low_sem, *, pair_scale
@@ -198,7 +211,7 @@
     members = everyone_ref.shape[0]
     grid_rows, width = normed_ref.shape
     rest_rows = grid_rows - MAIN
-    me = me_ref[0]
+    me = flags_ref[1]
     first = FOLDS * rest_rows
     lane = lax.broadcasted_iota(jnp.int32, (members, LANES), 1)
     tails = everyone_ref[:, first:MAIN, :].astype(jnp.float32)
@@ -243,7 +256,7 @@
     for ref, at in places:
         ref[...] = dot(high_ref[:, at], send_ref[...]).astype(jnp.bfloat16)
 
-    @pl.when(over_ref[0] > 0)
+    @pl.when(flags_ref[0] > 0)
     def _():
         copy = pltpu.make_async_copy(low_hbm, low_ref, low_sem)
         copy.start()
@@ -254,14 +267,14 @@
 
 
 def tail_kernel(
-    over_ref, high_ref, send_ref, first_ref, second_ref, landed_ref, low_hbm, out_hbm, share_ref,
+    flags_ref, high_ref, send_ref, first_ref, second_ref, landed_ref, low_hbm, out_hbm, share_ref,
     low_ref, sum_ref, out_ref, low_sem, out_sems
 ):
     rows = send_ref.shape[0]
     own = slice(rows, 2 * rows)
     sum_ref[...] = dot(high_ref[:, own], send_ref[...])
 
-    @pl.when(over_ref[0] > 0)
+    @pl.when(flags_ref[0] > 0)
     def _():
         copy = pltpu.make_async_copy(low_hbm, low_ref, low_sem)
         copy.start()
@@ -329,7 +342,7 @@
     first = to_neighbours(latent, 0)
     second = to_neighbours(latent, 1)
     outs = [
-        shape((1,), i32),
+        pltpu.SMEM((2,), i32),
         pltpu.HBM((grid_rows, 3 * mesh_rows), b16),
         pltpu.HBM((mesh_rows, 3 * grid_rows), b16),
         pltpu.VMEM((grid_rows, 3 * mesh_rows), b16),
@@ -342,27 +355,34 @@
         pltpu.VMEM((grid_rows, LANES), f32),
         pltpu.VMEM((grid_rows, LANES), f32),
     ]
+    ins = [
+        me,
+        edge_count,
+        edge_src.reshape(1, -1),
+        edge_dst.reshape(1, -1),
+        area_weight[None, :],
+        var_weight[None, :],
+        out_weight,
+        target,
+        node_weight,
+        latent,
+        grid_latent,
+    ]
+    smem = pltpu.SMEM
     (
-        over, low, back_low, high, back_high, base, node, node_turned, out_pad, out_turned, target_turned, weight
+        flags, low, back_low, high, back_high, base, node, node_turned, out_pad, out_turned, target_turned, weight
     ) = pl.pallas_call(
         edges_kernel,
         out_shape=outs,
-        in_specs=[SMEM] * 2 + [VMEM] * 6 + [HBM] * 3,
+        in_specs=[HBM] * len(ins),
         out_specs=[SMEM] + [HBM] * 2 + [VMEM] * 9,
-        scratch_shapes=[held(v) for v in (latent, grid_latent, *outs[1:3])] + [dma((3,)), dma((2,))],
+        scratch_shapes=[smem((1,), i32), smem(edge_count.shape, i32)]
+        + [held(v) for v in (*ins[2:8], *ins[9:], *outs[1:3])]
+        + [dma((len(ins),)), dma((2,))],
         compiler_params=PARAMS,
         cost_estimate=cost_of(500, 8),
-    )(
-        me,
-        edge_count,
-        edge_src[0],
-        edge_dst[0],
-        out_weight,
-        target,
-        area_weight[:, None],
-        jnp.pad(var_weight, (0, LANES - variables))[None, :],
-        *in_hbm(latent, grid_latent, node_weight),
-    )
+    )(*in_hbm(*ins))
+    flags = pltpu.with_memory_space_constraint(flags, pltpu.SMEM)
 
     outs = [
         pltpu.VMEM((members, MAIN, LANES), jnp.int16),
@@ -380,7 +400,7 @@
         scratch_shapes=[held(low), pltpu.VMEM((grid_rows, width), f32), dma],
         compiler_params=PARAMS,
         cost_estimate=cost_of(1000, 8),
-    )(over, high, base, first, second, node, out_turned, target_turned, weight, *in_hbm(low))
+    )(flags, high, base, first, second, node, out_turned, target_turned, weight, *in_hbm(low))
     everyone = lax.all_to_all(shared, "member", 0, 0, tiled=True)
 
     pair_scale = (1.0 - (1.0 - ALPHA) / members) / (members - 1)
@@ -393,13 +413,13 @@
     blocks, first_part, second_part, grad_send = pl.pallas_call(
         functools.partial(backward_kernel, pair_scale=pair_scale),
         out_shape=outs,
-        in_specs=[SMEM] * 2 + [VMEM] * 10 + [HBM],
+        in_specs=[SMEM] + [VMEM] * 10 + [HBM],
         out_specs=[VMEM] * 4,
         scratch_shapes=[held(back_low), pltpu.VMEM((FOLDS, members, LANES), f32), dma],
         compiler_params=PARAMS,
         cost_estimate=cost_of(1000, 8),
     )(
-        me, over, everyone, folded, lead, weight, gate, out_pad, node_turned, normed, inverse, back_high,
+        flags, everyone, folded, lead, weight, gate, out_pad, node_turned, normed, inverse, back_high,
         *in_hbm(back_low),
     )
     landed = lax.all_to_all(blocks, "member", 0, 0, tiled=True)
@@ -419,7 +439,7 @@
         ],
         compiler_params=PARAMS,
         cost_estimate=cost_of(130, 3),
-    )(over, back_high, grad_send, first_back, second_back, landed, *in_hbm(back_low))
+    )(flags, back_high, grad_send, first_back, second_back, landed, *in_hbm(back_low))
     return (grad_latent[None], grid_share.T)
 
 

time: 81.7 us -> 79.8 us (0.977)
  waiting for transfers between devices: 1.7 us -> 8.35 us
  local copies, waits for them, and re-layouts: 4.66 us -> 0 us
  Pallas kernels: 12.6 us -> 8.98 us
    ppermute x4, waiting for transfers between devices: 1.7 us -> 8.35 us  [to_neighbours(): return lax.ppermute(value, ('member', 'grid'), pairs)]
    unnamed x7 -> x0, local copies, waits for them, and re-layouts: 3.19 us -> none
    pallas_call x1, Pallas kernels: 4.85 us -> 2.88 us  [per_device(): pl.pallas_call(edges_kernel, out_shape=outs, in_specs=[HBM] * len(ins), o...]
    broadcast_in_dim x2 -> x0, local copies, waits for them, and re-layouts: 1.47 us -> none  [the longest x1 0.81 us: per_device(): area_weight[:, None]]
  transfers between devices with their start and end apart: 4 -> 4, of which waited for: 1 -> 2; matrix products, arithmetic and copies ran while one was open for 3% -> 0% of each run, Pallas kernels for 6% -> 4%
where the time goes in v5:
time: 79.8 us; the launch traced here: 79.6 us
  blocking collectives  40.6 us (51%)
  starting transfers between devices  21 us (26%)
  Pallas kernels  8.98 us (11%)
  waiting for transfers between devices  8.35 us (10%)
    all_to_all x1, blocking collectives, per_device(): everyone = lax.all_to_all(shared, 'member', 0, 0, tiled=True)  22.8 us
    ppermute x4, starting transfers between devices, to_neighbours(): return lax.ppermute(value, ('member', 'grid'), pairs)  21 us
    all_to_all x1, blocking collectives, per_device(): landed = lax.all_to_all(blocks, 'member', 0, 0, tiled=True)  17.8 us
    ppermute x4, waiting for transfers between devices, to_neighbours(): return lax.ppermute(value, ('member', 'grid'), pairs)  8.35 us
    pallas_call x1, Pallas kernels, per_device(): pl.pallas_call(edges_kernel, out_shape=outs, in_specs=[HBM] * len(ins), o...  2.88 us
    pallas_call x1, Pallas kernels, per_device(): pl.pallas_call(functools.partial(backward_kernel, pair_scale=pair_scale),...  2.19 us
    pallas_call x1, Pallas kernels, per_device(): pl.pallas_call(forward_kernel, out_shape=outs, in_specs=[SMEM] + [VMEM] *...  2.02 us
    pallas_call x1, Pallas kernels, per_device(): pl.pallas_call(tail_kernel, out_shape=[pltpu.HBM((mesh_rows, width), b16)...  1.89 us
  transfers between devices with their start and end apart: 4, of which 2 were waited for; matrix products, arithmetic and copies ran while one was open for 0% of the time, Pallas kernels for 4%

profile of v5, /device:TPU:1, one launch (start us, length us, event | category | flops | bytes accessed | tf_op | source)
XLA Modules:
  0.0 79.6 jit_solution(5231239773832729975)
XLA Ops:
  0.6 4.4 %collective-permute-start.1 = (bf16[256,1024]{1,0:T(8,128)(2,1)}, bf16[256,1024]{1,0:T(8,128)(2,1)S(1)}, u32[]{:S(2)}, u32[]{:S(2)}) collective-permute-start(bf16[256,1024]{1,0:T(8,128)(2,1)} %bitcast.8), channel_id=1, source_target_pairs={{0,31},{1,0},{2,1},{3,2},{4,3},{5,4},{6,5},{7,6},{8,7},{9,8},{10,9... | collective-permute-start | bytes 1572872 | tf_op jit(solution)/shard_map/ppermute | solution.py:31
  5.0 10.5 %collective-permute-start = (bf16[256,1024]{1,0:T(8,128)(2,1)}, bf16[256,1024]{1,0:T(8,128)(2,1)S(1)}, u32[]{:S(2)}, u32[]{:S(2)}) collective-permute-start(bf16[256,1024]{1,0:T(8,128)(2,1)} %bitcast.9), channel_id=1, source_target_pairs={{0,1},{1,2},{2,3},{3,4},{4,5},{5,6},{6,7},{7,8},{8,9},{9,10},{10,1... | collective-permute-start | bytes 1572872 | tf_op jit(solution)/shard_map/ppermute | solution.py:31
  15.5 2.9 %shard_map.113 = (s32[2]{0:T(128)S(4)}, bf16[256,768]{1,0:T(8,128)(2,1)}, bf16[256,768]{1,0:T(8,128)(2,1)}, bf16[256,768]{1,0:T(8,128)(2,1)S(1)}, bf16[256,768]{...) custom-call(s32[1]{0:T(128)} %bitcast.me_hbm, ...), custom_call_target="tpu_custom_call" | custom-call | flops 524288000 | bytes 8388608 | tf_op jit(solution)/shard_map/pallas_call | solution.py:374
  18.4 1.9 %collective-permute-done.1.second_ref = bf16[256,1024]{1,0:T(8,128)(2,1)S(1)} collective-permute-done((bf16[256,1024]{1,0:T(8,128)(2,1)}, bf16[256,1024]{1,0:T(8,128)(2,1)S(1)}, u32[]{:S(2)}, u32[]{:S(2)}) %collective-permute-start.1) | collective-permute-done | bytes 524320 | tf_op jit(solution)/shard_map/ppermute | solution.py:31
  20.4 6.4 %collective-permute-done.first_ref = bf16[256,1024]{1,0:T(8,128)(2,1)S(1)} collective-permute-done((bf16[256,1024]{1,0:T(8,128)(2,1)}, bf16[256,1024]{1,0:T(8,128)(2,1)S(1)}, u32[]{:S(2)}, u32[]{:S(2)}) %collective-permute-start) | collective-permute-done | bytes 524320 | tf_op jit(solution)/shard_map/ppermute | solution.py:31
  26.8 2.0 %shard_map.114 = (s16[16,208,128]{2,1,0:T(8,128)(2,1)S(1)}, f32[208,128]{1,0:T(8,128)S(1)}, f32[256,128]{1,0:T(8,128)S(1)}, f32[256,1024]{1,0:T(8,128)S(1)}, f32...) custom-call(s32[2]{0:T(128)S(4)} %get-tuple-element.26.flags_ref, bf16[256,768]{1,0:T(8,128)(2,1)S(1)} %get-tuple-element.28.high_ref, ...), custom_call_target="tpu_custom_call" | custom-call | flops 1048576000 | bytes 8388608 | tf_op jit(solution)/shard_map/pallas_call | solution.py:395
  28.8 22.8 %all_to_all.10.everyone_ref = s16[16,208,128]{2,1,0:T(8,128)(2,1)S(1)} all-to-all(s16[16,208,128]{2,1,0:T(8,128)(2,1)S(1)} %get-tuple-element.35), channel_id=1, replica_groups=mesh['member'=16,'grid'=32] {'member'}, dimensions={0} | all-to-all | bytes 1703936 | tf_op jit(solution)/shard_map/all_to_all | solution.py:404
  51.6 2.2 %shard_map.115 = (bf16[16,128,128]{2,1,0:T(8,128)(2,1)S(1)}, bf16[256,1024]{1,0:T(8,128)(2,1)S(1)}, bf16[256,1024]{1,0:T(8,128)(2,1)S(1)}, bf16[256,1024]{1,0:T(8,128)(2,1)S(1)}) custom-call(s32[2]{0:T(128)S(4)} %get-tuple-element.26.flags_ref, s16[16,208,128]{2,1,0:T(8,128)(2,1)S(1)} %all_to_all.10.everyone_ref, f32[208,128]{1,0:T(8,128)S(1)} %get-tuple-element.36.fold_ref, ...), custom_call_target="tpu_custom_call" | custom-call | flops 1048576000 | bytes 8388608 | tf_op jit(solution)/shard_map/pallas_call | solution.py:413
  53.7 4.2 %collective-permute-start.2 = (bf16[256,1024]{1,0:T(8,128)(2,1)S(1)}, bf16[256,1024]{1,0:T(8,128)(2,1)S(1)}, u32[]{:S(2)}, u32[]{:S(2)}) collective-permute-start(bf16[256,1024]{1,0:T(8,128)(2,1)S(1)} %get-tuple-element.45), channel_id=1, source_target_pairs={{0,1},{1,2},{2,3},{3,4},{4,5},{5,6},{6,7},{7,8},{8,9},{9,10},{10,1... | collective-permute-start | bytes 1572872 | tf_op jit(solution)/shard_map/ppermute | solution.py:31
  57.9 1.9 %collective-permute-start.3 = (bf16[256,1024]{1,0:T(8,128)(2,1)S(1)}, bf16[256,1024]{1,0:T(8,128)(2,1)S(1)}, u32[]{:S(2)}, u32[]{:S(2)}) collective-permute-start(bf16[256,1024]{1,0:T(8,128)(2,1)S(1)} %get-tuple-element.46), channel_id=1, source_target_pairs={{0,31},{1,0},{2,1},{3,2},{4,3},{5,4},{6,5},{7,6},{8,7},{9,8},{10,9... | collective-permute-start | bytes 1572872 | tf_op jit(solution)/shard_map/ppermute | solution.py:31
  59.8 17.8 %all_to_all.11.landed_ref = bf16[16,128,128]{2,1,0:T(8,128)(2,1)S(1)} all-to-all(bf16[16,128,128]{2,1,0:T(8,128)(2,1)S(1)} %get-tuple-element.47), channel_id=1, replica_groups=mesh['member'=16,'grid'=32] {'member'}, dimensions={0} | all-to-all | bytes 1048576 | tf_op jit(solution)/shard_map/all_to_all | solution.py:425
  77.7 0.0 collective-permute-done.2.first_ref
  77.7 0.0 collective-permute-done.3.second_ref
  77.7 1.9 %shard_map.116 = (bf16[256,1024]{1,0:T(8,128)(2,1)}, bf16[64,256]{1,0:T(8,128)(2,1)}) custom-call(s32[2]{0:T(128)S(4)} %get-tuple-element.26.flags_ref, bf16[256,768]{1,0:T(8,128)(2,1)S(1)} %get-tuple-element.27.high_ref, bf16[256,1024]{1,0:T(8,128)(2,1)S(1)} %get-tuple-element.44.send_ref, bf16[256,1024]{1,0:T(8,128)(2,1)S(1)} %collective-permute-done.2.first_ref, ...), custom_call_target="tpu_custom_call" | custom-call | flops 136314880 | bytes 3145728 | tf_op jit(solution)/shard_map/pallas_call | solution.py:428
Async XLA Ops:
  0.6 19.7 %collective-permute-start.1 = (bf16[256,1024]{1,0:T(8,128)(2,1)}, bf16[256,1024]{1,0:T(8,128)(2,1)S(1)}, u32[]{:S(2)}, u32[]{:S(2)}) collective-permute-start(bf16[256,1024]{1,0:T(8,128)(2,1)} %bitcast.8), channel_id=1, source_target_pairs={{0,31},{1,0},{2,1},{3,2},{4,3},{5,4},{6,5},{7,6},{8,7},{9,8},{10,9... | collective-permute-start | bytes 1572872 | tf_op jit(solution)/shard_map/ppermute | solution.py:31
  5.0 21.8 %collective-permute-start = (bf16[256,1024]{1,0:T(8,128)(2,1)}, bf16[256,1024]{1,0:T(8,128)(2,1)S(1)}, u32[]{:S(2)}, u32[]{:S(2)}) collective-permute-start(bf16[256,1024]{1,0:T(8,128)(2,1)} %bitcast.9), channel_id=1, source_target_pairs={{0,1},{1,2},{2,3},{3,4},{4,5},{5,6},{6,7},{7,8},{8,9},{9,10},{10,1... | collective-permute-start | bytes 1572872 | tf_op jit(solution)/shard_map/ppermute | solution.py:31
  53.7 23.9 %collective-permute-start.2 = (bf16[256,1024]{1,0:T(8,128)(2,1)S(1)}, bf16[256,1024]{1,0:T(8,128)(2,1)S(1)}, u32[]{:S(2)}, u32[]{:S(2)}) collective-permute-start(bf16[256,1024]{1,0:T(8,128)(2,1)S(1)} %get-tuple-element.45), channel_id=1, source_target_pairs={{0,1},{1,2},{2,3},{3,4},{4,5},{5,6},{6,7},{7,8},{8,9},{9,10},{10,1... | collective-permute-start | bytes 1572872 | tf_op jit(solution)/shard_map/ppermute | solution.py:31
  57.9 19.8 %collective-permute-start.3 = (bf16[256,1024]{1,0:T(8,128)(2,1)S(1)}, bf16[256,1024]{1,0:T(8,128)(2,1)S(1)}, u32[]{:S(2)}, u32[]{:S(2)}) collective-permute-start(bf16[256,1024]{1,0:T(8,128)(2,1)S(1)} %get-tuple-element.46), channel_id=1, source_target_pairs={{0,31},{1,0},{2,1},{3,2},{4,3},{5,4},{6,5},{7,6},{8,7},{9,8},{10,9... | collective-permute-start | bytes 1572872 | tf_op jit(solution)/shard_map/ppermute | solution.py:31

commit v6 on v5

--- a/solution.py
+++ b/solution.py
@@ -205,7 +205,7 @@
 def backward_kernel(
     flags_ref, everyone_ref, fold_ref, lead_ref, weight_ref, gate_ref,
     pad_ref, turned_ref, normed_ref, inverse_ref, high_ref, low_hbm,
-    blocks_ref, first_ref, second_ref, send_ref,
+    keep_ref, give_ref, first_ref, second_ref, send_ref,
     low_ref, scale_ref, low_sem, *, pair_scale
 ):
     members = everyone_ref.shape[0]
@@ -246,12 +246,15 @@
     send_ref[...] = grad_summed.astype(jnp.bfloat16)
     half = grid_rows // 2
     lower = lax.broadcasted_iota(jnp.int32, (half, LANES), 1) < LANES // 2
+    odd = lax.rem(me, 2) == 1
     for pair in range(width // LANES):
         at = slice(pair * LANES, (pair + 1) * LANES)
         top = grad_summed[:half, at]
         bottom = grad_summed[half:, at]
-        blocks_ref[2 * pair] = jnp.where(lower, top, turn(bottom, LANES // 2)).astype(jnp.bfloat16)
-        blocks_ref[2 * pair + 1] = jnp.where(lower, turn(top, LANES // 2), bottom).astype(jnp.bfloat16)
+        even_block = jnp.where(lower, top, turn(bottom, LANES // 2))
+        odd_block = jnp.where(lower, turn(top, LANES // 2), bottom)
+        keep_ref[pair] = jnp.where(odd, odd_block, even_block)
+        give_ref[pair] = jnp.where(odd, even_block, odd_block).astype(jnp.bfloat16)
     places = ((first_ref, slice(0, grid_rows)), (second_ref, slice(2 * grid_rows, 3 * grid_rows)))
     for ref, at in places:
         ref[...] = dot(high_ref[:, at], send_ref[...]).astype(jnp.bfloat16)
@@ -264,6 +267,10 @@
         for ref, at in places:
             total = dot(high_ref[:, at], send_ref[...]) + dot(low_ref[:, at], send_ref[...])
             ref[...] = total.astype(jnp.bfloat16)
+
+
+def pair_add_kernel(keep_ref, got_ref, out_ref):
+    out_ref[...] = (keep_ref[...] + got_ref[...].astype(jnp.float32)).astype(jnp.bfloat16)
 
 
 def tail_kernel(
@@ -405,16 +412,17 @@
 
     pair_scale = (1.0 - (1.0 - ALPHA) / members) / (members - 1)
     outs = [
-        pltpu.VMEM((members, grid_rows // 2, LANES), b16),
+        pltpu.VMEM((members // 2, grid_rows // 2, LANES), f32),
+        pltpu.VMEM((members // 2, grid_rows // 2, LANES), b16),
         pltpu.VMEM((mesh_rows, width), b16),
         pltpu.VMEM((mesh_rows, width), b16),
         pltpu.VMEM((grid_rows, width), b16),
     ]
-    blocks, first_part, second_part, grad_send = pl.pallas_call(
+    keep, give, first_part, second_part, grad_send = pl.pallas_call(
         functools.partial(backward_kernel, pair_scale=pair_scale),
         out_shape=outs,
         in_specs=[SMEM] + [VMEM] * 10 + [HBM],
-        out_specs=[VMEM] * 4,
+        out_specs=[VMEM] * 5,
         scratch_shapes=[held(back_low), pltpu.VMEM((FOLDS, members, LANES), f32), dma],
         compiler_params=PARAMS,
         cost_estimate=cost_of(1000, 8),
@@ -422,9 +430,19 @@
         flags, everyone, folded, lead, weight, gate, out_pad, node_turned, normed, inverse, back_high,
         *in_hbm(back_low),
     )
-    landed = lax.all_to_all(blocks, "member", 0, 0, tiled=True)
+    got = lax.ppermute(give, "member", [(member, member ^ 1) for member in range(members)])
     first_back = to_neighbours(first_part, 0)
     second_back = to_neighbours(second_part, 1)
+    (blocks,) = pl.pallas_call(
+        pair_add_kernel,
+        out_shape=[pltpu.VMEM(give.shape, b16)],
+        in_specs=[VMEM] * 2,
+        out_specs=[VMEM],
+        compiler_params=PARAMS,
+        cost_estimate=cost_of(1, 1),
+    )(keep, got)
+    cores = [[core + 2 * chip for chip in range(members // 2)] for core in range(2)]
+    landed = lax.all_to_all(blocks, "member", 0, 0, axis_index_groups=cores, tiled=True)
     grad_latent, grid_share = pl.pallas_call(
         tail_kernel,
         out_shape=[pltpu.HBM((mesh_rows, width), b16), shape((width // members, grid_rows), b16)],

time: 79.8 us -> 77.8 us (0.975)
  blocking collectives: 40.6 us -> 33 us
  starting transfers between devices: 21 us -> 25.3 us
  waiting for transfers between devices: 8.35 us -> 9.49 us
    all_to_all x1, blocking collectives: 17.8 us -> 10.3 us  [per_device(): lax.all_to_all(blocks, 'member', 0, 0, axis_index_groups=cores, tiled=True)]
    ppermute x0 -> x1, starting transfers between devices: none -> 4.3 us  [per_device(): lax.ppermute(give, 'member', [(member, member ^ 1) for member in range(me...]
    ppermute x0 -> x1, waiting for transfers between devices: none -> 1.14 us  [per_device(): lax.ppermute(give, 'member', [(member, member ^ 1) for member in range(me...]
  transfers between devices with their start and end apart: 4 -> 5, of which waited for: 2 -> 3; matrix products, arithmetic and copies ran while one was open for 0% -> 0% of each run, Pallas kernels for 4% -> 4%
where the time goes in v6:
time: 77.8 us; the launch traced here: 77.5 us
  blocking collectives  33 us (42%)
  starting transfers between devices  25.3 us (33%)
  waiting for transfers between devices  9.49 us (12%)
  Pallas kernels  9.01 us (12%)
    all_to_all x1, blocking collectives, per_device(): everyone = lax.all_to_all(shared, 'member', 0, 0, tiled=True)  22.8 us
    ppermute x4, starting transfers between devices, to_neighbours(): return lax.ppermute(value, ('member', 'grid'), pairs)  21 us
    all_to_all x1, blocking collectives, per_device(): lax.all_to_all(blocks, 'member', 0, 0, axis_index_groups=cores, tiled=True)  10.3 us
    ppermute x4, waiting for transfers between devices, to_neighbours(): return lax.ppermute(value, ('member', 'grid'), pairs)  8.35 us
    ppermute x1, starting transfers between devices, per_device(): lax.ppermute(give, 'member', [(member, member ^ 1) for member in range(me...  4.3 us
    pallas_call x1, Pallas kernels, per_device(): pl.pallas_call(edges_kernel, out_shape=outs, in_specs=[HBM] * len(ins), o...  2.88 us
    pallas_call x1, Pallas kernels, per_device(): pl.pallas_call(functools.partial(backward_kernel, pair_scale=pair_scale),...  2.21 us
    pallas_call x1, Pallas kernels, per_device(): pl.pallas_call(forward_kernel, out_shape=outs, in_specs=[SMEM] + [VMEM] *...  2.02 us
  transfers between devices with their start and end apart: 5, of which 3 were waited for; matrix products, arithmetic and copies ran while one was open for 0% of the time, Pallas kernels for 4%

profile of v6, /device:TPU:1, one launch (start us, length us, event | category | flops | bytes accessed | tf_op | source)
XLA Modules:
  0.0 77.5 jit_solution(18316578533800562793)
XLA Ops:
  0.6 4.4 %collective-permute-start.1 = (bf16[256,1024]{1,0:T(8,128)(2,1)}, bf16[256,1024]{1,0:T(8,128)(2,1)S(1)}, u32[]{:S(2)}, u32[]{:S(2)}) collective-permute-start(bf16[256,1024]{1,0:T(8,128)(2,1)} %bitcast.8), channel_id=1, source_target_pairs={{0,31},{1,0},{2,1},{3,2},{4,3},{5,4},{6,5},{7,6},{8,7},{9,8},{10,9... | collective-permute-start | bytes 1572872 | tf_op jit(solution)/shard_map/ppermute | solution.py:31
  5.0 10.5 %collective-permute-start = (bf16[256,1024]{1,0:T(8,128)(2,1)}, bf16[256,1024]{1,0:T(8,128)(2,1)S(1)}, u32[]{:S(2)}, u32[]{:S(2)}) collective-permute-start(bf16[256,1024]{1,0:T(8,128)(2,1)} %bitcast.9), channel_id=1, source_target_pairs={{0,1},{1,2},{2,3},{3,4},{4,5},{5,6},{6,7},{7,8},{8,9},{9,10},{10,1... | collective-permute-start | bytes 1572872 | tf_op jit(solution)/shard_map/ppermute | solution.py:31
  15.5 2.9 %shard_map.113 = (s32[2]{0:T(128)S(4)}, bf16[256,768]{1,0:T(8,128)(2,1)}, bf16[256,768]{1,0:T(8,128)(2,1)}, bf16[256,768]{1,0:T(8,128)(2,1)S(1)}, bf16[256,768]{...) custom-call(s32[1]{0:T(128)} %bitcast.me_hbm, ...), custom_call_target="tpu_custom_call" | custom-call | flops 524288000 | bytes 8388608 | tf_op jit(solution)/shard_map/pallas_call | solution.py:381
  18.4 1.9 %collective-permute-done.1.second_ref = bf16[256,1024]{1,0:T(8,128)(2,1)S(1)} collective-permute-done((bf16[256,1024]{1,0:T(8,128)(2,1)}, bf16[256,1024]{1,0:T(8,128)(2,1)S(1)}, u32[]{:S(2)}, u32[]{:S(2)}) %collective-permute-start.1) | collective-permute-done | bytes 524320 | tf_op jit(solution)/shard_map/ppermute | solution.py:31
  20.4 6.4 %collective-permute-done.first_ref = bf16[256,1024]{1,0:T(8,128)(2,1)S(1)} collective-permute-done((bf16[256,1024]{1,0:T(8,128)(2,1)}, bf16[256,1024]{1,0:T(8,128)(2,1)S(1)}, u32[]{:S(2)}, u32[]{:S(2)}) %collective-permute-start) | collective-permute-done | bytes 524320 | tf_op jit(solution)/shard_map/ppermute | solution.py:31
  26.8 2.0 %shard_map.114 = (s16[16,208,128]{2,1,0:T(8,128)(2,1)S(1)}, f32[208,128]{1,0:T(8,128)S(1)}, f32[256,128]{1,0:T(8,128)S(1)}, f32[256,1024]{1,0:T(8,128)S(1)}, f32...) custom-call(s32[2]{0:T(128)S(4)} %get-tuple-element.27.flags_ref, bf16[256,768]{1,0:T(8,128)(2,1)S(1)} %get-tuple-element.29.high_ref, ...), custom_call_target="tpu_custom_call" | custom-call | flops 1048576000 | bytes 8388608 | tf_op jit(solution)/shard_map/pallas_call | solution.py:402
  28.8 22.8 %all_to_all.10.everyone_ref = s16[16,208,128]{2,1,0:T(8,128)(2,1)S(1)} all-to-all(s16[16,208,128]{2,1,0:T(8,128)(2,1)S(1)} %get-tuple-element.36), channel_id=1, replica_groups=mesh['member'=16,'grid'=32] {'member'}, dimensions={0} | all-to-all | bytes 1703936 | tf_op jit(solution)/shard_map/all_to_all | solution.py:411
  51.6 2.2 %shard_map.115 = (f32[8,128,128]{2,1,0:T(8,128)S(1)}, bf16[8,128,128]{2,1,0:T(8,128)(2,1)S(1)}, bf16[256,1024]{1,0:T(8,128)(2,1)S(1)}, bf16[256,1024]{1,0:T(8,128)(2,1)S(1)}, bf16[256,1024]{1,0:T(8,128)(2,1)S(1)}) custom-call(s32[2]{0:T(128)S(4)} %get-tuple-element.27.flags_ref, s16[16,208,128]{2,1,0:T(8,128)(2,1)S(1)} %all_to_all.10.everyone_ref, ...), custom_call_target="tpu_custom_call" | custom-call | flops 1048576000 | bytes 8388608 | tf_op jit(solution)/shard_map/pallas_call | solution.py:421
  53.8 4.2 %collective-permute-start.2 = (bf16[256,1024]{1,0:T(8,128)(2,1)S(1)}, bf16[256,1024]{1,0:T(8,128)(2,1)S(1)}, u32[]{:S(2)}, u32[]{:S(2)}) collective-permute-start(bf16[256,1024]{1,0:T(8,128)(2,1)S(1)} %get-tuple-element.46), channel_id=1, source_target_pairs={{0,1},{1,2},{2,3},{3,4},{4,5},{5,6},{6,7},{7,8},{8,9},{9,10},{10,1... | collective-permute-start | bytes 1572872 | tf_op jit(solution)/shard_map/ppermute | solution.py:31
  57.9 1.9 %collective-permute-start.3 = (bf16[256,1024]{1,0:T(8,128)(2,1)S(1)}, bf16[256,1024]{1,0:T(8,128)(2,1)S(1)}, u32[]{:S(2)}, u32[]{:S(2)}) collective-permute-start(bf16[256,1024]{1,0:T(8,128)(2,1)S(1)} %get-tuple-element.47), channel_id=1, source_target_pairs={{0,31},{1,0},{2,1},{3,2},{4,3},{5,4},{6,5},{7,6},{8,7},{9,8},{10,9... | collective-permute-start | bytes 1572872 | tf_op jit(solution)/shard_map/ppermute | solution.py:31
  59.9 4.3 %collective-permute-start.4 = (bf16[8,128,128]{2,1,0:T(8,128)(2,1)S(1)}, bf16[8,128,128]{2,1,0:T(8,128)(2,1)S(1)}, u32[]{:S(2)}, u32[]{:S(2)}) collective-permute-start(bf16[8,128,128]{2,1,0:T(8,128)(2,1)S(1)} %get-tuple-element.49), channel_id=1, source_target_pairs={{0,32},{32,0},{64,96},{96,64},{128,160},{160,128},{192,224},{224,1... | collective-permute-start | bytes 786440 | tf_op jit(solution)/shard_map/ppermute | solution.py:433
  64.2 1.1 %collective-permute-done.4.got_ref = bf16[8,128,128]{2,1,0:T(8,128)(2,1)S(1)} collective-permute-done((bf16[8,128,128]{2,1,0:T(8,128)(2,1)S(1)}, bf16[8,128,128]{2,1,0:T(8,128)(2,1)S(1)}, u32[]{:S(2)}, u32[]{:S(2)}) %collective-permute-start.4) | collective-permute-done | bytes 262176 | tf_op jit(solution)/shard_map/ppermute | solution.py:433
  65.4 10.3 %all_to_all.11.landed_ref = bf16[8,128,128]{2,1,0:T(8,128)(2,1)S(1)} all-to-all(bf16[8,128,128]{2,1,0:T(8,128)(2,1)S(1)} %shard_map.116), channel_id=1, replica_groups={{0,64,128,192,256,320,384,448},{32,96,160,224,288,352,416,480},{1,65,12..., dimensions={0} | all-to-all | bytes 524288 | tf_op jit(solution)/shard_map/all_to_all | solution.py:445
  75.6 0.0 collective-permute-done.2.first_ref
  75.7 0.0 collective-permute-done.3.second_ref
  75.7 1.9 %shard_map.117 = (bf16[256,1024]{1,0:T(8,128)(2,1)}, bf16[64,256]{1,0:T(8,128)(2,1)}) custom-call(s32[2]{0:T(128)S(4)} %get-tuple-element.27.flags_ref, bf16[256,768]{1,0:T(8,128)(2,1)S(1)} %get-tuple-element.28.high_ref, bf16[256,1024]{1,0:T(8,128)(2,1)S(1)} %get-tuple-element.45.send_ref, bf16[256,1024]{1,0:T(8,128)(2,1)S(1)} %collective-permute-done.2.first_ref, ...), custom_call_target="tpu_custom_call" | custom-call | flops 136314880 | bytes 3145728 | tf_op jit(solution)/shard_map/pallas_call | solution.py:446
  (1 shorter events, 0.0 us)
Async XLA Ops:
  0.6 19.7 %collective-permute-start.1 = (bf16[256,1024]{1,0:T(8,128)(2,1)}, bf16[256,1024]{1,0:T(8,128)(2,1)S(1)}, u32[]{:S(2)}, u32[]{:S(2)}) collective-permute-start(bf16[256,1024]{1,0:T(8,128)(2,1)} %bitcast.8), channel_id=1, source_target_pairs={{0,31},{1,0},{2,1},{3,2},{4,3},{5,4},{6,5},{7,6},{8,7},{9,8},{10,9... | collective-permute-start | bytes 1572872 | tf_op jit(solution)/shard_map/ppermute | solution.py:31
  5.0 21.8 %collective-permute-start = (bf16[256,1024]{1,0:T(8,128)(2,1)}, bf16[256,1024]{1,0:T(8,128)(2,1)S(1)}, u32[]{:S(2)}, u32[]{:S(2)}) collective-permute-start(bf16[256,1024]{1,0:T(8,128)(2,1)} %bitcast.9), channel_id=1, source_target_pairs={{0,1},{1,2},{2,3},{3,4},{4,5},{5,6},{6,7},{7,8},{8,9},{9,10},{10,1... | collective-permute-start | bytes 1572872 | tf_op jit(solution)/shard_map/ppermute | solution.py:31
  53.8 21.9 %collective-permute-start.2 = (bf16[256,1024]{1,0:T(8,128)(2,1)S(1)}, bf16[256,1024]{1,0:T(8,128)(2,1)S(1)}, u32[]{:S(2)}, u32[]{:S(2)}) collective-permute-start(bf16[256,1024]{1,0:T(8,128)(2,1)S(1)} %get-tuple-element.46), channel_id=1, source_target_pairs={{0,1},{1,2},{2,3},{3,4},{4,5},{5,6},{6,7},{7,8},{8,9},{9,10},{10,1... | collective-permute-start | bytes 1572872 | tf_op jit(solution)/shard_map/ppermute | solution.py:31
  57.9 17.7 %collective-permute-start.3 = (bf16[256,1024]{1,0:T(8,128)(2,1)S(1)}, bf16[256,1024]{1,0:T(8,128)(2,1)S(1)}, u32[]{:S(2)}, u32[]{:S(2)}) collective-permute-start(bf16[256,1024]{1,0:T(8,128)(2,1)S(1)} %get-tuple-element.47), channel_id=1, source_target_pairs={{0,31},{1,0},{2,1},{3,2},{4,3},{5,4},{6,5},{7,6},{8,7},{9,8},{10,9... | collective-permute-start | bytes 1572872 | tf_op jit(solution)/shard_map/ppermute | solution.py:31
  59.9 5.4 %collective-permute-start.4 = (bf16[8,128,128]{2,1,0:T(8,128)(2,1)S(1)}, bf16[8,128,128]{2,1,0:T(8,128)(2,1)S(1)}, u32[]{:S(2)}, u32[]{:S(2)}) collective-permute-start(bf16[8,128,128]{2,1,0:T(8,128)(2,1)S(1)} %get-tuple-element.49), channel_id=1, source_target_pairs={{0,32},{32,0},{64,96},{96,64},{128,160},{160,128},{192,224},{224,1... | collective-permute-start | bytes 786440 | tf_op jit(solution)/shard_map/ppermute | solution.py:433

commit v7 on v6

--- a/solution.py
+++ b/solution.py
@@ -203,33 +203,35 @@
 
 
 def backward_kernel(
-    flags_ref, everyone_ref, fold_ref, lead_ref, weight_ref, gate_ref,
+    flags_ref, alike_ref, unlike_ref, fold_ref, lead_ref, weight_ref, gate_ref,
     pad_ref, turned_ref, normed_ref, inverse_ref, high_ref, low_hbm,
     keep_ref, give_ref, first_ref, second_ref, send_ref,
     low_ref, scale_ref, low_sem, *, pair_scale
 ):
-    members = everyone_ref.shape[0]
+    chips = alike_ref.shape[0]
     grid_rows, width = normed_ref.shape
     rest_rows = grid_rows - MAIN
     me = flags_ref[1]
     first = FOLDS * rest_rows
-    lane = lax.broadcasted_iota(jnp.int32, (members, LANES), 1)
-    tails = everyone_ref[:, first:MAIN, :].astype(jnp.float32)
-    code = jnp.zeros((members, LANES), jnp.float32)
-    for k in range(FOLDS):
-        piece = turn(tails[:, k, :], FOLD * k - VARS)
-        code = jnp.where((lane >= FOLD * k) & (lane < FOLD * (k + 1)), piece, code)
-    scale = jnp.exp2(code * (1.0 / CODE)) * (1.0 / STEPS)
-    for k in range(FOLDS):
-        scale_ref[k] = jnp.where(lane < VARS, scale, turn(scale, VARS - FOLD * k))
+    lane = lax.broadcasted_iota(jnp.int32, (chips, LANES), 1)
+    for core, ref in enumerate((alike_ref, unlike_ref)):
+        tails = ref[:, first:MAIN, :].astype(jnp.float32)
+        code = jnp.zeros((chips, LANES), jnp.float32)
+        for k in range(FOLDS):
+            piece = turn(tails[:, k, :], FOLD * k - VARS)
+            code = jnp.where((lane >= FOLD * k) & (lane < FOLD * (k + 1)), piece, code)
+        scale = jnp.exp2(code * (1.0 / CODE)) * (1.0 / STEPS)
+        for k in range(FOLDS):
+            scale_ref[core, k] = jnp.where(lane < VARS, scale, turn(scale, VARS - FOLD * k))
 
     bounds = [(k * rest_rows, (k + 1) * rest_rows) for k in range(FOLDS)] + [(first, MAIN)]
     parts = [jnp.zeros((high - low, LANES), jnp.float32) for low, high in bounds]
-    for step in range(1, members):
-        other = lax.rem(me + step, members)
+    others = [(0, alike_ref, lax.rem(me // 2 + step, chips)) for step in range(1, chips)]
+    others += [(1, unlike_ref, chip) for chip in range(chips)]
+    for core, ref, other in others:
         for i, (low, high) in enumerate(bounds):
-            factor = scale_ref[min(i, FOLDS - 1), pl.ds(other, 1), :]
-            theirs = everyone_ref[other, low:high, :].astype(jnp.float32) * factor
+            factor = scale_ref[core, min(i, FOLDS - 1), pl.ds(other, 1), :]
+            theirs = ref[other, low:high, :].astype(jnp.float32) * factor
             parts[i] = parts[i] + smooth_slope(fold_ref[low:high, :] - theirs)
     pair_sum = unfold(jnp.concatenate(parts, axis=0), grid_rows)
     real = lanes_of(pair_sum) < VARS
@@ -392,7 +394,7 @@
     flags = pltpu.with_memory_space_constraint(flags, pltpu.SMEM)
 
     outs = [
-        pltpu.VMEM((members, MAIN, LANES), jnp.int16),
+        pltpu.VMEM((members // 2, MAIN, LANES), jnp.int16),
         pltpu.VMEM((MAIN, LANES), f32),
         pltpu.VMEM((grid_rows, LANES), f32),
         pltpu.VMEM((grid_rows, width), f32),
@@ -408,7 +410,10 @@
         compiler_params=PARAMS,
         cost_estimate=cost_of(1000, 8),
     )(flags, high, base, first, second, node, out_turned, target_turned, weight, *in_hbm(low))
-    everyone = lax.all_to_all(shared, "member", 0, 0, tiled=True)
+    cores = [[core + 2 * chip for chip in range(members // 2)] for core in range(2)]
+    swap = [(member, member ^ 1) for member in range(members)]
+    alike = lax.all_to_all(shared, "member", 0, 0, axis_index_groups=cores, tiled=True)
+    unlike = lax.ppermute(alike, "member", swap)
 
     pair_scale = (1.0 - (1.0 - ALPHA) / members) / (members - 1)
     outs = [
@@ -421,16 +426,16 @@
     keep, give, first_part, second_part, grad_send = pl.pallas_call(
         functools.partial(backward_kernel, pair_scale=pair_scale),
         out_shape=outs,
-        in_specs=[SMEM] + [VMEM] * 10 + [HBM],
+        in_specs=[SMEM] + [VMEM] * 11 + [HBM],
         out_specs=[VMEM] * 5,
-        scratch_shapes=[held(back_low), pltpu.VMEM((FOLDS, members, LANES), f32), dma],
+        scratch_shapes=[held(back_low), pltpu.VMEM((2, FOLDS, members // 2, LANES), f32), dma],
         compiler_params=PARAMS,
         cost_estimate=cost_of(1000, 8),
     )(
-        flags, everyone, folded, lead, weight, gate, out_pad, node_turned, normed, inverse, back_high,
+        flags, alike, unlike, folded, lead, weight, gate, out_pad, node_turned, normed, inverse, back_high,
         *in_hbm(back_low),
     )
-    got = lax.ppermute(give, "member", [(member, member ^ 1) for member in range(members)])
+    got = lax.ppermute(give, "member", swap)
     first_back = to_neighbours(first_part, 0)
     second_back = to_neighbours(second_part, 1)
     (blocks,) = pl.pallas_call(
@@ -441,7 +446,6 @@
         compiler_params=PARAMS,
         cost_estimate=cost_of(1, 1),
     )(keep, got)
-    cores = [[core + 2 * chip for chip in range(members // 2)] for core in range(2)]
     landed = lax.all_to_all(blocks, "member", 0, 0, axis_index_groups=cores, tiled=True)
     grad_latent, grid_share = pl.pallas_call(
         tail_kernel,

time: 77.8 us -> 75.3 us (0.968)
  blocking collectives: 33 us -> 24.8 us
  starting transfers between devices: 25.3 us -> 29.6 us
  waiting for transfers between devices: 9.49 us -> 10.9 us
    all_to_all x1, blocking collectives: 22.8 us -> 14.8 us  [per_device(): lax.all_to_all(shared, 'member', 0, 0, axis_index_groups=cores, tiled=True)]
    ppermute x1 -> x2, starting transfers between devices: 4.3 us -> 7.63 us  [the longest x1 4.52 us: per_device(): unlike = lax.ppermute(alike, 'member', swap)]
    ppermute x1 -> x2, waiting for transfers between devices: 1.14 us -> 2.51 us  [the longest x1 1.37 us: per_device(): unlike = lax.ppermute(alike, 'member', swap)]
    ppermute x4, starting transfers between devices: 21 us -> 22 us  [to_neighbours(): return lax.ppermute(value, ('member', 'grid'), pairs)]
  transfers between devices with their start and end apart: 5 -> 6, of which waited for: 3 -> 4; matrix products, arithmetic and copies ran while one was open for 0% -> 0% of each run, Pallas kernels for 4% -> 4%
where the time goes in v7:
time: 75.3 us; the launch traced here: 75 us
  starting transfers between devices  29.6 us (39%)
  blocking collectives  24.8 us (33%)
  waiting for transfers between devices  10.9 us (14%)
  Pallas kernels  8.96 us (12%)
    ppermute x4, starting transfers between devices, to_neighbours(): return lax.ppermute(value, ('member', 'grid'), pairs)  22 us
    all_to_all x1, blocking collectives, per_device(): lax.all_to_all(shared, 'member', 0, 0, axis_index_groups=cores, tiled=True)  14.8 us
    all_to_all x1, blocking collectives, per_device(): lax.all_to_all(blocks, 'member', 0, 0, axis_index_groups=cores, tiled=True)  9.97 us
    ppermute x4, waiting for transfers between devices, to_neighbours(): return lax.ppermute(value, ('member', 'grid'), pairs)  8.35 us
    ppermute x1, starting transfers between devices, per_device(): unlike = lax.ppermute(alike, 'member', swap)  4.52 us
    ppermute x1, starting transfers between devices, per_device(): got = lax.ppermute(give, 'member', swap)  3.12 us
    pallas_call x1, Pallas kernels, per_device(): pl.pallas_call(edges_kernel, out_shape=outs, in_specs=[HBM] * len(ins), o...  2.88 us
    pallas_call x1, Pallas kernels, per_device(): pl.pallas_call(functools.partial(backward_kernel, pair_scale=pair_scale),...  2.2 us
  transfers between devices with their start and end apart: 6, of which 4 were waited for; matrix products, arithmetic and copies ran while one was open for 0% of the time, Pallas kernels for 4%

profile of v7, /device:TPU:1, one launch (start us, length us, event | category | flops | bytes accessed | tf_op | source)
XLA Modules:
  0.0 75.0 jit_solution(15344026123354940418)
XLA Ops:
  0.6 4.4 %collective-permute-start.1 = (bf16[256,1024]{1,0:T(8,128)(2,1)}, bf16[256,1024]{1,0:T(8,128)(2,1)S(1)}, u32[]{:S(2)}, u32[]{:S(2)}) collective-permute-start(bf16[256,1024]{1,0:T(8,128)(2,1)} %bitcast.8), channel_id=1, source_target_pairs={{0,31},{1,0},{2,1},{3,2},{4,3},{5,4},{6,5},{7,6},{8,7},{9,8},{10,9... | collective-permute-start | bytes 1572872 | tf_op jit(solution)/shard_map/ppermute | solution.py:31
  5.0 10.5 %collective-permute-start = (bf16[256,1024]{1,0:T(8,128)(2,1)}, bf16[256,1024]{1,0:T(8,128)(2,1)S(1)}, u32[]{:S(2)}, u32[]{:S(2)}) collective-permute-start(bf16[256,1024]{1,0:T(8,128)(2,1)} %bitcast.9), channel_id=1, source_target_pairs={{0,1},{1,2},{2,3},{3,4},{4,5},{5,6},{6,7},{7,8},{8,9},{9,10},{10,1... | collective-permute-start | bytes 1572872 | tf_op jit(solution)/shard_map/ppermute | solution.py:31
  15.5 2.9 %shard_map.113 = (s32[2]{0:T(128)S(4)}, bf16[256,768]{1,0:T(8,128)(2,1)}, bf16[256,768]{1,0:T(8,128)(2,1)}, bf16[256,768]{1,0:T(8,128)(2,1)S(1)}, bf16[256,768]{...) custom-call(s32[1]{0:T(128)} %bitcast.me_hbm, ...), custom_call_target="tpu_custom_call" | custom-call | flops 524288000 | bytes 8388608 | tf_op jit(solution)/shard_map/pallas_call | solution.py:383
  18.4 1.9 %collective-permute-done.1.second_ref = bf16[256,1024]{1,0:T(8,128)(2,1)S(1)} collective-permute-done((bf16[256,1024]{1,0:T(8,128)(2,1)}, bf16[256,1024]{1,0:T(8,128)(2,1)S(1)}, u32[]{:S(2)}, u32[]{:S(2)}) %collective-permute-start.1) | collective-permute-done | bytes 524320 | tf_op jit(solution)/shard_map/ppermute | solution.py:31
  20.4 6.4 %collective-permute-done.first_ref = bf16[256,1024]{1,0:T(8,128)(2,1)S(1)} collective-permute-done((bf16[256,1024]{1,0:T(8,128)(2,1)}, bf16[256,1024]{1,0:T(8,128)(2,1)S(1)}, u32[]{:S(2)}, u32[]{:S(2)}) %collective-permute-start) | collective-permute-done | bytes 524320 | tf_op jit(solution)/shard_map/ppermute | solution.py:31
  26.8 2.0 %shard_map.114 = (s16[8,208,128]{2,1,0:T(8,128)(2,1)S(1)}, f32[208,128]{1,0:T(8,128)S(1)}, f32[256,128]{1,0:T(8,128)S(1)}, f32[256,1024]{1,0:T(8,128)S(1)}, f32[...) custom-call(s32[2]{0:T(128)S(4)} %get-tuple-element.27.flags_ref, bf16[256,768]{1,0:T(8,128)(2,1)S(1)} %get-tuple-element.29.high_ref, ...), custom_call_target="tpu_custom_call" | custom-call | flops 1048576000 | bytes 8388608 | tf_op jit(solution)/shard_map/pallas_call | solution.py:404
  28.8 14.8 %all_to_all.10.alike_ref = s16[8,208,128]{2,1,0:T(8,128)(2,1)S(1)} all-to-all(s16[8,208,128]{2,1,0:T(8,128)(2,1)S(1)} %get-tuple-element.36), channel_id=1, replica_groups={{0,64,128,192,256,320,384,448},{32,96,160,224,288,352,416,480},{1,65,12..., dimensions={0} | all-to-all | bytes 851968 | tf_op jit(solution)/shard_map/all_to_all | solution.py:415
  43.6 4.5 %collective-permute-start.2 = (s16[8,208,128]{2,1,0:T(8,128)(2,1)S(1)}, s16[8,208,128]{2,1,0:T(8,128)(2,1)S(1)}, u32[]{:S(2)}, u32[]{:S(2)}) collective-permute-start(s16[8,208,128]{2,1,0:T(8,128)(2,1)S(1)} %all_to_all.10.alike_ref), channel_id=1, source_target_pairs={{0,32},{32,0},{64,96},{96,64},{128,160},{160,128},{192,224},{224,1... | collective-permute-start | bytes 1277960 | tf_op jit(solution)/shard_map/ppermute | solution.py:416
  48.1 1.4 %collective-permute-done.2.unlike_ref = s16[8,208,128]{2,1,0:T(8,128)(2,1)S(1)} collective-permute-done((s16[8,208,128]{2,1,0:T(8,128)(2,1)S(1)}, s16[8,208,128]{2,1,0:T(8,128)(2,1)S(1)}, u32[]{:S(2)}, u32[]{:S(2)}) %collective-permute-start.2) | collective-permute-done | bytes 426016 | tf_op jit(solution)/shard_map/ppermute | solution.py:416
  49.5 2.2 %shard_map.115 = (f32[8,128,128]{2,1,0:T(8,128)S(1)}, bf16[8,128,128]{2,1,0:T(8,128)(2,1)S(1)}, bf16[256,1024]{1,0:T(8,128)(2,1)S(1)}, bf16[256,1024]{1,0:T(8,128)(2,1)S(1)}, bf16[256,1024]{1,0:T(8,128)(2,1)S(1)}) custom-call(s32[2]{0:T(128)S(4)} %get-tuple-element.27.flags_ref, s16[8,208,128]{2,1,0:T(8,128)(2,1)S(1)} %all_to_all.10.alike_ref, ...), custom_call_target="tpu_custom_call" | custom-call | flops 1048576000 | bytes 8388608 | tf_op jit(solution)/shard_map/pallas_call | solution.py:426
  51.7 5.2 %collective-permute-start.3 = (bf16[256,1024]{1,0:T(8,128)(2,1)S(1)}, bf16[256,1024]{1,0:T(8,128)(2,1)S(1)}, u32[]{:S(2)}, u32[]{:S(2)}) collective-permute-start(bf16[256,1024]{1,0:T(8,128)(2,1)S(1)} %get-tuple-element.46), channel_id=1, source_target_pairs={{0,1},{1,2},{2,3},{3,4},{4,5},{5,6},{6,7},{7,8},{8,9},{9,10},{10,1... | collective-permute-start | bytes 1572872 | tf_op jit(solution)/shard_map/ppermute | solution.py:31
  56.9 1.9 %collective-permute-start.4 = (bf16[256,1024]{1,0:T(8,128)(2,1)S(1)}, bf16[256,1024]{1,0:T(8,128)(2,1)S(1)}, u32[]{:S(2)}, u32[]{:S(2)}) collective-permute-start(bf16[256,1024]{1,0:T(8,128)(2,1)S(1)} %get-tuple-element.47), channel_id=1, source_target_pairs={{0,31},{1,0},{2,1},{3,2},{4,3},{5,4},{6,5},{7,6},{8,7},{9,8},{10,9... | collective-permute-start | bytes 1572872 | tf_op jit(solution)/shard_map/ppermute | solution.py:31
  58.8 3.1 %collective-permute-start.5 = (bf16[8,128,128]{2,1,0:T(8,128)(2,1)S(1)}, bf16[8,128,128]{2,1,0:T(8,128)(2,1)S(1)}, u32[]{:S(2)}, u32[]{:S(2)}) collective-permute-start(bf16[8,128,128]{2,1,0:T(8,128)(2,1)S(1)} %get-tuple-element.49), channel_id=1, source_target_pairs={{0,32},{32,0},{64,96},{96,64},{128,160},{160,128},{192,224},{224,1... | collective-permute-start | bytes 786440 | tf_op jit(solution)/shard_map/ppermute | solution.py:438
  61.9 1.1 %collective-permute-done.5.got_ref = bf16[8,128,128]{2,1,0:T(8,128)(2,1)S(1)} collective-permute-done((bf16[8,128,128]{2,1,0:T(8,128)(2,1)S(1)}, bf16[8,128,128]{2,1,0:T(8,128)(2,1)S(1)}, u32[]{:S(2)}, u32[]{:S(2)}) %collective-permute-start.5) | collective-permute-done | bytes 262176 | tf_op jit(solution)/shard_map/ppermute | solution.py:438
  63.1 10.0 %all_to_all.11.landed_ref = bf16[8,128,128]{2,1,0:T(8,128)(2,1)S(1)} all-to-all(bf16[8,128,128]{2,1,0:T(8,128)(2,1)S(1)} %shard_map.116), channel_id=1, replica_groups={{0,64,128,192,256,320,384,448},{32,96,160,224,288,352,416,480},{1,65,12..., dimensions={0} | all-to-all | bytes 524288 | tf_op jit(solution)/shard_map/all_to_all | solution.py:449
  73.1 0.0 collective-permute-done.3.first_ref
  73.1 0.0 collective-permute-done.4.second_ref
  73.1 1.9 %shard_map.117 = (bf16[256,1024]{1,0:T(8,128)(2,1)}, bf16[64,256]{1,0:T(8,128)(2,1)}) custom-call(s32[2]{0:T(128)S(4)} %get-tuple-element.27.flags_ref, bf16[256,768]{1,0:T(8,128)(2,1)S(1)} %get-tuple-element.28.high_ref, bf16[256,1024]{1,0:T(8,128)(2,1)S(1)} %get-tuple-element.45.send_ref, bf16[256,1024]{1,0:T(8,128)(2,1)S(1)} %collective-permute-done.3.first_ref, ...), custom_call_target="tpu_custom_call" | custom-call | flops 136314880 | bytes 3145728 | tf_op jit(solution)/shard_map/pallas_call | solution.py:450
  (1 shorter events, 0.0 us)
Async XLA Ops:
  0.6 19.7 %collective-permute-start.1 = (bf16[256,1024]{1,0:T(8,128)(2,1)}, bf16[256,1024]{1,0:T(8,128)(2,1)S(1)}, u32[]{:S(2)}, u32[]{:S(2)}) collective-permute-start(bf16[256,1024]{1,0:T(8,128)(2,1)} %bitcast.8), channel_id=1, source_target_pairs={{0,31},{1,0},{2,1},{3,2},{4,3},{5,4},{6,5},{7,6},{8,7},{9,8},{10,9... | collective-permute-start | bytes 1572872 | tf_op jit(solution)/shard_map/ppermute | solution.py:31
  5.0 21.8 %collective-permute-start = (bf16[256,1024]{1,0:T(8,128)(2,1)}, bf16[256,1024]{1,0:T(8,128)(2,1)S(1)}, u32[]{:S(2)}, u32[]{:S(2)}) collective-permute-start(bf16[256,1024]{1,0:T(8,128)(2,1)} %bitcast.9), channel_id=1, source_target_pairs={{0,1},{1,2},{2,3},{3,4},{4,5},{5,6},{6,7},{7,8},{8,9},{9,10},{10,1... | collective-permute-start | bytes 1572872 | tf_op jit(solution)/shard_map/ppermute | solution.py:31
  43.6 5.9 %collective-permute-start.2 = (s16[8,208,128]{2,1,0:T(8,128)(2,1)S(1)}, s16[8,208,128]{2,1,0:T(8,128)(2,1)S(1)}, u32[]{:S(2)}, u32[]{:S(2)}) collective-permute-start(s16[8,208,128]{2,1,0:T(8,128)(2,1)S(1)} %all_to_all.10.alike_ref), channel_id=1, source_target_pairs={{0,32},{32,0},{64,96},{96,64},{128,160},{160,128},{192,224},{224,1... | collective-permute-start | bytes 1277960 | tf_op jit(solution)/shard_map/ppermute | solution.py:416
  51.7 21.4 %collective-permute-start.3 = (bf16[256,1024]{1,0:T(8,128)(2,1)S(1)}, bf16[256,1024]{1,0:T(8,128)(2,1)S(1)}, u32[]{:S(2)}, u32[]{:S(2)}) collective-permute-start(bf16[256,1024]{1,0:T(8,128)(2,1)S(1)} %get-tuple-element.46), channel_id=1, source_target_pairs={{0,1},{1,2},{2,3},{3,4},{4,5},{5,6},{6,7},{7,8},{8,9},{9,10},{10,1... | collective-permute-start | bytes 1572872 | tf_op jit(solution)/shard_map/ppermute | solution.py:31
  56.9 16.2 %collective-permute-start.4 = (bf16[256,1024]{1,0:T(8,128)(2,1)S(1)}, bf16[256,1024]{1,0:T(8,128)(2,1)S(1)}, u32[]{:S(2)}, u32[]{:S(2)}) collective-permute-start(bf16[256,1024]{1,0:T(8,128)(2,1)S(1)} %get-tuple-element.47), channel_id=1, source_target_pairs={{0,31},{1,0},{2,1},{3,2},{4,3},{5,4},{6,5},{7,6},{8,7},{9,8},{10,9... | collective-permute-start | bytes 1572872 | tf_op jit(solution)/shard_map/ppermute | solution.py:31
  58.8 4.3 %collective-permute-start.5 = (bf16[8,128,128]{2,1,0:T(8,128)(2,1)S(1)}, bf16[8,128,128]{2,1,0:T(8,128)(2,1)S(1)}, u32[]{:S(2)}, u32[]{:S(2)}) collective-permute-start(bf16[8,128,128]{2,1,0:T(8,128)(2,1)S(1)} %get-tuple-element.49), channel_id=1, source_target_pairs={{0,32},{32,0},{64,96},{96,64},{128,160},{160,128},{192,224},{224,1... | collective-permute-start | bytes 786440 | tf_op jit(solution)/shard_map/ppermute | solution.py:438

commit v8 on v7

--- a/solution.py
+++ b/solution.py
@@ -13,11 +13,14 @@
 LANES = 128
 VARS = 100
 MAIN = 208
+TAIL = 16
 FOLD = 25
 FOLDS = 4
 STEPS = 32767.0
 CODE = 256.0
 LOWEST = -20.0
+BLOCK = 256
+EARLY = 2
 VMEM_LIMIT = 20 * 1024 * 1024
 
 
@@ -55,17 +58,15 @@
     )
 
 
-def store_counts(counts, at, high_ref, low_ref):
+def parts_of(counts):
     high = counts.astype(jnp.bfloat16)
-    high_ref[:, at] = high
-    low_ref[:, at] = (counts - high.astype(jnp.float32)).astype(jnp.bfloat16)
-    return jnp.max(counts)
+    return (counts - high.astype(jnp.float32)).astype(jnp.bfloat16), high
 
 
 def edges_kernel(
     me_hbm, count_hbm, src_hbm, dst_hbm, area_hbm, var_hbm, out_hbm, target_hbm, node_hbm, latent_hbm, grid_hbm,
     flags_ref, low_hbm, back_low_hbm,
-    high_ref, back_high_ref, base_ref, node_ref, node_turned_ref, pad_ref, turned_ref, target_turned_ref, weight_ref,
+    high_ref, back_ref, back_own_ref, base_ref, node_ref, node_turned_ref, pad_ref, turned_ref, target_turned_ref, weight_ref,
     me_ref, count_ref, src_ref, dst_ref, area_ref, var_ref, out_ref, target_ref, latent_ref, grid_ref,
     low_ref, back_low_ref, in_sems, out_sems,
 ):
@@ -87,13 +88,15 @@
         targets = one_hot(jnp.where(live, dst_ref[:, at], -1), size)
         sources = one_hot(src_ref[:, at], size)
         counts = count_pairs(targets, sources)
-        most = jnp.maximum(
-            most, store_counts(counts, slice(place * size, (place + 1) * size), high_ref, low_ref)
-        )
+        most = jnp.maximum(most, jnp.max(counts))
+        columns = slice(place * size, (place + 1) * size)
+        low_ref[:, columns], high_ref[:, columns] = parts_of(counts)
         back = 2 - place
-        store_counts(
-            count_pairs(sources, targets), slice(back * size, (back + 1) * size), back_high_ref, back_low_ref
-        )
+        back_low_ref[:, back * size : (back + 1) * size], high = parts_of(count_pairs(sources, targets))
+        if place == 1:
+            back_own_ref[...] = high
+        else:
+            back_ref[:, (back // 2) * size : (back // 2 + 1) * size] = high
     flags_ref[0] = (most > 256.0).astype(jnp.int32)
     flags_ref[1] = me_ref[0]
     stores = start_all((low_ref, back_low_ref), (low_hbm, back_low_hbm), out_sems)
@@ -133,29 +136,33 @@
     return copies
 
 
+def blocks_of(width):
+    return [slice(start, start + BLOCK) for start in range(0, width, BLOCK)]
+
+
 def dot(left, right):
     return jnp.dot(left, right, preferred_element_type=jnp.float32)
 
 
-def forward_kernel(
-    flags_ref, high_ref, base_ref, first_ref, second_ref, node_ref, turned_ref, target_ref, weight_ref, low_hbm,
-    shared_ref, fold_ref, lead_ref, gate_ref, normed_ref, inverse_ref,
-    low_ref, sum_ref, low_sem,
-):
-    size = first_ref.shape[0]
-
-    def gather(counts_ref):
-        return dot(counts_ref[:, :size], first_ref[...]) + dot(counts_ref[:, 2 * size :], second_ref[...])
-
-    sum_ref[...] = gather(high_ref) + base_ref[...]
+def gather_kernel(flags_ref, high_ref, base_ref, rows_ref, low_hbm, out_ref, low_ref, low_sem, *, place):
+    size = rows_ref.shape[0]
+    at = slice(place * size, (place + 1) * size)
+    out_ref[...] = base_ref[...] + dot(high_ref[:, at], rows_ref[...])
 
     @pl.when(flags_ref[0] > 0)
     def _():
         copy = pltpu.make_async_copy(low_hbm, low_ref, low_sem)
         copy.start()
         copy.wait()
-        sum_ref[...] += gather(low_ref)
-
+        out_ref[...] += dot(low_ref[:, at], rows_ref[...])
+
+
+def forward_kernel(
+    flags_ref, high_ref, base_ref, rows_ref, node_ref, turned_ref, target_ref, weight_ref, low_hbm,
+    shared_ref, fold_ref, lead_ref, gate_ref, normed_ref, inverse_ref,
+    low_ref, sum_ref, low_sem, *, place
+):
+    gather_kernel(flags_ref, high_ref, base_ref, rows_ref, low_hbm, sum_ref, low_ref, low_sem, place=place)
     summed = sum_ref[...]
     centered = summed - jnp.mean(summed, axis=-1, keepdims=True)
     inverse = lax.rsqrt(jnp.mean(centered * centered, axis=-1, keepdims=True) + EPS)
@@ -165,8 +172,7 @@
     pre_act = dot(normed.astype(jnp.bfloat16), node_ref[...])
     gate_sig = 0.5 + 0.5 * jnp.tanh(0.5 * pre_act)
     gate_ref[...] = gate_sig * (1.0 + pre_act * (1.0 - gate_sig))
-    hidden = (pre_act * gate_sig).astype(jnp.bfloat16)
-    pred = dot(hidden, turned_ref[...])
+    pred = dot((pre_act * gate_sig).astype(jnp.bfloat16), turned_ref[...])
     largest = jnp.max(jnp.abs(pred), axis=0, keepdims=True)
     code = jnp.ceil(jnp.log2(jnp.maximum(largest, 2.0**LOWEST)) * CODE)
     whole = jnp.round(pred * (jnp.exp2(code * (-1.0 / CODE)) * STEPS))
@@ -202,72 +208,92 @@
     return jnp.concatenate([values, rest], axis=0)
 
 
+def pair_parts(ref, others, fold_ref, scale_ref):
+    chips = ref.shape[0]
+    rest_rows = (MAIN - TAIL) // FOLDS
+    first = FOLDS * rest_rows
+    lane = lax.broadcasted_iota(jnp.int32, (chips, LANES), 1)
+    tails = ref[:, first:MAIN, :].astype(jnp.float32)
+    code = jnp.zeros((chips, LANES), jnp.float32)
+    for k in range(FOLDS):
+        piece = turn(tails[:, k, :], FOLD * k - VARS)
+        code = jnp.where((lane >= FOLD * k) & (lane < FOLD * (k + 1)), piece, code)
+    scale = jnp.exp2(code * (1.0 / CODE)) * (1.0 / STEPS)
+    for k in range(FOLDS):
+        scale_ref[k] = jnp.where(lane < VARS, scale, turn(scale, VARS - FOLD * k))
+
+    bounds = [(k * rest_rows, (k + 1) * rest_rows) for k in range(FOLDS)] + [(first, MAIN)]
+    parts = [jnp.zeros((high - low, LANES), jnp.float32) for low, high in bounds]
+    for other in others:
+        for i, (low, high) in enumerate(bounds):
+            factor = scale_ref[min(i, FOLDS - 1), pl.ds(other, 1), :]
+            theirs = ref[other, low:high, :].astype(jnp.float32) * factor
+            parts[i] = parts[i] + smooth_slope(fold_ref[low:high, :] - theirs)
+    return parts
+
+
+def alike_kernel(flags_ref, alike_ref, fold_ref, out_ref, scale_ref):
+    chips = alike_ref.shape[0]
+    others = [lax.rem(flags_ref[1] // 2 + step, chips) for step in range(1, chips)]
+    out_ref[...] = jnp.concatenate(pair_parts(alike_ref, others, fold_ref, scale_ref), axis=0)
+
+
 def backward_kernel(
-    flags_ref, alike_ref, unlike_ref, fold_ref, lead_ref, weight_ref, gate_ref,
+    flags_ref, alike_sum_ref, unlike_ref, fold_ref, lead_ref, weight_ref, gate_ref,
     pad_ref, turned_ref, normed_ref, inverse_ref, high_ref, low_hbm,
     keep_ref, give_ref, first_ref, second_ref, send_ref,
-    low_ref, scale_ref, low_sem, *, pair_scale
+    low_ref, scale_ref, pre_ref, grad_ref, low_sem, *, pair_scale
 ):
-    chips = alike_ref.shape[0]
     grid_rows, width = normed_ref.shape
-    rest_rows = grid_rows - MAIN
     me = flags_ref[1]
-    first = FOLDS * rest_rows
-    lane = lax.broadcasted_iota(jnp.int32, (chips, LANES), 1)
-    for core, ref in enumerate((alike_ref, unlike_ref)):
-        tails = ref[:, first:MAIN, :].astype(jnp.float32)
-        code = jnp.zeros((chips, LANES), jnp.float32)
-        for k in range(FOLDS):
-            piece = turn(tails[:, k, :], FOLD * k - VARS)
-            code = jnp.where((lane >= FOLD * k) & (lane < FOLD * (k + 1)), piece, code)
-        scale = jnp.exp2(code * (1.0 / CODE)) * (1.0 / STEPS)
-        for k in range(FOLDS):
-            scale_ref[core, k] = jnp.where(lane < VARS, scale, turn(scale, VARS - FOLD * k))
-
-    bounds = [(k * rest_rows, (k + 1) * rest_rows) for k in range(FOLDS)] + [(first, MAIN)]
-    parts = [jnp.zeros((high - low, LANES), jnp.float32) for low, high in bounds]
-    others = [(0, alike_ref, lax.rem(me // 2 + step, chips)) for step in range(1, chips)]
-    others += [(1, unlike_ref, chip) for chip in range(chips)]
-    for core, ref, other in others:
-        for i, (low, high) in enumerate(bounds):
-            factor = scale_ref[core, min(i, FOLDS - 1), pl.ds(other, 1), :]
-            theirs = ref[other, low:high, :].astype(jnp.float32) * factor
-            parts[i] = parts[i] + smooth_slope(fold_ref[low:high, :] - theirs)
-    pair_sum = unfold(jnp.concatenate(parts, axis=0), grid_rows)
+    chips = unlike_ref.shape[0]
+    parts = pair_parts(unlike_ref, list(range(chips)), fold_ref, scale_ref)
+    pair_sum = unfold(jnp.concatenate(parts, axis=0) + alike_sum_ref[...], grid_rows)
     real = lanes_of(pair_sum) < VARS
     grad_pred = lead_ref[...] - pair_scale * weight_ref[...] * jnp.where(real, pair_sum, 0.0)
-    grad_hidden = dot(grad_pred.astype(jnp.bfloat16), pad_ref[...])
-    grad_pre = (grad_hidden * gate_ref[...]).astype(jnp.bfloat16)
-    grad_normed = dot(grad_pre, turned_ref[...])
-    normed = normed_ref[...]
-    grad_summed = inverse_ref[...] * (
-        grad_normed
-        - jnp.mean(grad_normed, axis=-1, keepdims=True)
-        - normed * jnp.mean(grad_normed * normed, axis=-1, keepdims=True)
-    )
-    send_ref[...] = grad_summed.astype(jnp.bfloat16)
+    grad_pred_b = grad_pred.astype(jnp.bfloat16)
+    for at in blocks_of(width):
+        pre_ref[:, at] = (dot(grad_pred_b, pad_ref[:, at]) * gate_ref[:, at]).astype(jnp.bfloat16)
+    plain = jnp.zeros((grid_rows, LANES), jnp.float32)
+    along = jnp.zeros((grid_rows, LANES), jnp.float32)
+    for at in blocks_of(width):
+        grad_normed = dot(pre_ref[...], turned_ref[:, at])
+        grad_ref[:, at] = grad_normed
+        product = grad_normed * normed_ref[:, at]
+        for lane in range(0, BLOCK, LANES):
+            plain = plain + grad_normed[:, lane : lane + LANES]
+            along = along + product[:, lane : lane + LANES]
+    plain = jnp.sum(plain, axis=-1, keepdims=True) * (1.0 / width)
+    along = jnp.sum(along, axis=-1, keepdims=True) * (1.0 / width)
+    inverse = inverse_ref[...]
     half = grid_rows // 2
     lower = lax.broadcasted_iota(jnp.int32, (half, LANES), 1) < LANES // 2
     odd = lax.rem(me, 2) == 1
     for pair in range(width // LANES):
         at = slice(pair * LANES, (pair + 1) * LANES)
-        top = grad_summed[:half, at]
-        bottom = grad_summed[half:, at]
+        grad_summed = inverse * (grad_ref[:, at] - plain - normed_ref[:, at] * along)
+        send_ref[:, at] = grad_summed.astype(jnp.bfloat16)
+        top = grad_summed[:half, :]
+        bottom = grad_summed[half:, :]
         even_block = jnp.where(lower, top, turn(bottom, LANES // 2))
         odd_block = jnp.where(lower, turn(top, LANES // 2), bottom)
         keep_ref[pair] = jnp.where(odd, odd_block, even_block)
         give_ref[pair] = jnp.where(odd, even_block, odd_block).astype(jnp.bfloat16)
-    places = ((first_ref, slice(0, grid_rows)), (second_ref, slice(2 * grid_rows, 3 * grid_rows)))
-    for ref, at in places:
-        ref[...] = dot(high_ref[:, at], send_ref[...]).astype(jnp.bfloat16)
+    sides = ((first_ref, 0), (second_ref, 1))
+    for ref, side in sides:
+        for at in blocks_of(width):
+            counts = high_ref[:, side * grid_rows : (side + 1) * grid_rows]
+            ref[:, at] = dot(counts, send_ref[:, at]).astype(jnp.bfloat16)
 
     @pl.when(flags_ref[0] > 0)
     def _():
         copy = pltpu.make_async_copy(low_hbm, low_ref, low_sem)
         copy.start()
         copy.wait()
-        for ref, at in places:
-            total = dot(high_ref[:, at], send_ref[...]) + dot(low_ref[:, at], send_ref[...])
+        for ref, side in sides:
+            at = slice(side * grid_rows, (side + 1) * grid_rows)
+            low_at = slice(2 * side * grid_rows, (2 * side + 1) * grid_rows)
+            total = dot(high_ref[:, at], send_ref[...]) + dot(low_ref[:, low_at], send_ref[...])
             ref[...] = total.astype(jnp.bfloat16)
 
 
@@ -276,19 +302,18 @@
 
 
 def tail_kernel(
-    flags_ref, high_ref, send_ref, first_ref, second_ref, landed_ref, low_hbm, out_hbm, share_ref,
-    low_ref, sum_ref, out_ref, low_sem, out_sems
+    flags_ref, own_ref, send_ref, first_ref, second_ref, landed_ref, low_hbm, out_hbm, share_hbm,
+    low_ref, sum_ref, out_ref, share_ref, low_sem, out_sems, share_sem
 ):
     rows = send_ref.shape[0]
-    own = slice(rows, 2 * rows)
-    sum_ref[...] = dot(high_ref[:, own], send_ref[...])
+    sum_ref[...] = dot(own_ref[...], send_ref[...])
 
     @pl.when(flags_ref[0] > 0)
     def _():
         copy = pltpu.make_async_copy(low_hbm, low_ref, low_sem)
         copy.start()
         copy.wait()
-        sum_ref[...] += dot(low_ref[:, own], send_ref[...])
+        sum_ref[...] += dot(low_ref[:, rows : 2 * rows], send_ref[...])
 
     parts = out_sems.shape[0]
     stores = []
@@ -306,6 +331,8 @@
     flipped = total.T
     share_ref[:, :half] = flipped[:share, :].astype(jnp.bfloat16)
     share_ref[:, half:] = flipped[share:, :].astype(jnp.bfloat16)
+    stores.append(pltpu.make_async_copy(share_ref, share_hbm, share_sem))
+    stores[-1].start()
     for store in stores:
         store.wait()
 
@@ -355,7 +382,8 @@
         pltpu.HBM((grid_rows, 3 * mesh_rows), b16),
         pltpu.HBM((mesh_rows, 3 * grid_rows), b16),
         pltpu.VMEM((grid_rows, 3 * mesh_rows), b16),
-        pltpu.VMEM((mesh_rows, 3 * grid_rows), b16),
+        pltpu.VMEM((mesh_rows, 2 * grid_rows), b16),
+        pltpu.VMEM((mesh_rows, grid_rows), b16),
         pltpu.VMEM((grid_rows, width), f32),
         pltpu.VMEM((width, width), b16),
         pltpu.VMEM((width, width), b16),
@@ -379,12 +407,12 @@
     ]
     smem = pltpu.SMEM
     (
-        flags, low, back_low, high, back_high, base, node, node_turned, out_pad, out_turned, target_turned, weight
+        flags, low, back_low, high, back, back_own, base, node, node_turned, out_pad, out_turned, target_turned, weight
     ) = pl.pallas_call(
         edges_kernel,
         out_shape=outs,
         in_specs=[HBM] * len(ins),
-        out_specs=[SMEM] + [HBM] * 2 + [VMEM] * 9,
+        out_specs=[SMEM] + [HBM] * 2 + [VMEM] * 10,
         scratch_shapes=[smem((1,), i32), smem(edge_count.shape, i32)]
         + [held(v) for v in (*ins[2:8], *ins[9:], *outs[1:3])]
         + [dma((len(ins),)), dma((2,))],
@@ -393,6 +421,16 @@
     )(*in_hbm(*ins))
     flags = pltpu.with_memory_space_constraint(flags, pltpu.SMEM)
 
+    some_cost = cost_of(1000, 8)
+    (most_rows,) = pl.pallas_call(
+        functools.partial(gather_kernel, place=EARLY),
+        out_shape=[pltpu.VMEM((grid_rows, width), f32)],
+        in_specs=[SMEM] + [VMEM] * 3 + [HBM],
+        out_specs=[VMEM],
+        scratch_shapes=[held(low), dma],
+        compiler_params=PARAMS,
+        cost_estimate=cost_of(130, 2),
+    )(flags, high, base, (first, second)[EARLY // 2], *in_hbm(low))
     outs = [
         pltpu.VMEM((members // 2, MAIN, LANES), jnp.int16),
         pltpu.VMEM((MAIN, LANES), f32),
@@ -402,18 +440,29 @@
         pltpu.VMEM((grid_rows, 1), f32),
     ]
     shared, folded, lead, gate, normed, inverse = pl.pallas_call(
-        forward_kernel,
+        functools.partial(forward_kernel, place=2 - EARLY),
         out_shape=outs,
-        in_specs=[SMEM] + [VMEM] * 8 + [HBM],
+        in_specs=[SMEM] + [VMEM] * 7 + [HBM],
         out_specs=[VMEM] * len(outs),
         scratch_shapes=[held(low), pltpu.VMEM((grid_rows, width), f32), dma],
         compiler_params=PARAMS,
-        cost_estimate=cost_of(1000, 8),
-    )(flags, high, base, first, second, node, out_turned, target_turned, weight, *in_hbm(low))
+        cost_estimate=some_cost,
+    )(
+        flags, high, most_rows, (second, first)[EARLY // 2], node, out_turned, target_turned, weight, *in_hbm(low)
+    )
     cores = [[core + 2 * chip for chip in range(members // 2)] for core in range(2)]
     swap = [(member, member ^ 1) for member in range(members)]
     alike = lax.all_to_all(shared, "member", 0, 0, axis_index_groups=cores, tiled=True)
     unlike = lax.ppermute(alike, "member", swap)
+    (alike_sum,) = pl.pallas_call(
+        alike_kernel,
+        out_shape=[pltpu.VMEM((MAIN, LANES), f32)],
+        in_specs=[SMEM] + [VMEM] * 2,
+        out_specs=[VMEM],
+        scratch_shapes=[pltpu.VMEM((FOLDS, members // 2, LANES), f32)],
+        compiler_params=PARAMS,
+        cost_estimate=cost_of(10, 1),
+    )(flags, alike, folded)
 
     pair_scale = (1.0 - (1.0 - ALPHA) / members) / (members - 1)
     outs = [
@@ -428,11 +477,17 @@
         out_shape=outs,
         in_specs=[SMEM] + [VMEM] * 11 + [HBM],
         out_specs=[VMEM] * 5,
-        scratch_shapes=[held(back_low), pltpu.VMEM((2, FOLDS, members // 2, LANES), f32), dma],
+        scratch_shapes=[
+            held(back_low),
+            pltpu.VMEM((FOLDS, members // 2, LANES), f32),
+            pltpu.VMEM((grid_rows, width), b16),
+            pltpu.VMEM((grid_rows, width), f32),
+            dma,
+        ],
         compiler_params=PARAMS,
         cost_estimate=cost_of(1000, 8),
     )(
-        flags, alike, unlike, folded, lead, weight, gate, out_pad, node_turned, normed, inverse, back_high,
+        flags, alike_sum, unlike, folded, lead, weight, gate, out_pad, node_turned, normed, inverse, back,
         *in_hbm(back_low),
     )
     got = lax.ppermute(give, "member", swap)
@@ -447,21 +502,24 @@
         cost_estimate=cost_of(1, 1),
     )(keep, got)
     landed = lax.all_to_all(blocks, "member", 0, 0, axis_index_groups=cores, tiled=True)
+    share = shape((width // members, grid_rows), b16)
     grad_latent, grid_share = pl.pallas_call(
         tail_kernel,
-        out_shape=[pltpu.HBM((mesh_rows, width), b16), shape((width // members, grid_rows), b16)],
+        out_shape=[pltpu.HBM((mesh_rows, width), b16), pltpu.HBM(share.shape, b16)],
         in_specs=[SMEM] + [VMEM] * 5 + [HBM],
-        out_specs=[HBM, VMEM],
+        out_specs=[HBM, HBM],
         scratch_shapes=[
             held(back_low),
             pltpu.VMEM((mesh_rows, width), f32),
             pltpu.VMEM((mesh_rows, width), b16),
+            held(share),
             dma,
             dma((4,)),
+            dma,
         ],
         compiler_params=PARAMS,
         cost_estimate=cost_of(130, 3),
-    )(flags, back_high, grad_send, first_back, second_back, landed, *in_hbm(back_low))
+    )(flags, back_own, grad_send, first_back, second_back, landed, *in_hbm(back_low))
     return (grad_latent[None], grid_share.T)
 
 

time: 75.3 us -> 74.3 us (0.987)
    pallas_call x1 -> x3, Pallas kernels: 1.97 us -> 2.49 us  [the longest x1 1.82 us: per_device(): pl.pallas_call(functools.partial(forward_kernel, place=2 - EARLY), out_sh...]
  transfers between devices with their start and end apart: 6 -> 6, of which waited for: 4 -> 4; matrix products, arithmetic and copies ran while one was open for 0% -> 0% of each run, Pallas kernels for 4% -> 5%
where the time goes in v8:
time: 74.3 us; the launch traced here: 74 us
  starting transfers between devices  29.6 us (40%)
  blocking collectives  24.8 us (33%)
  waiting for transfers between devices  10.2 us (14%)
  Pallas kernels  8.63 us (12%)
    ppermute x4, starting transfers between devices, to_neighbours(): return lax.ppermute(value, ('member', 'grid'), pairs)  22 us
    all_to_all x1, blocking collectives, per_device(): lax.all_to_all(shared, 'member', 0, 0, axis_index_groups=cores, tiled=True)  14.8 us
    all_to_all x1, blocking collectives, per_device(): lax.all_to_all(blocks, 'member', 0, 0, axis_index_groups=cores, tiled=True)  9.99 us
    ppermute x4, waiting for transfers between devices, to_neighbours(): return lax.ppermute(value, ('member', 'grid'), pairs)  8.06 us
    ppermute x1, starting transfers between devices, per_device(): unlike = lax.ppermute(alike, 'member', swap)  4.52 us
    ppermute x1, starting transfers between devices, per_device(): got = lax.ppermute(give, 'member', swap)  3.09 us
    pallas_call x1, Pallas kernels, per_device(): pl.pallas_call(edges_kernel, out_shape=outs, in_specs=[HBM] * len(ins), o...  2.86 us
    pallas_call x1, Pallas kernels, per_device(): pl.pallas_call(functools.partial(backward_kernel, pair_scale=pair_scale),...  1.97 us
  transfers between devices with their start and end apart: 6, of which 4 were waited for; matrix products, arithmetic and copies ran while one was open for 0% of the time, Pallas kernels for 5%

profile of v8, /device:TPU:1, one launch (start us, length us, event | category | flops | bytes accessed | tf_op | source)
XLA Modules:
  0.0 74.0 jit_solution(13799395643922413311)
XLA Ops:
  0.6 4.4 %collective-permute-start = (bf16[256,1024]{1,0:T(8,128)(2,1)}, bf16[256,1024]{1,0:T(8,128)(2,1)S(1)}, u32[]{:S(2)}, u32[]{:S(2)}) collective-permute-start(bf16[256,1024]{1,0:T(8,128)(2,1)} %bitcast.8), channel_id=1, source_target_pairs={{0,31},{1,0},{2,1},{3,2},{4,3},{5,4},{6,5},{7,6},{8,7},{9,8},{10,9... | collective-permute-start | bytes 1572872 | tf_op jit(solution)/shard_map/ppermute | solution.py:34
  5.0 10.5 %collective-permute-start.1 = (bf16[256,1024]{1,0:T(8,128)(2,1)}, bf16[256,1024]{1,0:T(8,128)(2,1)S(1)}, u32[]{:S(2)}, u32[]{:S(2)}) collective-permute-start(bf16[256,1024]{1,0:T(8,128)(2,1)} %bitcast.9), channel_id=1, source_target_pairs={{0,1},{1,2},{2,3},{3,4},{4,5},{5,6},{6,7},{7,8},{8,9},{9,10},{10,1... | collective-permute-start | bytes 1572872 | tf_op jit(solution)/shard_map/ppermute | solution.py:34
  15.5 2.9 %shard_map.113 = (s32[2]{0:T(128)S(4)}, bf16[256,768]{1,0:T(8,128)(2,1)}, bf16[256,768]{1,0:T(8,128)(2,1)}, bf16[256,768]{1,0:T(8,128)(2,1)S(1)}, bf16[256,512]{...) custom-call(s32[1]{0:T(128)} %bitcast.me_hbm, ...), custom_call_target="tpu_custom_call" | custom-call | flops 524288000 | bytes 8388608 | tf_op jit(solution)/shard_map/pallas_call | solution.py:411
  18.4 2.0 %collective-permute-done.rows_ref = bf16[256,1024]{1,0:T(8,128)(2,1)S(1)} collective-permute-done((bf16[256,1024]{1,0:T(8,128)(2,1)}, bf16[256,1024]{1,0:T(8,128)(2,1)S(1)}, u32[]{:S(2)}, u32[]{:S(2)}) %collective-permute-start) | collective-permute-done | bytes 524320 | tf_op jit(solution)/shard_map/ppermute | solution.py:34
  20.4 0.3 shard_map.114.base_ref
  20.7 6.1 %collective-permute-done.1.rows_ref = bf16[256,1024]{1,0:T(8,128)(2,1)S(1)} collective-permute-done((bf16[256,1024]{1,0:T(8,128)(2,1)}, bf16[256,1024]{1,0:T(8,128)(2,1)S(1)}, u32[]{:S(2)}, u32[]{:S(2)}) %collective-permute-start.1) | collective-permute-done | bytes 524320 | tf_op jit(solution)/shard_map/ppermute | solution.py:34
  26.8 1.8 %shard_map.115 = (s16[8,208,128]{2,1,0:T(8,128)(2,1)S(1)}, f32[208,128]{1,0:T(8,128)S(1)}, f32[256,128]{1,0:T(8,128)S(1)}, f32[256,1024]{1,0:T(8,128)S(1)}, f32[...) custom-call(s32[2]{0:T(128)S(4)} %get-tuple-element.28.flags_ref, bf16[256,768]{1,0:T(8,128)(2,1)S(1)} %get-tuple-element.30.high_ref, ...), custom_call_target="tpu_custom_call" | custom-call | flops 1048576000 | bytes 8388608 | tf_op jit(solution)/shard_map/pallas_call | solution.py:442
  28.6 14.8 %all_to_all.10.alike_ref = s16[8,208,128]{2,1,0:T(8,128)(2,1)S(1)} all-to-all(s16[8,208,128]{2,1,0:T(8,128)(2,1)S(1)} %get-tuple-element.37), channel_id=1, replica_groups={{0,64,128,192,256,320,384,448},{32,96,160,224,288,352,416,480},{1,65,12..., dimensions={0} | all-to-all | bytes 851968 | tf_op jit(solution)/shard_map/all_to_all | solution.py:455
  43.4 4.5 %collective-permute-start.2 = (s16[8,208,128]{2,1,0:T(8,128)(2,1)S(1)}, s16[8,208,128]{2,1,0:T(8,128)(2,1)S(1)}, u32[]{:S(2)}, u32[]{:S(2)}) collective-permute-start(s16[8,208,128]{2,1,0:T(8,128)(2,1)S(1)} %all_to_all.10.alike_ref), channel_id=1, source_target_pairs={{0,32},{32,0},{64,96},{96,64},{128,160},{160,128},{192,224},{224,1... | collective-permute-start | bytes 1277960 | tf_op jit(solution)/shard_map/ppermute | solution.py:456
  47.9 0.4 shard_map.116.alike_sum_ref
  48.3 1.0 %collective-permute-done.2.unlike_ref = s16[8,208,128]{2,1,0:T(8,128)(2,1)S(1)} collective-permute-done((s16[8,208,128]{2,1,0:T(8,128)(2,1)S(1)}, s16[8,208,128]{2,1,0:T(8,128)(2,1)S(1)}, u32[]{:S(2)}, u32[]{:S(2)}) %collective-permute-start.2) | collective-permute-done | bytes 426016 | tf_op jit(solution)/shard_map/ppermute | solution.py:456
  49.3 2.0 %shard_map.117 = (f32[8,128,128]{2,1,0:T(8,128)S(1)}, bf16[8,128,128]{2,1,0:T(8,128)(2,1)S(1)}, bf16[256,1024]{1,0:T(8,128)(2,1)S(1)}, bf16[256,1024]{1,0:T(8,128)(2,1)S(1)}, bf16[256,1024]{1,0:T(8,128)(2,1)S(1)}) custom-call(s32[2]{0:T(128)S(4)} %get-tuple-element.28.flags_ref, f32[208,128]{1,0:T(8,128)S(1)} %shard_map.116.alike_sum_ref, ...), custom_call_target="tpu_custom_call" | custom-call | flops 1048576000 | bytes 8388608 | tf_op jit(solution)/shard_map/pallas_call | solution.py:475
  51.3 5.2 %collective-permute-start.3 = (bf16[256,1024]{1,0:T(8,128)(2,1)S(1)}, bf16[256,1024]{1,0:T(8,128)(2,1)S(1)}, u32[]{:S(2)}, u32[]{:S(2)}) collective-permute-start(bf16[256,1024]{1,0:T(8,128)(2,1)S(1)} %get-tuple-element.48), channel_id=1, source_target_pairs={{0,1},{1,2},{2,3},{3,4},{4,5},{5,6},{6,7},{7,8},{8,9},{9,10},{10,1... | collective-permute-start | bytes 1572872 | tf_op jit(solution)/shard_map/ppermute | solution.py:34
  56.5 1.9 %collective-permute-start.4 = (bf16[256,1024]{1,0:T(8,128)(2,1)S(1)}, bf16[256,1024]{1,0:T(8,128)(2,1)S(1)}, u32[]{:S(2)}, u32[]{:S(2)}) collective-permute-start(bf16[256,1024]{1,0:T(8,128)(2,1)S(1)} %get-tuple-element.49), channel_id=1, source_target_pairs={{0,31},{1,0},{2,1},{3,2},{4,3},{5,4},{6,5},{7,6},{8,7},{9,8},{10,9... | collective-permute-start | bytes 1572872 | tf_op jit(solution)/shard_map/ppermute | solution.py:34
  58.4 3.1 %collective-permute-start.5 = (bf16[8,128,128]{2,1,0:T(8,128)(2,1)S(1)}, bf16[8,128,128]{2,1,0:T(8,128)(2,1)S(1)}, u32[]{:S(2)}, u32[]{:S(2)}) collective-permute-start(bf16[8,128,128]{2,1,0:T(8,128)(2,1)S(1)} %get-tuple-element.51), channel_id=1, source_target_pairs={{0,32},{32,0},{64,96},{96,64},{128,160},{160,128},{192,224},{224,1... | collective-permute-start | bytes 786440 | tf_op jit(solution)/shard_map/ppermute | solution.py:493
  61.5 1.1 %collective-permute-done.5.got_ref = bf16[8,128,128]{2,1,0:T(8,128)(2,1)S(1)} collective-permute-done((bf16[8,128,128]{2,1,0:T(8,128)(2,1)S(1)}, bf16[8,128,128]{2,1,0:T(8,128)(2,1)S(1)}, u32[]{:S(2)}, u32[]{:S(2)}) %collective-permute-start.5) | collective-permute-done | bytes 262176 | tf_op jit(solution)/shard_map/ppermute | solution.py:493
  62.7 10.0 %all_to_all.11.landed_ref = bf16[8,128,128]{2,1,0:T(8,128)(2,1)S(1)} all-to-all(bf16[8,128,128]{2,1,0:T(8,128)(2,1)S(1)} %shard_map.118), channel_id=1, replica_groups={{0,64,128,192,256,320,384,448},{32,96,160,224,288,352,416,480},{1,65,12..., dimensions={0} | all-to-all | bytes 524288 | tf_op jit(solution)/shard_map/all_to_all | solution.py:504
  72.7 0.0 collective-permute-done.3.first_ref
  72.7 0.0 collective-permute-done.4.second_ref
  72.7 1.3 %shard_map.119 = (bf16[256,1024]{1,0:T(8,128)(2,1)}, bf16[64,256]{1,0:T(8,128)(2,1)}) custom-call(s32[2]{0:T(128)S(4)} %get-tuple-element.28.flags_ref, bf16[256,256]{1,0:T(8,128)(2,1)S(1)} %get-tuple-element.29.own_ref, bf16[256,1024]{1,0:T(8,128)(2,1)S(1)} %get-tuple-element.47.send_ref, bf16[256,1024]{1,0:T(8,128)(2,1)S(1)} %collective-permute-done.3.first_ref, ...), custom_call_target="tpu_custom_call" | custom-call | flops 136314880 | bytes 3145728 | tf_op jit(solution)/shard_map/pallas_call | solution.py:506
  (1 shorter events, 0.0 us)
Async XLA Ops:
  0.6 19.7 %collective-permute-start = (bf16[256,1024]{1,0:T(8,128)(2,1)}, bf16[256,1024]{1,0:T(8,128)(2,1)S(1)}, u32[]{:S(2)}, u32[]{:S(2)}) collective-permute-start(bf16[256,1024]{1,0:T(8,128)(2,1)} %bitcast.8), channel_id=1, source_target_pairs={{0,31},{1,0},{2,1},{3,2},{4,3},{5,4},{6,5},{7,6},{8,7},{9,8},{10,9... | collective-permute-start | bytes 1572872 | tf_op jit(solution)/shard_map/ppermute | solution.py:34
  5.0 21.8 %collective-permute-start.1 = (bf16[256,1024]{1,0:T(8,128)(2,1)}, bf16[256,1024]{1,0:T(8,128)(2,1)S(1)}, u32[]{:S(2)}, u32[]{:S(2)}) collective-permute-start(bf16[256,1024]{1,0:T(8,128)(2,1)} %bitcast.9), channel_id=1, source_target_pairs={{0,1},{1,2},{2,3},{3,4},{4,5},{5,6},{6,7},{7,8},{8,9},{9,10},{10,1... | collective-permute-start | bytes 1572872 | tf_op jit(solution)/shard_map/ppermute | solution.py:34
  43.4 5.9 %collective-permute-start.2 = (s16[8,208,128]{2,1,0:T(8,128)(2,1)S(1)}, s16[8,208,128]{2,1,0:T(8,128)(2,1)S(1)}, u32[]{:S(2)}, u32[]{:S(2)}) collective-permute-start(s16[8,208,128]{2,1,0:T(8,128)(2,1)S(1)} %all_to_all.10.alike_ref), channel_id=1, source_target_pairs={{0,32},{32,0},{64,96},{96,64},{128,160},{160,128},{192,224},{224,1... | collective-permute-start | bytes 1277960 | tf_op jit(solution)/shard_map/ppermute | solution.py:456
  51.3 21.4 %collective-permute-start.3 = (bf16[256,1024]{1,0:T(8,128)(2,1)S(1)}, bf16[256,1024]{1,0:T(8,128)(2,1)S(1)}, u32[]{:S(2)}, u32[]{:S(2)}) collective-permute-start(bf16[256,1024]{1,0:T(8,128)(2,1)S(1)} %get-tuple-element.48), channel_id=1, source_target_pairs={{0,1},{1,2},{2,3},{3,4},{4,5},{5,6},{6,7},{7,8},{8,9},{9,10},{10,1... | collective-permute-start | bytes 1572872 | tf_op jit(solution)/shard_map/ppermute | solution.py:34
  56.5 16.2 %collective-permute-start.4 = (bf16[256,1024]{1,0:T(8,128)(2,1)S(1)}, bf16[256,1024]{1,0:T(8,128)(2,1)S(1)}, u32[]{:S(2)}, u32[]{:S(2)}) collective-permute-start(bf16[256,1024]{1,0:T(8,128)(2,1)S(1)} %get-tuple-element.49), channel_id=1, source_target_pairs={{0,31},{1,0},{2,1},{3,2},{4,3},{5,4},{6,5},{7,6},{8,7},{9,8},{10,9... | collective-permute-start | bytes 1572872 | tf_op jit(solution)/shard_map/ppermute | solution.py:34
  58.4 4.2 %collective-permute-start.5 = (bf16[8,128,128]{2,1,0:T(8,128)(2,1)S(1)}, bf16[8,128,128]{2,1,0:T(8,128)(2,1)S(1)}, u32[]{:S(2)}, u32[]{:S(2)}) collective-permute-start(bf16[8,128,128]{2,1,0:T(8,128)(2,1)S(1)} %get-tuple-element.51), channel_id=1, source_target_pairs={{0,32},{32,0},{64,96},{96,64},{128,160},{160,128},{192,224},{224,1... | collective-permute-start | bytes 786440 | tf_op jit(solution)/shard_map/ppermute | solution.py:493

commit v9 on v8

--- a/solution.py
+++ b/solution.py
@@ -158,8 +158,8 @@
 
 
 def forward_kernel(
-    flags_ref, high_ref, base_ref, rows_ref, node_ref, turned_ref, target_ref, weight_ref, low_hbm,
-    shared_ref, fold_ref, lead_ref, gate_ref, normed_ref, inverse_ref,
+    flags_ref, high_ref, base_ref, rows_ref, node_ref, turned_ref, low_hbm,
+    shared_ref, pred_ref, pre_ref, normed_ref, inverse_ref,
     low_ref, sum_ref, low_sem, *, place
 ):
     gather_kernel(flags_ref, high_ref, base_ref, rows_ref, low_hbm, sum_ref, low_ref, low_sem, place=place)
@@ -170,17 +170,16 @@
     normed_ref[...] = normed
     inverse_ref[...] = inverse
     pre_act = dot(normed.astype(jnp.bfloat16), node_ref[...])
+    pre_ref[...] = pre_act
     gate_sig = 0.5 + 0.5 * jnp.tanh(0.5 * pre_act)
-    gate_ref[...] = gate_sig * (1.0 + pre_act * (1.0 - gate_sig))
     pred = dot((pre_act * gate_sig).astype(jnp.bfloat16), turned_ref[...])
+    pred_ref[...] = pred
     largest = jnp.max(jnp.abs(pred), axis=0, keepdims=True)
     code = jnp.ceil(jnp.log2(jnp.maximum(largest, 2.0**LOWEST)) * CODE)
     whole = jnp.round(pred * (jnp.exp2(code * (-1.0 / CODE)) * STEPS))
     packed = fold(whole, code).astype(jnp.int16)
     for member in range(shared_ref.shape[0]):
         shared_ref[member] = packed
-    lead_ref[...] = weight_ref[...] * smooth_slope(pred - target_ref[...])
-    fold_ref[...] = fold(pred)
 
 
 def fold(values, code=None):
@@ -232,10 +231,19 @@
     return parts
 
 
-def alike_kernel(flags_ref, alike_ref, fold_ref, out_ref, scale_ref):
+def alike_kernel(
+    flags_ref, alike_ref, pred_ref, pre_ref, target_ref, weight_ref,
+    out_ref, fold_ref, lead_ref, gate_ref, scale_ref
+):
+    pred = pred_ref[...]
+    fold_ref[...] = fold(pred)
+    lead_ref[...] = weight_ref[...] * smooth_slope(pred - target_ref[...])
     chips = alike_ref.shape[0]
     others = [lax.rem(flags_ref[1] // 2 + step, chips) for step in range(1, chips)]
     out_ref[...] = jnp.concatenate(pair_parts(alike_ref, others, fold_ref, scale_ref), axis=0)
+    pre_act = pre_ref[...]
+    gate_sig = 0.5 + 0.5 * jnp.tanh(0.5 * pre_act)
+    gate_ref[...] = gate_sig * (1.0 + pre_act * (1.0 - gate_sig))
 
 
 def backward_kernel(
@@ -269,21 +277,25 @@
     half = grid_rows // 2
     lower = lax.broadcasted_iota(jnp.int32, (half, LANES), 1) < LANES // 2
     odd = lax.rem(me, 2) == 1
-    for pair in range(width // LANES):
-        at = slice(pair * LANES, (pair + 1) * LANES)
-        grad_summed = inverse * (grad_ref[:, at] - plain - normed_ref[:, at] * along)
-        send_ref[:, at] = grad_summed.astype(jnp.bfloat16)
-        top = grad_summed[:half, :]
-        bottom = grad_summed[half:, :]
-        even_block = jnp.where(lower, top, turn(bottom, LANES // 2))
-        odd_block = jnp.where(lower, turn(top, LANES // 2), bottom)
-        keep_ref[pair] = jnp.where(odd, odd_block, even_block)
-        give_ref[pair] = jnp.where(odd, even_block, odd_block).astype(jnp.bfloat16)
     sides = ((first_ref, 0), (second_ref, 1))
-    for ref, side in sides:
-        for at in blocks_of(width):
+    for block in blocks_of(width):
+        summed_b = []
+        for start in range(block.start, block.stop, LANES):
+            at = slice(start, start + LANES)
+            pair = start // LANES
+            grad_summed = inverse * (grad_ref[:, at] - plain - normed_ref[:, at] * along)
+            summed_b.append(grad_summed.astype(jnp.bfloat16))
+            top = grad_summed[:half, :]
+            bottom = grad_summed[half:, :]
+            even_block = jnp.where(lower, top, turn(bottom, LANES // 2))
+            odd_block = jnp.where(lower, turn(top, LANES // 2), bottom)
+            keep_ref[pair] = jnp.where(odd, odd_block, even_block)
+            give_ref[pair] = jnp.where(odd, even_block, odd_block).astype(jnp.bfloat16)
+        summed_b = jnp.concatenate(summed_b, axis=1)
+        send_ref[:, block] = summed_b
+        for ref, side in sides:
             counts = high_ref[:, side * grid_rows : (side + 1) * grid_rows]
-            ref[:, at] = dot(counts, send_ref[:, at]).astype(jnp.bfloat16)
+            ref[:, block] = dot(counts, summed_b).astype(jnp.bfloat16)
 
     @pl.when(flags_ref[0] > 0)
     def _():
@@ -297,29 +309,31 @@
             ref[...] = total.astype(jnp.bfloat16)
 
 
-def pair_add_kernel(keep_ref, got_ref, out_ref):
+def pair_add_kernel(keep_ref, got_ref, after_ref, out_ref):
     out_ref[...] = (keep_ref[...] + got_ref[...].astype(jnp.float32)).astype(jnp.bfloat16)
 
 
-def tail_kernel(
-    flags_ref, own_ref, send_ref, first_ref, second_ref, landed_ref, low_hbm, out_hbm, share_hbm,
-    low_ref, sum_ref, out_ref, share_ref, low_sem, out_sems, share_sem
-):
+def own_kernel(flags_ref, own_ref, send_ref, low_hbm, out_ref, low_ref, low_sem):
     rows = send_ref.shape[0]
-    sum_ref[...] = dot(own_ref[...], send_ref[...])
+    out_ref[...] = dot(own_ref[...], send_ref[...])
 
     @pl.when(flags_ref[0] > 0)
     def _():
         copy = pltpu.make_async_copy(low_hbm, low_ref, low_sem)
         copy.start()
         copy.wait()
-        sum_ref[...] += dot(low_ref[:, rows : 2 * rows], send_ref[...])
-
+        out_ref[...] += dot(low_ref[:, rows : 2 * rows], send_ref[...])
+
+
+def tail_kernel(
+    own_ref, first_ref, second_ref, landed_ref, out_hbm, share_hbm, out_ref, share_ref, out_sems, share_sem
+):
+    rows = own_ref.shape[0]
     parts = out_sems.shape[0]
     stores = []
     for part in range(parts):
         at = slice(part * rows // parts, (part + 1) * rows // parts)
-        total = sum_ref[at, :] + first_ref[at, :].astype(jnp.float32) + second_ref[at, :].astype(jnp.float32)
+        total = own_ref[at, :] + first_ref[at, :].astype(jnp.float32) + second_ref[at, :].astype(jnp.float32)
         out_ref[at, :] = total.astype(jnp.bfloat16)
         stores.append(pltpu.make_async_copy(out_ref.at[at, :], out_hbm.at[at, :], out_sems.at[part]))
         stores[-1].start()
@@ -433,36 +447,40 @@
     )(flags, high, base, (first, second)[EARLY // 2], *in_hbm(low))
     outs = [
         pltpu.VMEM((members // 2, MAIN, LANES), jnp.int16),
-        pltpu.VMEM((MAIN, LANES), f32),
         pltpu.VMEM((grid_rows, LANES), f32),
         pltpu.VMEM((grid_rows, width), f32),
         pltpu.VMEM((grid_rows, width), f32),
         pltpu.VMEM((grid_rows, 1), f32),
     ]
-    shared, folded, lead, gate, normed, inverse = pl.pallas_call(
+    shared, pred, pre_act, normed, inverse = pl.pallas_call(
         functools.partial(forward_kernel, place=2 - EARLY),
         out_shape=outs,
-        in_specs=[SMEM] + [VMEM] * 7 + [HBM],
+        in_specs=[SMEM] + [VMEM] * 5 + [HBM],
         out_specs=[VMEM] * len(outs),
         scratch_shapes=[held(low), pltpu.VMEM((grid_rows, width), f32), dma],
         compiler_params=PARAMS,
         cost_estimate=some_cost,
     )(
-        flags, high, most_rows, (second, first)[EARLY // 2], node, out_turned, target_turned, weight, *in_hbm(low)
+        flags, high, most_rows, (second, first)[EARLY // 2], node, out_turned, *in_hbm(low)
     )
     cores = [[core + 2 * chip for chip in range(members // 2)] for core in range(2)]
     swap = [(member, member ^ 1) for member in range(members)]
     alike = lax.all_to_all(shared, "member", 0, 0, axis_index_groups=cores, tiled=True)
     unlike = lax.ppermute(alike, "member", swap)
-    (alike_sum,) = pl.pallas_call(
+    alike_sum, folded, lead, gate = pl.pallas_call(
         alike_kernel,
-        out_shape=[pltpu.VMEM((MAIN, LANES), f32)],
-        in_specs=[SMEM] + [VMEM] * 2,
-        out_specs=[VMEM],
+        out_shape=[
+            pltpu.VMEM((MAIN, LANES), f32),
+            pltpu.VMEM((MAIN, LANES), f32),
+            pltpu.VMEM((grid_rows, LANES), f32),
+            pltpu.VMEM((grid_rows, width), f32),
+        ],
+        in_specs=[SMEM] + [VMEM] * 5,
+        out_specs=[VMEM] * 4,
         scratch_shapes=[pltpu.VMEM((FOLDS, members // 2, LANES), f32)],
         compiler_params=PARAMS,
         cost_estimate=cost_of(10, 1),
-    )(flags, alike, folded)
+    )(flags, alike, pred, pre_act, target_turned, weight)
 
     pair_scale = (1.0 - (1.0 - ALPHA) / members) / (members - 1)
     outs = [
@@ -493,33 +511,34 @@
     got = lax.ppermute(give, "member", swap)
     first_back = to_neighbours(first_part, 0)
     second_back = to_neighbours(second_part, 1)
+    (own_part,) = pl.pallas_call(
+        own_kernel,
+        out_shape=[pltpu.VMEM((mesh_rows, width), f32)],
+        in_specs=[SMEM] + [VMEM] * 2 + [HBM],
+        out_specs=[VMEM],
+        scratch_shapes=[held(back_low), dma],
+        compiler_params=PARAMS,
+        cost_estimate=cost_of(130, 2),
+    )(flags, back_own, grad_send, *in_hbm(back_low))
     (blocks,) = pl.pallas_call(
         pair_add_kernel,
         out_shape=[pltpu.VMEM(give.shape, b16)],
-        in_specs=[VMEM] * 2,
+        in_specs=[VMEM] * 3,
         out_specs=[VMEM],
         compiler_params=PARAMS,
         cost_estimate=cost_of(1, 1),
-    )(keep, got)
+    )(keep, got, own_part)
     landed = lax.all_to_all(blocks, "member", 0, 0, axis_index_groups=cores, tiled=True)
     share = shape((width // members, grid_rows), b16)
     grad_latent, grid_share = pl.pallas_call(
         tail_kernel,
         out_shape=[pltpu.HBM((mesh_rows, width), b16), pltpu.HBM(share.shape, b16)],
-        in_specs=[SMEM] + [VMEM] * 5 + [HBM],
+        in_specs=[VMEM] * 4,
         out_specs=[HBM, HBM],
-        scratch_shapes=[
-            held(back_low),
-            pltpu.VMEM((mesh_rows, width), f32),
-            pltpu.VMEM((mesh_rows, width), b16),
-            held(share),
-            dma,
-            dma((4,)),
-            dma,
-        ],
-        compiler_params=PARAMS,
-        cost_estimate=cost_of(130, 3),
-    )(flags, back_own, grad_send, first_back, second_back, landed, *in_hbm(back_low))
+        scratch_shapes=[pltpu.VMEM((mesh_rows, width), b16), held(share), dma((4,)), dma],
+        compiler_params=PARAMS,
+        cost_estimate=cost_of(1, 3),
+    )(own_part, first_back, second_back, landed)
     return (grad_latent[None], grid_share.T)
 
 

time: 74.3 us -> 73.7 us (level)
  waiting for transfers between devices: 10.2 us -> 9.41 us
    pallas_call x1 -> x2, Pallas kernels: 0.36 us -> 1.15 us  [the longest x1 0.83 us: per_device(): pl.pallas_call(alike_kernel, out_shape=[pltpu.VMEM((MAIN, LANES), f32), p...]
  transfers between devices with their start and end apart: 6 -> 6, of which waited for: 4 -> 4; matrix products, arithmetic and copies ran while one was open for 0% -> 0% of each run, Pallas kernels for 5% -> 6%
where the time goes in v9:
time: 73.7 us; the launch traced here: 73.4 us
  starting transfers between devices  29.6 us (40%)
  blocking collectives  24.8 us (34%)
  waiting for transfers between devices  9.41 us (13%)
  Pallas kernels  8.8 us (12%)
  between operations  0.74 us (1%)
    ppermute x4, starting transfers between devices, to_neighbours(): return lax.ppermute(value, ('member', 'grid'), pairs)  22 us
    all_to_all x1, blocking collectives, per_device(): lax.all_to_all(shared, 'member', 0, 0, axis_index_groups=cores, tiled=True)  14.8 us
    all_to_all x1, blocking collectives, per_device(): lax.all_to_all(blocks, 'member', 0, 0, axis_index_groups=cores, tiled=True)  9.99 us
    ppermute x4, waiting for transfers between devices, to_neighbours(): return lax.ppermute(value, ('member', 'grid'), pairs)  8.06 us
    ppermute x1, starting transfers between devices, per_device(): unlike = lax.ppermute(alike, 'member', swap)  4.52 us
    ppermute x1, starting transfers between devices, per_device(): got = lax.ppermute(give, 'member', swap)  3.1 us
    pallas_call x1, Pallas kernels, per_device(): pl.pallas_call(edges_kernel, out_shape=outs, in_specs=[HBM] * len(ins), o...  2.86 us
    pallas_call x1, Pallas kernels, per_device(): pl.pallas_call(functools.partial(backward_kernel, pair_scale=pair_scale),...  1.84 us
  transfers between devices with their start and end apart: 6, of which 4 were waited for; matrix products, arithmetic and copies ran while one was open for 0% of the time, Pallas kernels for 6%

profile of v9, /device:TPU:1, one launch (start us, length us, event | category | flops | bytes accessed | tf_op | source)
XLA Modules:
  0.0 73.4 jit_solution(12843388778737367618)
XLA Ops:
  0.6 4.4 %collective-permute-start = (bf16[256,1024]{1,0:T(8,128)(2,1)}, bf16[256,1024]{1,0:T(8,128)(2,1)S(1)}, u32[]{:S(2)}, u32[]{:S(2)}) collective-permute-start(bf16[256,1024]{1,0:T(8,128)(2,1)} %bitcast.8), channel_id=1, source_target_pairs={{0,31},{1,0},{2,1},{3,2},{4,3},{5,4},{6,5},{7,6},{8,7},{9,8},{10,9... | collective-permute-start | bytes 1572872 | tf_op jit(solution)/shard_map/ppermute | solution.py:34
  5.0 10.5 %collective-permute-start.1 = (bf16[256,1024]{1,0:T(8,128)(2,1)}, bf16[256,1024]{1,0:T(8,128)(2,1)S(1)}, u32[]{:S(2)}, u32[]{:S(2)}) collective-permute-start(bf16[256,1024]{1,0:T(8,128)(2,1)} %bitcast.9), channel_id=1, source_target_pairs={{0,1},{1,2},{2,3},{3,4},{4,5},{5,6},{6,7},{7,8},{8,9},{9,10},{10,1... | collective-permute-start | bytes 1572872 | tf_op jit(solution)/shard_map/ppermute | solution.py:34
  15.5 2.9 %shard_map.113 = (s32[2]{0:T(128)S(4)}, bf16[256,768]{1,0:T(8,128)(2,1)}, bf16[256,768]{1,0:T(8,128)(2,1)}, bf16[256,768]{1,0:T(8,128)(2,1)S(1)}, bf16[256,512]{...) custom-call(s32[1]{0:T(128)} %bitcast.me_hbm, ...), custom_call_target="tpu_custom_call" | custom-call | flops 524288000 | bytes 8388608 | tf_op jit(solution)/shard_map/pallas_call | solution.py:425
  18.4 2.0 %collective-permute-done.rows_ref = bf16[256,1024]{1,0:T(8,128)(2,1)S(1)} collective-permute-done((bf16[256,1024]{1,0:T(8,128)(2,1)}, bf16[256,1024]{1,0:T(8,128)(2,1)S(1)}, u32[]{:S(2)}, u32[]{:S(2)}) %collective-permute-start) | collective-permute-done | bytes 524320 | tf_op jit(solution)/shard_map/ppermute | solution.py:34
  20.4 0.3 shard_map.114.base_ref
  20.7 6.1 %collective-permute-done.1.rows_ref = bf16[256,1024]{1,0:T(8,128)(2,1)S(1)} collective-permute-done((bf16[256,1024]{1,0:T(8,128)(2,1)}, bf16[256,1024]{1,0:T(8,128)(2,1)S(1)}, u32[]{:S(2)}, u32[]{:S(2)}) %collective-permute-start.1) | collective-permute-done | bytes 524320 | tf_op jit(solution)/shard_map/ppermute | solution.py:34
  26.8 1.7 %shard_map.115 = (s16[8,208,128]{2,1,0:T(8,128)(2,1)S(1)}, f32[256,128]{1,0:T(8,128)S(1)}, f32[256,1024]{1,0:T(8,128)S(1)}, f32[256,1024]{1,0:T(8,128)S(1)}, f32[256,1]{1,0:T(8,128)S(1)}) custom-call(s32[2]{0:T(128)S(4)} %get-tuple-element.31.flags_ref, bf16[256,768]{1,0:T(8,128)(2,1)S(1)} %get-tuple-element.33.high_ref, ...), custom_call_target="tpu_custom_call" | custom-call | flops 1048576000 | bytes 8388608 | tf_op jit(solution)/shard_map/pallas_call | solution.py:455
  28.4 14.8 %all_to_all.10.alike_ref = s16[8,208,128]{2,1,0:T(8,128)(2,1)S(1)} all-to-all(s16[8,208,128]{2,1,0:T(8,128)(2,1)S(1)} %get-tuple-element.38), channel_id=1, replica_groups={{0,64,128,192,256,320,384,448},{32,96,160,224,288,352,416,480},{1,65,12..., dimensions={0} | all-to-all | bytes 851968 | tf_op jit(solution)/shard_map/all_to_all | solution.py:468
  43.2 4.5 %collective-permute-start.2 = (s16[8,208,128]{2,1,0:T(8,128)(2,1)S(1)}, s16[8,208,128]{2,1,0:T(8,128)(2,1)S(1)}, u32[]{:S(2)}, u32[]{:S(2)}) collective-permute-start(s16[8,208,128]{2,1,0:T(8,128)(2,1)S(1)} %all_to_all.10.alike_ref), channel_id=1, source_target_pairs={{0,32},{32,0},{64,96},{96,64},{128,160},{160,128},{192,224},{224,1... | collective-permute-start | bytes 1277960 | tf_op jit(solution)/shard_map/ppermute | solution.py:469
  47.8 0.8 %shard_map.116 = (f32[208,128]{1,0:T(8,128)S(1)}, f32[208,128]{1,0:T(8,128)S(1)}, f32[256,128]{1,0:T(8,128)S(1)}, f32[256,1024]{1,0:T(8,128)S(1)}) custom-call(s32[2]{0:T(128)S(4)} %get-tuple-element.31.flags_ref, s16[8,208,128]{2,1,0:T(8,128)(2,1)S(1)} %all_to_all.10.alike_ref, f32[256,128]{1,0:T(8,128)S(1)} %get-tuple-element.39.pred_ref, ...), custom_call_target="tpu_custom_call" | custom-call | flops 10485760 | bytes 1048576 | tf_op jit(solution)/shard_map/pallas_call | solution.py:470
  48.6 0.5 collective-permute-done.2.unlike_ref
  49.1 1.8 %shard_map.117 = (f32[8,128,128]{2,1,0:T(8,128)S(1)}, bf16[8,128,128]{2,1,0:T(8,128)(2,1)S(1)}, bf16[256,1024]{1,0:T(8,128)(2,1)S(1)}, bf16[256,1024]{1,0:T(8,128)(2,1)S(1)}, bf16[256,1024]{1,0:T(8,128)(2,1)S(1)}) custom-call(s32[2]{0:T(128)S(4)} %get-tuple-element.31.flags_ref, f32[208,128]{1,0:T(8,128)S(1)} %get-tuple-element.43.alike_sum_ref, ...), custom_call_target="tpu_custom_call" | custom-call | flops 1048576000 | bytes 8388608 | tf_op jit(solution)/shard_map/pallas_call | solution.py:493
  51.0 5.2 %collective-permute-start.3 = (bf16[256,1024]{1,0:T(8,128)(2,1)S(1)}, bf16[256,1024]{1,0:T(8,128)(2,1)S(1)}, u32[]{:S(2)}, u32[]{:S(2)}) collective-permute-start(bf16[256,1024]{1,0:T(8,128)(2,1)S(1)} %get-tuple-element.54), channel_id=1, source_target_pairs={{0,1},{1,2},{2,3},{3,4},{4,5},{5,6},{6,7},{7,8},{8,9},{9,10},{10,1... | collective-permute-start | bytes 1572872 | tf_op jit(solution)/shard_map/ppermute | solution.py:34
  56.2 1.9 %collective-permute-start.4 = (bf16[256,1024]{1,0:T(8,128)(2,1)S(1)}, bf16[256,1024]{1,0:T(8,128)(2,1)S(1)}, u32[]{:S(2)}, u32[]{:S(2)}) collective-permute-start(bf16[256,1024]{1,0:T(8,128)(2,1)S(1)} %get-tuple-element.55), channel_id=1, source_target_pairs={{0,31},{1,0},{2,1},{3,2},{4,3},{5,4},{6,5},{7,6},{8,7},{9,8},{10,9... | collective-permute-start | bytes 1572872 | tf_op jit(solution)/shard_map/ppermute | solution.py:34
  58.1 3.1 %collective-permute-start.5 = (bf16[8,128,128]{2,1,0:T(8,128)(2,1)S(1)}, bf16[8,128,128]{2,1,0:T(8,128)(2,1)S(1)}, u32[]{:S(2)}, u32[]{:S(2)}) collective-permute-start(bf16[8,128,128]{2,1,0:T(8,128)(2,1)S(1)} %get-tuple-element.57), channel_id=1, source_target_pairs={{0,32},{32,0},{64,96},{96,64},{128,160},{160,128},{192,224},{224,1... | collective-permute-start | bytes 786440 | tf_op jit(solution)/shard_map/ppermute | solution.py:511
  61.2 0.3 shard_map.118.after_ref.own_ref
  61.6 0.8 %collective-permute-done.5.got_ref = bf16[8,128,128]{2,1,0:T(8,128)(2,1)S(1)} collective-permute-done((bf16[8,128,128]{2,1,0:T(8,128)(2,1)S(1)}, bf16[8,128,128]{2,1,0:T(8,128)(2,1)S(1)}, u32[]{:S(2)}, u32[]{:S(2)}) %collective-permute-start.5) | collective-permute-done | bytes 262176 | tf_op jit(solution)/shard_map/ppermute | solution.py:511
  62.4 10.0 %all_to_all.11.landed_ref = bf16[8,128,128]{2,1,0:T(8,128)(2,1)S(1)} all-to-all(bf16[8,128,128]{2,1,0:T(8,128)(2,1)S(1)} %shard_map.119), channel_id=1, replica_groups={{0,64,128,192,256,320,384,448},{32,96,160,224,288,352,416,480},{1,65,12..., dimensions={0} | all-to-all | bytes 524288 | tf_op jit(solution)/shard_map/all_to_all | solution.py:531
  72.4 0.0 collective-permute-done.3.first_ref
  72.4 0.0 collective-permute-done.4.second_ref
  72.4 0.9 %shard_map.120 = (bf16[256,1024]{1,0:T(8,128)(2,1)}, bf16[64,256]{1,0:T(8,128)(2,1)}) custom-call(f32[256,1024]{1,0:T(8,128)S(1)} %shard_map.118.after_ref.own_ref, bf16[256,1024]{1,0:T(8,128)(2,1)S(1)} %collective-permute-done.3.first_ref, bf16[256,1024]{1,0:T(8,128)(2,1)S(1)} %collective-permute-done.4.second_ref, ...), custom_call_target="tpu_custom_call" | custom-call | flops 1048576 | bytes 3145728 | tf_op jit(solution)/shard_map/pallas_call | solution.py:533
  (1 shorter events, 0.0 us)
Async XLA Ops:
  0.6 19.7 %collective-permute-start = (bf16[256,1024]{1,0:T(8,128)(2,1)}, bf16[256,1024]{1,0:T(8,128)(2,1)S(1)}, u32[]{:S(2)}, u32[]{:S(2)}) collective-permute-start(bf16[256,1024]{1,0:T(8,128)(2,1)} %bitcast.8), channel_id=1, source_target_pairs={{0,31},{1,0},{2,1},{3,2},{4,3},{5,4},{6,5},{7,6},{8,7},{9,8},{10,9... | collective-permute-start | bytes 1572872 | tf_op jit(solution)/shard_map/ppermute | solution.py:34
  5.0 21.8 %collective-permute-start.1 = (bf16[256,1024]{1,0:T(8,128)(2,1)}, bf16[256,1024]{1,0:T(8,128)(2,1)S(1)}, u32[]{:S(2)}, u32[]{:S(2)}) collective-permute-start(bf16[256,1024]{1,0:T(8,128)(2,1)} %bitcast.9), channel_id=1, source_target_pairs={{0,1},{1,2},{2,3},{3,4},{4,5},{5,6},{6,7},{7,8},{8,9},{9,10},{10,1... | collective-permute-start | bytes 1572872 | tf_op jit(solution)/shard_map/ppermute | solution.py:34
  43.2 5.9 %collective-permute-start.2 = (s16[8,208,128]{2,1,0:T(8,128)(2,1)S(1)}, s16[8,208,128]{2,1,0:T(8,128)(2,1)S(1)}, u32[]{:S(2)}, u32[]{:S(2)}) collective-permute-start(s16[8,208,128]{2,1,0:T(8,128)(2,1)S(1)} %all_to_all.10.alike_ref), channel_id=1, source_target_pairs={{0,32},{32,0},{64,96},{96,64},{128,160},{160,128},{192,224},{224,1... | collective-permute-start | bytes 1277960 | tf_op jit(solution)/shard_map/ppermute | solution.py:469
  51.0 21.4 %collective-permute-start.3 = (bf16[256,1024]{1,0:T(8,128)(2,1)S(1)}, bf16[256,1024]{1,0:T(8,128)(2,1)S(1)}, u32[]{:S(2)}, u32[]{:S(2)}) collective-permute-start(bf16[256,1024]{1,0:T(8,128)(2,1)S(1)} %get-tuple-element.54), channel_id=1, source_target_pairs={{0,1},{1,2},{2,3},{3,4},{4,5},{5,6},{6,7},{7,8},{8,9},{9,10},{10,1... | collective-permute-start | bytes 1572872 | tf_op jit(solution)/shard_map/ppermute | solution.py:34
  56.2 16.2 %collective-permute-start.4 = (bf16[256,1024]{1,0:T(8,128)(2,1)S(1)}, bf16[256,1024]{1,0:T(8,128)(2,1)S(1)}, u32[]{:S(2)}, u32[]{:S(2)}) collective-permute-start(bf16[256,1024]{1,0:T(8,128)(2,1)S(1)} %get-tuple-element.55), channel_id=1, source_target_pairs={{0,31},{1,0},{2,1},{3,2},{4,3},{5,4},{6,5},{7,6},{8,7},{9,8},{10,9... | collective-permute-start | bytes 1572872 | tf_op jit(solution)/shard_map/ppermute | solution.py:34
  58.1 4.2 %collective-permute-start.5 = (bf16[8,128,128]{2,1,0:T(8,128)(2,1)S(1)}, bf16[8,128,128]{2,1,0:T(8,128)(2,1)S(1)}, u32[]{:S(2)}, u32[]{:S(2)}) collective-permute-start(bf16[8,128,128]{2,1,0:T(8,128)(2,1)S(1)} %get-tuple-element.57), channel_id=1, source_target_pairs={{0,32},{32,0},{64,96},{96,64},{128,160},{160,128},{192,224},{224,1... | collective-permute-start | bytes 786440 | tf_op jit(solution)/shard_map/ppermute | solution.py:511

commit v10 on v9

--- a/solution.py
+++ b/solution.py
@@ -208,60 +208,55 @@
 
 
 def pair_parts(ref, others, fold_ref, scale_ref):
-    chips = ref.shape[0]
+    cores, chips = ref.shape[:2]
     rest_rows = (MAIN - TAIL) // FOLDS
     first = FOLDS * rest_rows
     lane = lax.broadcasted_iota(jnp.int32, (chips, LANES), 1)
-    tails = ref[:, first:MAIN, :].astype(jnp.float32)
-    code = jnp.zeros((chips, LANES), jnp.float32)
-    for k in range(FOLDS):
-        piece = turn(tails[:, k, :], FOLD * k - VARS)
-        code = jnp.where((lane >= FOLD * k) & (lane < FOLD * (k + 1)), piece, code)
-    scale = jnp.exp2(code * (1.0 / CODE)) * (1.0 / STEPS)
-    for k in range(FOLDS):
-        scale_ref[k] = jnp.where(lane < VARS, scale, turn(scale, VARS - FOLD * k))
+    for core in range(cores):
+        tails = ref[core, :, first:MAIN, :].astype(jnp.float32)
+        code = jnp.zeros((chips, LANES), jnp.float32)
+        for k in range(FOLDS):
+            piece = turn(tails[:, k, :], FOLD * k - VARS)
+            code = jnp.where((lane >= FOLD * k) & (lane < FOLD * (k + 1)), piece, code)
+        scale = jnp.exp2(code * (1.0 / CODE)) * (1.0 / STEPS)
+        for k in range(FOLDS):
+            scale_ref[core, k] = jnp.where(lane < VARS, scale, turn(scale, VARS - FOLD * k))
 
     bounds = [(k * rest_rows, (k + 1) * rest_rows) for k in range(FOLDS)] + [(first, MAIN)]
     parts = [jnp.zeros((high - low, LANES), jnp.float32) for low, high in bounds]
-    for other in others:
+    for core, chip in others:
         for i, (low, high) in enumerate(bounds):
-            factor = scale_ref[min(i, FOLDS - 1), pl.ds(other, 1), :]
-            theirs = ref[other, low:high, :].astype(jnp.float32) * factor
+            factor = scale_ref[core, min(i, FOLDS - 1), pl.ds(chip, 1), :]
+            theirs = ref[core, chip, low:high, :].astype(jnp.float32) * factor
             parts[i] = parts[i] + smooth_slope(fold_ref[low:high, :] - theirs)
     return parts
 
 
-def alike_kernel(
-    flags_ref, alike_ref, pred_ref, pre_ref, target_ref, weight_ref,
-    out_ref, fold_ref, lead_ref, gate_ref, scale_ref
-):
-    pred = pred_ref[...]
-    fold_ref[...] = fold(pred)
-    lead_ref[...] = weight_ref[...] * smooth_slope(pred - target_ref[...])
-    chips = alike_ref.shape[0]
-    others = [lax.rem(flags_ref[1] // 2 + step, chips) for step in range(1, chips)]
-    out_ref[...] = jnp.concatenate(pair_parts(alike_ref, others, fold_ref, scale_ref), axis=0)
-    pre_act = pre_ref[...]
-    gate_sig = 0.5 + 0.5 * jnp.tanh(0.5 * pre_act)
-    gate_ref[...] = gate_sig * (1.0 + pre_act * (1.0 - gate_sig))
-
-
 def backward_kernel(
-    flags_ref, alike_sum_ref, unlike_ref, fold_ref, lead_ref, weight_ref, gate_ref,
-    pad_ref, turned_ref, normed_ref, inverse_ref, high_ref, low_hbm,
-    keep_ref, give_ref, first_ref, second_ref, send_ref,
-    low_ref, scale_ref, pre_ref, grad_ref, low_sem, *, pair_scale
+    flags_ref, everyone_ref, pred_ref, target_ref, weight_ref, pre_act_ref,
+    pad_ref, turned_ref, normed_ref, inverse_ref, high_ref, own_ref, low_hbm,
+    keep_ref, give_ref, first_ref, second_ref, own_out_ref,
+    low_ref, scale_ref, fold_ref, pre_ref, grad_ref, send_ref, low_sem, *, pair_scale
 ):
     grid_rows, width = normed_ref.shape
     me = flags_ref[1]
-    chips = unlike_ref.shape[0]
-    parts = pair_parts(unlike_ref, list(range(chips)), fold_ref, scale_ref)
-    pair_sum = unfold(jnp.concatenate(parts, axis=0) + alike_sum_ref[...], grid_rows)
+    chips = everyone_ref.shape[1]
+    pred = pred_ref[...]
+    fold_ref[...] = fold(pred)
+    lead = weight_ref[...] * smooth_slope(pred - target_ref[...])
+    core, chip = lax.rem(me, 2), me // 2
+    others = [(core, lax.rem(chip + step, chips)) for step in range(1, chips)]
+    others += [(1 - core, step) for step in range(chips)]
+    parts = pair_parts(everyone_ref, others, fold_ref, scale_ref)
+    pair_sum = unfold(jnp.concatenate(parts, axis=0), grid_rows)
     real = lanes_of(pair_sum) < VARS
-    grad_pred = lead_ref[...] - pair_scale * weight_ref[...] * jnp.where(real, pair_sum, 0.0)
+    grad_pred = lead - pair_scale * weight_ref[...] * jnp.where(real, pair_sum, 0.0)
     grad_pred_b = grad_pred.astype(jnp.bfloat16)
     for at in blocks_of(width):
-        pre_ref[:, at] = (dot(grad_pred_b, pad_ref[:, at]) * gate_ref[:, at]).astype(jnp.bfloat16)
+        pre_act = pre_act_ref[:, at]
+        gate_sig = 0.5 + 0.5 * jnp.tanh(0.5 * pre_act)
+        gate = gate_sig * (1.0 + pre_act * (1.0 - gate_sig))
+        pre_ref[:, at] = (dot(grad_pred_b, pad_ref[:, at]) * gate).astype(jnp.bfloat16)
     plain = jnp.zeros((grid_rows, LANES), jnp.float32)
     along = jnp.zeros((grid_rows, LANES), jnp.float32)
     for at in blocks_of(width):
@@ -296,6 +291,7 @@
         for ref, side in sides:
             counts = high_ref[:, side * grid_rows : (side + 1) * grid_rows]
             ref[:, block] = dot(counts, summed_b).astype(jnp.bfloat16)
+        own_out_ref[:, block] = dot(own_ref[...], summed_b)
 
     @pl.when(flags_ref[0] > 0)
     def _():
@@ -307,22 +303,12 @@
             low_at = slice(2 * side * grid_rows, (2 * side + 1) * grid_rows)
             total = dot(high_ref[:, at], send_ref[...]) + dot(low_ref[:, low_at], send_ref[...])
             ref[...] = total.astype(jnp.bfloat16)
-
-
-def pair_add_kernel(keep_ref, got_ref, after_ref, out_ref):
-    out_ref[...] = (keep_ref[...] + got_ref[...].astype(jnp.float32)).astype(jnp.bfloat16)
-
-
-def own_kernel(flags_ref, own_ref, send_ref, low_hbm, out_ref, low_ref, low_sem):
-    rows = send_ref.shape[0]
-    out_ref[...] = dot(own_ref[...], send_ref[...])
-
-    @pl.when(flags_ref[0] > 0)
-    def _():
-        copy = pltpu.make_async_copy(low_hbm, low_ref, low_sem)
-        copy.start()
-        copy.wait()
-        out_ref[...] += dot(low_ref[:, rows : 2 * rows], send_ref[...])
+        own_out_ref[...] += dot(low_ref[:, grid_rows : 2 * grid_rows], send_ref[...])
+
+
+def pair_add_kernel(flags_ref, keep_ref, given_ref, out_ref):
+    other = 1 - lax.rem(flags_ref[1], 2)
+    out_ref[...] = (keep_ref[...] + given_ref[other].astype(jnp.float32)).astype(jnp.bfloat16)
 
 
 def tail_kernel(
@@ -464,70 +450,48 @@
         flags, high, most_rows, (second, first)[EARLY // 2], node, out_turned, *in_hbm(low)
     )
     cores = [[core + 2 * chip for chip in range(members // 2)] for core in range(2)]
-    swap = [(member, member ^ 1) for member in range(members)]
+    pairs = [[2 * chip, 2 * chip + 1] for chip in range(members // 2)]
     alike = lax.all_to_all(shared, "member", 0, 0, axis_index_groups=cores, tiled=True)
-    unlike = lax.ppermute(alike, "member", swap)
-    alike_sum, folded, lead, gate = pl.pallas_call(
-        alike_kernel,
-        out_shape=[
-            pltpu.VMEM((MAIN, LANES), f32),
-            pltpu.VMEM((MAIN, LANES), f32),
-            pltpu.VMEM((grid_rows, LANES), f32),
-            pltpu.VMEM((grid_rows, width), f32),
-        ],
-        in_specs=[SMEM] + [VMEM] * 5,
-        out_specs=[VMEM] * 4,
-        scratch_shapes=[pltpu.VMEM((FOLDS, members // 2, LANES), f32)],
-        compiler_params=PARAMS,
-        cost_estimate=cost_of(10, 1),
-    )(flags, alike, pred, pre_act, target_turned, weight)
-
+    everyone = lax.all_gather(alike, "member", axis=0, axis_index_groups=pairs, tiled=False)
     pair_scale = (1.0 - (1.0 - ALPHA) / members) / (members - 1)
     outs = [
         pltpu.VMEM((members // 2, grid_rows // 2, LANES), f32),
         pltpu.VMEM((members // 2, grid_rows // 2, LANES), b16),
         pltpu.VMEM((mesh_rows, width), b16),
         pltpu.VMEM((mesh_rows, width), b16),
-        pltpu.VMEM((grid_rows, width), b16),
+        pltpu.VMEM((mesh_rows, width), f32),
     ]
-    keep, give, first_part, second_part, grad_send = pl.pallas_call(
+    keep, give, first_part, second_part, own_part = pl.pallas_call(
         functools.partial(backward_kernel, pair_scale=pair_scale),
         out_shape=outs,
         in_specs=[SMEM] + [VMEM] * 11 + [HBM],
         out_specs=[VMEM] * 5,
         scratch_shapes=[
             held(back_low),
-            pltpu.VMEM((FOLDS, members // 2, LANES), f32),
+            pltpu.VMEM((2, FOLDS, members // 2, LANES), f32),
+            pltpu.VMEM((MAIN, LANES), f32),
             pltpu.VMEM((grid_rows, width), b16),
             pltpu.VMEM((grid_rows, width), f32),
+            pltpu.VMEM((grid_rows, width), b16),
             dma,
         ],
         compiler_params=PARAMS,
         cost_estimate=cost_of(1000, 8),
     )(
-        flags, alike_sum, unlike, folded, lead, weight, gate, out_pad, node_turned, normed, inverse, back,
+        flags, everyone, pred, target_turned, weight, pre_act, out_pad, node_turned, normed, inverse, back, back_own,
         *in_hbm(back_low),
     )
-    got = lax.ppermute(give, "member", swap)
+    given = lax.all_gather(give, "member", axis=0, axis_index_groups=pairs, tiled=False)
     first_back = to_neighbours(first_part, 0)
     second_back = to_neighbours(second_part, 1)
-    (own_part,) = pl.pallas_call(
-        own_kernel,
-        out_shape=[pltpu.VMEM((mesh_rows, width), f32)],
-        in_specs=[SMEM] + [VMEM] * 2 + [HBM],
-        out_specs=[VMEM],
-        scratch_shapes=[held(back_low), dma],
-        compiler_params=PARAMS,
-        cost_estimate=cost_of(130, 2),
-    )(flags, back_own, grad_send, *in_hbm(back_low))
     (blocks,) = pl.pallas_call(
         pair_add_kernel,
         out_shape=[pltpu.VMEM(give.shape, b16)],
-        in_specs=[VMEM] * 3,
+        in_specs=[SMEM] + [VMEM] * 2,
         out_specs=[VMEM],
         compiler_params=PARAMS,
         cost_estimate=cost_of(1, 1),
-    )(keep, got, own_part)
+    )(flags, keep, given)
     landed = lax.all_to_all(blocks, "member", 0, 0, axis_index_groups=cores, tiled=True)
     share = shape((width // members, grid_rows), b16)
     grad_latent, grid_share = pl.pallas_call(

time: 73.7 us -> 71.9 us (0.976)
  blocking collectives: 24.8 us -> 32.5 us
  starting transfers between devices: 29.6 us -> 22 us
  waiting for transfers between devices: 9.41 us -> 8.16 us
    all_gather x0 -> x2, blocking collectives: none -> 7.65 us  [the longest x1 4.65 us: per_device(): lax.all_gather(alike, 'member', axis=0, axis_index_groups=pairs, tiled=Fa...]
    ppermute x2 -> x0, starting transfers between devices: 7.62 us -> none  [the longest x1 4.52 us: per_device(): unlike = lax.ppermute(alike, 'member', swap)]
    ppermute x2 -> x0, waiting for transfers between devices: 1.35 us -> none  [the longest x1 0.82 us: per_device(): got = lax.ppermute(give, 'member', swap)]
    pallas_call x2 -> x0, Pallas kernels: 1.15 us -> none  [the longest x1 0.83 us: per_device(): pl.pallas_call(alike_kernel, out_shape=[pltpu.VMEM((MAIN, LANES), f32), p...]
  transfers between devices with their start and end apart: 6 -> 4, of which waited for: 4 -> 3; matrix products, arithmetic and copies ran while one was open for 0% -> 0% of each run, Pallas kernels for 6% -> 4%
where the time goes in v10:
time: 71.9 us; the launch traced here: 71.6 us
  blocking collectives  32.5 us (45%)
  starting transfers between devices  22 us (31%)
  Pallas kernels  8.24 us (11%)
  waiting for transfers between devices  8.16 us (11%)
    ppermute x4, starting transfers between devices, to_neighbours(): return lax.ppermute(value, ('member', 'grid'), pairs)  22 us
    all_to_all x1, blocking collectives, per_device(): lax.all_to_all(shared, 'member', 0, 0, axis_index_groups=cores, tiled=True)  14.8 us
    all_to_all x1, blocking collectives, per_device(): lax.all_to_all(blocks, 'member', 0, 0, axis_index_groups=cores, tiled=True)  10 us
    ppermute x4, waiting for transfers between devices, to_neighbours(): return lax.ppermute(value, ('member', 'grid'), pairs)  8.16 us
    all_gather x1, blocking collectives, per_device(): lax.all_gather(alike, 'member', axis=0, axis_index_groups=pairs, tiled=Fa...  4.65 us
    all_gather x1, blocking collectives, per_device(): lax.all_gather(give, 'member', axis=0, axis_index_groups=pairs, tiled=False)  3 us
    pallas_call x1, Pallas kernels, per_device(): pl.pallas_call(edges_kernel, out_shape=outs, in_specs=[HBM] * len(ins), o...  2.86 us
    pallas_call x1, Pallas kernels, per_device(): pl.pallas_call(functools.partial(backward_kernel, pair_scale=pair_scale),...  2.42 us
  transfers between devices with their start and end apart: 4, of which 3 were waited for; matrix products, arithmetic and copies ran while one was open for 0% of the time, Pallas kernels for 4%

profile of v10, /device:TPU:1, one launch (start us, length us, event | category | flops | bytes accessed | tf_op | source)
XLA Modules:
  0.0 71.6 jit_solution(11150229934542513137)
XLA Ops:
  0.6 4.4 %collective-permute-start = (bf16[256,1024]{1,0:T(8,128)(2,1)}, bf16[256,1024]{1,0:T(8,128)(2,1)S(1)}, u32[]{:S(2)}, u32[]{:S(2)}) collective-permute-start(bf16[256,1024]{1,0:T(8,128)(2,1)} %bitcast.12), channel_id=1, source_target_pairs={{0,31},{1,0},{2,1},{3,2},{4,3},{5,4},{6,5},{7,6},{8,7},{9,8},{10,9... | collective-permute-start | bytes 1572872 | tf_op jit(solution)/shard_map/ppermute | solution.py:34
  5.0 10.5 %collective-permute-start.1 = (bf16[256,1024]{1,0:T(8,128)(2,1)}, bf16[256,1024]{1,0:T(8,128)(2,1)S(1)}, u32[]{:S(2)}, u32[]{:S(2)}) collective-permute-start(bf16[256,1024]{1,0:T(8,128)(2,1)} %bitcast.13), channel_id=1, source_target_pairs={{0,1},{1,2},{2,3},{3,4},{4,5},{5,6},{6,7},{7,8},{8,9},{9,10},{10,1... | collective-permute-start | bytes 1572872 | tf_op jit(solution)/shard_map/ppermute | solution.py:34
  15.5 2.9 %shard_map.113 = (s32[2]{0:T(128)S(4)}, bf16[256,768]{1,0:T(8,128)(2,1)}, bf16[256,768]{1,0:T(8,128)(2,1)}, bf16[256,768]{1,0:T(8,128)(2,1)S(1)}, bf16[256,512]{...) custom-call(s32[1]{0:T(128)} %bitcast.me_hbm, ...), custom_call_target="tpu_custom_call" | custom-call | flops 524288000 | bytes 8388608 | tf_op jit(solution)/shard_map/pallas_call | solution.py:411
  18.4 2.0 %collective-permute-done.rows_ref = bf16[256,1024]{1,0:T(8,128)(2,1)S(1)} collective-permute-done((bf16[256,1024]{1,0:T(8,128)(2,1)}, bf16[256,1024]{1,0:T(8,128)(2,1)S(1)}, u32[]{:S(2)}, u32[]{:S(2)}) %collective-permute-start) | collective-permute-done | bytes 524320 | tf_op jit(solution)/shard_map/ppermute | solution.py:34
  20.4 0.3 shard_map.114.base_ref
  20.7 6.1 %collective-permute-done.1.rows_ref = bf16[256,1024]{1,0:T(8,128)(2,1)S(1)} collective-permute-done((bf16[256,1024]{1,0:T(8,128)(2,1)}, bf16[256,1024]{1,0:T(8,128)(2,1)S(1)}, u32[]{:S(2)}, u32[]{:S(2)}) %collective-permute-start.1) | collective-permute-done | bytes 524320 | tf_op jit(solution)/shard_map/ppermute | solution.py:34
  26.8 1.6 %shard_map.115 = (s16[8,208,128]{2,1,0:T(8,128)(2,1)S(1)}, f32[256,128]{1,0:T(8,128)S(1)}, f32[256,1024]{1,0:T(8,128)S(1)}, f32[256,1024]{1,0:T(8,128)S(1)}, f32[256,1]{1,0:T(8,128)S(1)}) custom-call(s32[2]{0:T(128)S(4)} %get-tuple-element.27.flags_ref, bf16[256,768]{1,0:T(8,128)(2,1)S(1)} %get-tuple-element.28.high_ref, ...), custom_call_target="tpu_custom_call" | custom-call | flops 1048576000 | bytes 8388608 | tf_op jit(solution)/shard_map/pallas_call | solution.py:441
  28.4 14.8 %all_to_all.10 = s16[8,208,128]{2,1,0:T(8,128)(2,1)S(1)} all-to-all(s16[8,208,128]{2,1,0:T(8,128)(2,1)S(1)} %get-tuple-element.33), channel_id=1, replica_groups={{0,64,128,192,256,320,384,448},{32,96,160,224,288,352,416,480},{1,65,12..., dimensions={0} | all-to-all | bytes 851968 | tf_op jit(solution)/shard_map/all_to_all | solution.py:454
  43.2 4.7 %all-gather = s16[16,208,128]{2,1,0:T(8,128)(2,1)S(1)} all-gather(s16[8,208,128]{2,1,0:T(8,128)(2,1)S(1)} %all_to_all.10), channel_id=2, replica_groups={{0,32},{64,96},{128,160},{192,224},{256,288},{320,352},{384,416},{448,4..., dimensions={0}, use_global_device_ids=true | all-gather | bytes 1277952 | tf_op jit(solution)/shard_map/all_gather | solution.py:455
  47.9 2.4 %shard_map.116 = (f32[8,128,128]{2,1,0:T(8,128)S(1)}, bf16[8,128,128]{2,1,0:T(8,128)(2,1)S(1)}, bf16[256,1024]{1,0:T(8,128)(2,1)S(1)}, bf16[256,1024]{1,0:T(8,128)(2,1)S(1)}, f32[256,1024]{1,0:T(8,128)S(1)}) custom-call(s32[2]{0:T(128)S(4)} %get-tuple-element.27.flags_ref, s16[2,8,208,128]{3,2,1,0:T(8,128)(2,1)S(1)} %bitcast.10, ...), custom_call_target="tpu_custom_call" | custom-call | flops 1048576000 | bytes 8388608 | tf_op jit(solution)/shard_map/pallas_call | solution.py:464
  50.3 5.2 %collective-permute-start.2 = (bf16[256,1024]{1,0:T(8,128)(2,1)S(1)}, bf16[256,1024]{1,0:T(8,128)(2,1)S(1)}, u32[]{:S(2)}, u32[]{:S(2)}) collective-permute-start(bf16[256,1024]{1,0:T(8,128)(2,1)S(1)} %get-tuple-element.46), channel_id=1, source_target_pairs={{0,1},{1,2},{2,3},{3,4},{4,5},{5,6},{6,7},{7,8},{8,9},{9,10},{10,1... | collective-permute-start | bytes 1572872 | tf_op jit(solution)/shard_map/ppermute | solution.py:34
  55.5 1.9 %collective-permute-start.3 = (bf16[256,1024]{1,0:T(8,128)(2,1)S(1)}, bf16[256,1024]{1,0:T(8,128)(2,1)S(1)}, u32[]{:S(2)}, u32[]{:S(2)}) collective-permute-start(bf16[256,1024]{1,0:T(8,128)(2,1)S(1)} %get-tuple-element.47), channel_id=1, source_target_pairs={{0,31},{1,0},{2,1},{3,2},{4,3},{5,4},{6,5},{7,6},{8,7},{9,8},{10,9... | collective-permute-start | bytes 1572872 | tf_op jit(solution)/shard_map/ppermute | solution.py:34
  57.5 3.0 %all-gather.1 = bf16[16,128,128]{2,1,0:T(8,128)(2,1)S(1)} all-gather(bf16[8,128,128]{2,1,0:T(8,128)(2,1)S(1)} %get-tuple-element.49), channel_id=3, replica_groups={{0,32},{64,96},{128,160},{192,224},{256,288},{320,352},{384,416},{448,4..., dimensions={0}, use_global_device_ids=true | all-gather | bytes 786432 | tf_op jit(solution)/shard_map/all_gather | solution.py:484
  60.5 10.0 %all_to_all.11.landed_ref = bf16[8,128,128]{2,1,0:T(8,128)(2,1)S(1)} all-to-all(bf16[8,128,128]{2,1,0:T(8,128)(2,1)S(1)} %shard_map.117), channel_id=1, replica_groups={{0,64,128,192,256,320,384,448},{32,96,160,224,288,352,416,480},{1,65,12..., dimensions={0} | all-to-all | bytes 524288 | tf_op jit(solution)/shard_map/all_to_all | solution.py:495
  70.5 0.0 collective-permute-done.2.first_ref
  70.6 0.1 collective-permute-done.3.second_ref
  70.7 0.9 %shard_map.118 = (bf16[256,1024]{1,0:T(8,128)(2,1)}, bf16[64,256]{1,0:T(8,128)(2,1)}) custom-call(f32[256,1024]{1,0:T(8,128)S(1)} %get-tuple-element.45.own_ref, bf16[256,1024]{1,0:T(8,128)(2,1)S(1)} %collective-permute-done.2.first_ref, bf16[256,1024]{1,0:T(8,128)(2,1)S(1)} %collective-permute-done.3.second_ref, bf16[8,128,128]{2,1,0:T(8,128)(2,1)S(1)} %all_to_all.11.landed_ref), custom_call_target="tpu_custom_call" | custom-call | flops 1048576 | bytes 3145728 | tf_op jit(solution)/shard_map/pallas_call | solution.py:497
  (1 shorter events, 0.0 us)
Async XLA Ops:
  0.6 19.7 %collective-permute-start = (bf16[256,1024]{1,0:T(8,128)(2,1)}, bf16[256,1024]{1,0:T(8,128)(2,1)S(1)}, u32[]{:S(2)}, u32[]{:S(2)}) collective-permute-start(bf16[256,1024]{1,0:T(8,128)(2,1)} %bitcast.12), channel_id=1, source_target_pairs={{0,31},{1,0},{2,1},{3,2},{4,3},{5,4},{6,5},{7,6},{8,7},{9,8},{10,9... | collective-permute-start | bytes 1572872 | tf_op jit(solution)/shard_map/ppermute | solution.py:34
  5.0 21.8 %collective-permute-start.1 = (bf16[256,1024]{1,0:T(8,128)(2,1)}, bf16[256,1024]{1,0:T(8,128)(2,1)S(1)}, u32[]{:S(2)}, u32[]{:S(2)}) collective-permute-start(bf16[256,1024]{1,0:T(8,128)(2,1)} %bitcast.13), channel_id=1, source_target_pairs={{0,1},{1,2},{2,3},{3,4},{4,5},{5,6},{6,7},{7,8},{8,9},{9,10},{10,1... | collective-permute-start | bytes 1572872 | tf_op jit(solution)/shard_map/ppermute | solution.py:34
  50.3 20.2 %collective-permute-start.2 = (bf16[256,1024]{1,0:T(8,128)(2,1)S(1)}, bf16[256,1024]{1,0:T(8,128)(2,1)S(1)}, u32[]{:S(2)}, u32[]{:S(2)}) collective-permute-start(bf16[256,1024]{1,0:T(8,128)(2,1)S(1)} %get-tuple-element.46), channel_id=1, source_target_pairs={{0,1},{1,2},{2,3},{3,4},{4,5},{5,6},{6,7},{7,8},{8,9},{9,10},{10,1... | collective-permute-start | bytes 1572872 | tf_op jit(solution)/shard_map/ppermute | solution.py:34
  55.5 15.1 %collective-permute-start.3 = (bf16[256,1024]{1,0:T(8,128)(2,1)S(1)}, bf16[256,1024]{1,0:T(8,128)(2,1)S(1)}, u32[]{:S(2)}, u32[]{:S(2)}) collective-permute-start(bf16[256,1024]{1,0:T(8,128)(2,1)S(1)} %get-tuple-element.47), channel_id=1, source_target_pairs={{0,31},{1,0},{2,1},{3,2},{4,3},{5,4},{6,5},{7,6},{8,7},{9,8},{10,9... | collective-permute-start | bytes 1572872 | tf_op jit(solution)/shard_map/ppermute | solution.py:34

commit v11 on v10

--- a/solution.py
+++ b/solution.py
@@ -17,7 +17,7 @@
 FOLD = 25
 FOLDS = 4
 STEPS = 32767.0
-CODE = 256.0
+CODE = 1.0
 LOWEST = -20.0
 BLOCK = 256
 EARLY = 2
@@ -159,7 +159,7 @@
 
 def forward_kernel(
     flags_ref, high_ref, base_ref, rows_ref, node_ref, turned_ref, low_hbm,
-    shared_ref, pred_ref, pre_ref, normed_ref, inverse_ref,
+    shared_ref, pred_ref, sent_ref, pre_ref, normed_ref, inverse_ref,
     low_ref, sum_ref, low_sem, *, place
 ):
     gather_kernel(flags_ref, high_ref, base_ref, rows_ref, low_hbm, sum_ref, low_ref, low_sem, place=place)
@@ -177,6 +177,7 @@
     largest = jnp.max(jnp.abs(pred), axis=0, keepdims=True)
     code = jnp.ceil(jnp.log2(jnp.maximum(largest, 2.0**LOWEST)) * CODE)
     whole = jnp.round(pred * (jnp.exp2(code * (-1.0 / CODE)) * STEPS))
+    sent_ref[...] = whole * (jnp.exp2(code * (1.0 / CODE)) * (1.0 / STEPS))
     packed = fold(whole, code).astype(jnp.int16)
     for member in range(shared_ref.shape[0]):
         shared_ref[member] = packed
@@ -233,7 +234,7 @@
 
 
 def backward_kernel(
-    flags_ref, everyone_ref, pred_ref, target_ref, weight_ref, pre_act_ref,
+    flags_ref, everyone_ref, pred_ref, sent_ref, target_ref, weight_ref, pre_act_ref,
     pad_ref, turned_ref, normed_ref, inverse_ref, high_ref, own_ref, low_hbm,
     keep_ref, give_ref, first_ref, second_ref, own_out_ref,
     low_ref, scale_ref, fold_ref, pre_ref, grad_ref, send_ref, low_sem, *, pair_scale
@@ -242,7 +243,7 @@
     me = flags_ref[1]
     chips = everyone_ref.shape[1]
     pred = pred_ref[...]
-    fold_ref[...] = fold(pred)
+    fold_ref[...] = fold(sent_ref[...])
     lead = weight_ref[...] * smooth_slope(pred - target_ref[...])
     core, chip = lax.rem(me, 2), me // 2
     others = [(core, lax.rem(chip + step, chips)) for step in range(1, chips)]
@@ -434,11 +435,12 @@
     outs = [
         pltpu.VMEM((members // 2, MAIN, LANES), jnp.int16),
         pltpu.VMEM((grid_rows, LANES), f32),
+        pltpu.VMEM((grid_rows, LANES), f32),
         pltpu.VMEM((grid_rows, width), f32),
         pltpu.VMEM((grid_rows, width), f32),
         pltpu.VMEM((grid_rows, 1), f32),
     ]
-    shared, pred, pre_act, normed, inverse = pl.pallas_call(
+    shared, pred, sent, pre_act, normed, inverse = pl.pallas_call(
         functools.partial(forward_kernel, place=2 - EARLY),
         out_shape=outs,
         in_specs=[SMEM] + [VMEM] * 5 + [HBM],
@@ -464,7 +466,7 @@
     keep, give, first_part, second_part, own_part = pl.pallas_call(
         functools.partial(backward_kernel, pair_scale=pair_scale),
         out_shape=outs,
-        in_specs=[SMEM] + [VMEM] * 11 + [HBM],
+        in_specs=[SMEM] + [VMEM] * 12 + [HBM],
         out_specs=[VMEM] * 5,
         scratch_shapes=[
             held(back_low),
@@ -478,7 +480,7 @@
         compiler_params=PARAMS,
         cost_estimate=cost_of(1000, 8),
     )(
-        flags, everyone, pred, target_turned, weight, pre_act, out_pad, node_turned, normed, inverse, back, back_own,
+        flags, everyone, pred, sent, target_turned, weight, pre_act, out_pad, node_turned, normed, inverse, back, back_own,
         *in_hbm(back_low),
     )
     given = lax.all_gather(give, "member", axis=0, axis_index_groups=pairs, tiled=False)

time: 71.9 us -> 71.9 us (level)
  no operation moved by 1% of the time
where the time goes in v11:
time: 71.9 us; the launch traced here: 71.6 us
  blocking collectives  32.5 us (45%)
  starting transfers between devices  22 us (31%)
  Pallas kernels  8.25 us (11%)
  waiting for transfers between devices  8.16 us (11%)
    ppermute x4, starting transfers between devices, to_neighbours(): return lax.ppermute(value, ('member', 'grid'), pairs)  22 us
    all_to_all x1, blocking collectives, per_device(): lax.all_to_all(shared, 'member', 0, 0, axis_index_groups=cores, tiled=True)  14.8 us
    all_to_all x1, blocking collectives, per_device(): lax.all_to_all(blocks, 'member', 0, 0, axis_index_groups=cores, tiled=True)  10 us
    ppermute x4, waiting for transfers between devices, to_neighbours(): return lax.ppermute(value, ('member', 'grid'), pairs)  8.16 us
    all_gather x1, blocking collectives, per_device(): lax.all_gather(alike, 'member', axis=0, axis_index_groups=pairs, tiled=Fa...  4.65 us
    all_gather x1, blocking collectives, per_device(): lax.all_gather(give, 'member', axis=0, axis_index_groups=pairs, tiled=False)  3 us
    pallas_call x1, Pallas kernels, per_device(): pl.pallas_call(edges_kernel, out_shape=outs, in_specs=[HBM] * len(ins), o...  2.86 us
    pallas_call x1, Pallas kernels, per_device(): pl.pallas_call(functools.partial(backward_kernel, pair_scale=pair_scale),...  2.43 us
  transfers between devices with their start and end apart: 4, of which 3 were waited for; matrix products, arithmetic and copies ran while one was open for 0% of the time, Pallas kernels for 4%

profile of v11, /device:TPU:1, one launch (start us, length us, event | category | flops | bytes accessed | tf_op | source)
XLA Modules:
  0.0 71.6 jit_solution(2857475750593447925)
XLA Ops:
  0.6 4.4 %collective-permute-start = (bf16[256,1024]{1,0:T(8,128)(2,1)}, bf16[256,1024]{1,0:T(8,128)(2,1)S(1)}, u32[]{:S(2)}, u32[]{:S(2)}) collective-permute-start(bf16[256,1024]{1,0:T(8,128)(2,1)} %bitcast.12), channel_id=1, source_target_pairs={{0,31},{1,0},{2,1},{3,2},{4,3},{5,4},{6,5},{7,6},{8,7},{9,8},{10,9... | collective-permute-start | bytes 1572872 | tf_op jit(solution)/shard_map/ppermute | solution.py:34
  5.0 10.5 %collective-permute-start.1 = (bf16[256,1024]{1,0:T(8,128)(2,1)}, bf16[256,1024]{1,0:T(8,128)(2,1)S(1)}, u32[]{:S(2)}, u32[]{:S(2)}) collective-permute-start(bf16[256,1024]{1,0:T(8,128)(2,1)} %bitcast.13), channel_id=1, source_target_pairs={{0,1},{1,2},{2,3},{3,4},{4,5},{5,6},{6,7},{7,8},{8,9},{9,10},{10,1... | collective-permute-start | bytes 1572872 | tf_op jit(solution)/shard_map/ppermute | solution.py:34
  15.5 2.9 %shard_map.113 = (s32[2]{0:T(128)S(4)}, bf16[256,768]{1,0:T(8,128)(2,1)}, bf16[256,768]{1,0:T(8,128)(2,1)}, bf16[256,768]{1,0:T(8,128)(2,1)S(1)}, bf16[256,512]{...) custom-call(s32[1]{0:T(128)} %bitcast.me_hbm, ...), custom_call_target="tpu_custom_call" | custom-call | flops 524288000 | bytes 8388608 | tf_op jit(solution)/shard_map/pallas_call | solution.py:412
  18.4 2.0 %collective-permute-done.rows_ref = bf16[256,1024]{1,0:T(8,128)(2,1)S(1)} collective-permute-done((bf16[256,1024]{1,0:T(8,128)(2,1)}, bf16[256,1024]{1,0:T(8,128)(2,1)S(1)}, u32[]{:S(2)}, u32[]{:S(2)}) %collective-permute-start) | collective-permute-done | bytes 524320 | tf_op jit(solution)/shard_map/ppermute | solution.py:34
  20.4 0.3 shard_map.114.base_ref
  20.7 6.1 %collective-permute-done.1.rows_ref = bf16[256,1024]{1,0:T(8,128)(2,1)S(1)} collective-permute-done((bf16[256,1024]{1,0:T(8,128)(2,1)}, bf16[256,1024]{1,0:T(8,128)(2,1)S(1)}, u32[]{:S(2)}, u32[]{:S(2)}) %collective-permute-start.1) | collective-permute-done | bytes 524320 | tf_op jit(solution)/shard_map/ppermute | solution.py:34
  26.8 1.6 %shard_map.115 = (s16[8,208,128]{2,1,0:T(8,128)(2,1)S(1)}, f32[256,128]{1,0:T(8,128)S(1)}, f32[256,128]{1,0:T(8,128)S(1)}, f32[256,1024]{1,0:T(8,128)S(1)}, f32[...) custom-call(s32[2]{0:T(128)S(4)} %get-tuple-element.28.flags_ref, bf16[256,768]{1,0:T(8,128)(2,1)S(1)} %get-tuple-element.29.high_ref, ...), custom_call_target="tpu_custom_call" | custom-call | flops 1048576000 | bytes 8388608 | tf_op jit(solution)/shard_map/pallas_call | solution.py:443
  28.4 14.8 %all_to_all.10 = s16[8,208,128]{2,1,0:T(8,128)(2,1)S(1)} all-to-all(s16[8,208,128]{2,1,0:T(8,128)(2,1)S(1)} %get-tuple-element.34), channel_id=1, replica_groups={{0,64,128,192,256,320,384,448},{32,96,160,224,288,352,416,480},{1,65,12..., dimensions={0} | all-to-all | bytes 851968 | tf_op jit(solution)/shard_map/all_to_all | solution.py:456
  43.2 4.7 %all-gather = s16[16,208,128]{2,1,0:T(8,128)(2,1)S(1)} all-gather(s16[8,208,128]{2,1,0:T(8,128)(2,1)S(1)} %all_to_all.10), channel_id=2, replica_groups={{0,32},{64,96},{128,160},{192,224},{256,288},{320,352},{384,416},{448,4..., dimensions={0}, use_global_device_ids=true | all-gather | bytes 1277952 | tf_op jit(solution)/shard_map/all_gather | solution.py:457
  47.9 2.4 %shard_map.116 = (f32[8,128,128]{2,1,0:T(8,128)S(1)}, bf16[8,128,128]{2,1,0:T(8,128)(2,1)S(1)}, bf16[256,1024]{1,0:T(8,128)(2,1)S(1)}, bf16[256,1024]{1,0:T(8,128)(2,1)S(1)}, f32[256,1024]{1,0:T(8,128)S(1)}) custom-call(s32[2]{0:T(128)S(4)} %get-tuple-element.28.flags_ref, s16[2,8,208,128]{3,2,1,0:T(8,128)(2,1)S(1)} %bitcast.10, ...), custom_call_target="tpu_custom_call" | custom-call | flops 1048576000 | bytes 8388608 | tf_op jit(solution)/shard_map/pallas_call | solution.py:466
  50.3 5.2 %collective-permute-start.2 = (bf16[256,1024]{1,0:T(8,128)(2,1)S(1)}, bf16[256,1024]{1,0:T(8,128)(2,1)S(1)}, u32[]{:S(2)}, u32[]{:S(2)}) collective-permute-start(bf16[256,1024]{1,0:T(8,128)(2,1)S(1)} %get-tuple-element.48), channel_id=1, source_target_pairs={{0,1},{1,2},{2,3},{3,4},{4,5},{5,6},{6,7},{7,8},{8,9},{9,10},{10,1... | collective-permute-start | bytes 1572872 | tf_op jit(solution)/shard_map/ppermute | solution.py:34
  55.5 1.9 %collective-permute-start.3 = (bf16[256,1024]{1,0:T(8,128)(2,1)S(1)}, bf16[256,1024]{1,0:T(8,128)(2,1)S(1)}, u32[]{:S(2)}, u32[]{:S(2)}) collective-permute-start(bf16[256,1024]{1,0:T(8,128)(2,1)S(1)} %get-tuple-element.49), channel_id=1, source_target_pairs={{0,31},{1,0},{2,1},{3,2},{4,3},{5,4},{6,5},{7,6},{8,7},{9,8},{10,9... | collective-permute-start | bytes 1572872 | tf_op jit(solution)/shard_map/ppermute | solution.py:34
  57.5 3.0 %all-gather.1 = bf16[16,128,128]{2,1,0:T(8,128)(2,1)S(1)} all-gather(bf16[8,128,128]{2,1,0:T(8,128)(2,1)S(1)} %get-tuple-element.51), channel_id=3, replica_groups={{0,32},{64,96},{128,160},{192,224},{256,288},{320,352},{384,416},{448,4..., dimensions={0}, use_global_device_ids=true | all-gather | bytes 786432 | tf_op jit(solution)/shard_map/all_gather | solution.py:486
  60.5 10.0 %all_to_all.11.landed_ref = bf16[8,128,128]{2,1,0:T(8,128)(2,1)S(1)} all-to-all(bf16[8,128,128]{2,1,0:T(8,128)(2,1)S(1)} %shard_map.117), channel_id=1, replica_groups={{0,64,128,192,256,320,384,448},{32,96,160,224,288,352,416,480},{1,65,12..., dimensions={0} | all-to-all | bytes 524288 | tf_op jit(solution)/shard_map/all_to_all | solution.py:497
  70.6 0.0 collective-permute-done.2.first_ref
  70.6 0.1 collective-permute-done.3.second_ref
  70.7 0.9 %shard_map.118 = (bf16[256,1024]{1,0:T(8,128)(2,1)}, bf16[64,256]{1,0:T(8,128)(2,1)}) custom-call(f32[256,1024]{1,0:T(8,128)S(1)} %get-tuple-element.47.own_ref, bf16[256,1024]{1,0:T(8,128)(2,1)S(1)} %collective-permute-done.2.first_ref, bf16[256,1024]{1,0:T(8,128)(2,1)S(1)} %collective-permute-done.3.second_ref, bf16[8,128,128]{2,1,0:T(8,128)(2,1)S(1)} %all_to_all.11.landed_ref), custom_call_target="tpu_custom_call" | custom-call | flops 1048576 | bytes 3145728 | tf_op jit(solution)/shard_map/pallas_call | solution.py:499
  (1 shorter events, 0.0 us)
Async XLA Ops:
  0.6 19.7 %collective-permute-start = (bf16[256,1024]{1,0:T(8,128)(2,1)}, bf16[256,1024]{1,0:T(8,128)(2,1)S(1)}, u32[]{:S(2)}, u32[]{:S(2)}) collective-permute-start(bf16[256,1024]{1,0:T(8,128)(2,1)} %bitcast.12), channel_id=1, source_target_pairs={{0,31},{1,0},{2,1},{3,2},{4,3},{5,4},{6,5},{7,6},{8,7},{9,8},{10,9... | collective-permute-start | bytes 1572872 | tf_op jit(solution)/shard_map/ppermute | solution.py:34
  5.0 21.8 %collective-permute-start.1 = (bf16[256,1024]{1,0:T(8,128)(2,1)}, bf16[256,1024]{1,0:T(8,128)(2,1)S(1)}, u32[]{:S(2)}, u32[]{:S(2)}) collective-permute-start(bf16[256,1024]{1,0:T(8,128)(2,1)} %bitcast.13), channel_id=1, source_target_pairs={{0,1},{1,2},{2,3},{3,4},{4,5},{5,6},{6,7},{7,8},{8,9},{9,10},{10,1... | collective-permute-start | bytes 1572872 | tf_op jit(solution)/shard_map/ppermute | solution.py:34
  50.3 20.2 %collective-permute-start.2 = (bf16[256,1024]{1,0:T(8,128)(2,1)S(1)}, bf16[256,1024]{1,0:T(8,128)(2,1)S(1)}, u32[]{:S(2)}, u32[]{:S(2)}) collective-permute-start(bf16[256,1024]{1,0:T(8,128)(2,1)S(1)} %get-tuple-element.48), channel_id=1, source_target_pairs={{0,1},{1,2},{2,3},{3,4},{4,5},{5,6},{6,7},{7,8},{8,9},{9,10},{10,1... | collective-permute-start | bytes 1572872 | tf_op jit(solution)/shard_map/ppermute | solution.py:34
  55.5 15.1 %collective-permute-start.3 = (bf16[256,1024]{1,0:T(8,128)(2,1)S(1)}, bf16[256,1024]{1,0:T(8,128)(2,1)S(1)}, u32[]{:S(2)}, u32[]{:S(2)}) collective-permute-start(bf16[256,1024]{1,0:T(8,128)(2,1)S(1)} %get-tuple-element.49), channel_id=1, source_target_pairs={{0,31},{1,0},{2,1},{3,2},{4,3},{5,4},{6,5},{7,6},{8,7},{9,8},{10,9... | collective-permute-start | bytes 1572872 | tf_op jit(solution)/shard_map/ppermute | solution.py:34

commit v12 on v11

--- a/solution.py
+++ b/solution.py
@@ -245,9 +245,7 @@
     pred = pred_ref[...]
     fold_ref[...] = fold(sent_ref[...])
     lead = weight_ref[...] * smooth_slope(pred - target_ref[...])
-    core, chip = lax.rem(me, 2), me // 2
-    others = [(core, lax.rem(chip + step, chips)) for step in range(1, chips)]
-    others += [(1 - core, step) for step in range(chips)]
+    others = [(core, chip) for core in range(2) for chip in range(chips)]
     parts = pair_parts(everyone_ref, others, fold_ref, scale_ref)
     pair_sum = unfold(jnp.concatenate(parts, axis=0), grid_rows)
     real = lanes_of(pair_sum) < VARS
@@ -501,7 +499,7 @@
         out_shape=[pltpu.HBM((mesh_rows, width), b16), pltpu.HBM(share.shape, b16)],
         in_specs=[VMEM] * 4,
         out_specs=[HBM, HBM],
-        scratch_shapes=[pltpu.VMEM((mesh_rows, width), b16), held(share), dma((4,)), dma],
+        scratch_shapes=[pltpu.VMEM((mesh_rows, width), b16), held(share), dma((8,)), dma],
         compiler_params=PARAMS,
         cost_estimate=cost_of(1, 3),
     )(own_part, first_back, second_back, landed)

time: 71.9 us -> 71.9 us (level)
  no operation moved by 1% of the time
where the time goes in v12:
time: 71.9 us; the launch traced here: 71.6 us
  blocking collectives  32.5 us (45%)
  starting transfers between devices  22 us (31%)
  Pallas kernels  8.24 us (11%)
  waiting for transfers between devices  8.15 us (11%)
    ppermute x4, starting transfers between devices, to_neighbours(): return lax.ppermute(value, ('member', 'grid'), pairs)  22 us
    all_to_all x1, blocking collectives, per_device(): lax.all_to_all(shared, 'member', 0, 0, axis_index_groups=cores, tiled=True)  14.8 us
    all_to_all x1, blocking collectives, per_device(): lax.all_to_all(blocks, 'member', 0, 0, axis_index_groups=cores, tiled=True)  10 us
    ppermute x4, waiting for transfers between devices, to_neighbours(): return lax.ppermute(value, ('member', 'grid'), pairs)  8.15 us
    all_gather x1, blocking collectives, per_device(): lax.all_gather(alike, 'member', axis=0, axis_index_groups=pairs, tiled=Fa...  4.65 us
    all_gather x1, blocking collectives, per_device(): lax.all_gather(give, 'member', axis=0, axis_index_groups=pairs, tiled=False)  3 us
    pallas_call x1, Pallas kernels, per_device(): pl.pallas_call(edges_kernel, out_shape=outs, in_specs=[HBM] * len(ins), o...  2.86 us
    pallas_call x1, Pallas kernels, per_device(): pl.pallas_call(functools.partial(backward_kernel, pair_scale=pair_scale),...  2.44 us
  transfers between devices with their start and end apart: 4, of which 3 were waited for; matrix products, arithmetic and copies ran while one was open for 0% of the time, Pallas kernels for 4%

profile of v12, /device:TPU:1, one launch (start us, length us, event | category | flops | bytes accessed | tf_op | source)
XLA Modules:
  0.0 71.6 jit_solution(12797125470864828081)
XLA Ops:
  0.6 4.4 %collective-permute-start = (bf16[256,1024]{1,0:T(8,128)(2,1)}, bf16[256,1024]{1,0:T(8,128)(2,1)S(1)}, u32[]{:S(2)}, u32[]{:S(2)}) collective-permute-start(bf16[256,1024]{1,0:T(8,128)(2,1)} %bitcast.12), channel_id=1, source_target_pairs={{0,31},{1,0},{2,1},{3,2},{4,3},{5,4},{6,5},{7,6},{8,7},{9,8},{10,9... | collective-permute-start | bytes 1572872 | tf_op jit(solution)/shard_map/ppermute | solution.py:34
  5.0 10.5 %collective-permute-start.1 = (bf16[256,1024]{1,0:T(8,128)(2,1)}, bf16[256,1024]{1,0:T(8,128)(2,1)S(1)}, u32[]{:S(2)}, u32[]{:S(2)}) collective-permute-start(bf16[256,1024]{1,0:T(8,128)(2,1)} %bitcast.13), channel_id=1, source_target_pairs={{0,1},{1,2},{2,3},{3,4},{4,5},{5,6},{6,7},{7,8},{8,9},{9,10},{10,1... | collective-permute-start | bytes 1572872 | tf_op jit(solution)/shard_map/ppermute | solution.py:34
  15.5 2.9 %shard_map.113 = (s32[2]{0:T(128)S(4)}, bf16[256,768]{1,0:T(8,128)(2,1)}, bf16[256,768]{1,0:T(8,128)(2,1)}, bf16[256,768]{1,0:T(8,128)(2,1)S(1)}, bf16[256,512]{...) custom-call(s32[1]{0:T(128)} %bitcast.me_hbm, ...), custom_call_target="tpu_custom_call" | custom-call | flops 524288000 | bytes 8388608 | tf_op jit(solution)/shard_map/pallas_call | solution.py:410
  18.4 2.0 %collective-permute-done.rows_ref = bf16[256,1024]{1,0:T(8,128)(2,1)S(1)} collective-permute-done((bf16[256,1024]{1,0:T(8,128)(2,1)}, bf16[256,1024]{1,0:T(8,128)(2,1)S(1)}, u32[]{:S(2)}, u32[]{:S(2)}) %collective-permute-start) | collective-permute-done | bytes 524320 | tf_op jit(solution)/shard_map/ppermute | solution.py:34
  20.4 0.3 shard_map.114.base_ref
  20.7 6.1 %collective-permute-done.1.rows_ref = bf16[256,1024]{1,0:T(8,128)(2,1)S(1)} collective-permute-done((bf16[256,1024]{1,0:T(8,128)(2,1)}, bf16[256,1024]{1,0:T(8,128)(2,1)S(1)}, u32[]{:S(2)}, u32[]{:S(2)}) %collective-permute-start.1) | collective-permute-done | bytes 524320 | tf_op jit(solution)/shard_map/ppermute | solution.py:34
  26.8 1.6 %shard_map.115 = (s16[8,208,128]{2,1,0:T(8,128)(2,1)S(1)}, f32[256,128]{1,0:T(8,128)S(1)}, f32[256,128]{1,0:T(8,128)S(1)}, f32[256,1024]{1,0:T(8,128)S(1)}, f32[...) custom-call(s32[2]{0:T(128)S(4)} %get-tuple-element.28.flags_ref, bf16[256,768]{1,0:T(8,128)(2,1)S(1)} %get-tuple-element.29.high_ref, ...), custom_call_target="tpu_custom_call" | custom-call | flops 1048576000 | bytes 8388608 | tf_op jit(solution)/shard_map/pallas_call | solution.py:441
  28.4 14.8 %all_to_all.10 = s16[8,208,128]{2,1,0:T(8,128)(2,1)S(1)} all-to-all(s16[8,208,128]{2,1,0:T(8,128)(2,1)S(1)} %get-tuple-element.34), channel_id=1, replica_groups={{0,64,128,192,256,320,384,448},{32,96,160,224,288,352,416,480},{1,65,12..., dimensions={0} | all-to-all | bytes 851968 | tf_op jit(solution)/shard_map/all_to_all | solution.py:454
  43.2 4.7 %all-gather = s16[16,208,128]{2,1,0:T(8,128)(2,1)S(1)} all-gather(s16[8,208,128]{2,1,0:T(8,128)(2,1)S(1)} %all_to_all.10), channel_id=2, replica_groups={{0,32},{64,96},{128,160},{192,224},{256,288},{320,352},{384,416},{448,4..., dimensions={0}, use_global_device_ids=true | all-gather | bytes 1277952 | tf_op jit(solution)/shard_map/all_gather | solution.py:455
  47.9 2.4 %shard_map.116 = (f32[8,128,128]{2,1,0:T(8,128)S(1)}, bf16[8,128,128]{2,1,0:T(8,128)(2,1)S(1)}, bf16[256,1024]{1,0:T(8,128)(2,1)S(1)}, bf16[256,1024]{1,0:T(8,128)(2,1)S(1)}, f32[256,1024]{1,0:T(8,128)S(1)}) custom-call(s32[2]{0:T(128)S(4)} %get-tuple-element.28.flags_ref, s16[2,8,208,128]{3,2,1,0:T(8,128)(2,1)S(1)} %bitcast.10, ...), custom_call_target="tpu_custom_call" | custom-call | flops 1048576000 | bytes 8388608 | tf_op jit(solution)/shard_map/pallas_call | solution.py:464
  50.3 5.2 %collective-permute-start.2 = (bf16[256,1024]{1,0:T(8,128)(2,1)S(1)}, bf16[256,1024]{1,0:T(8,128)(2,1)S(1)}, u32[]{:S(2)}, u32[]{:S(2)}) collective-permute-start(bf16[256,1024]{1,0:T(8,128)(2,1)S(1)} %get-tuple-element.48), channel_id=1, source_target_pairs={{0,1},{1,2},{2,3},{3,4},{4,5},{5,6},{6,7},{7,8},{8,9},{9,10},{10,1... | collective-permute-start | bytes 1572872 | tf_op jit(solution)/shard_map/ppermute | solution.py:34
  55.6 1.9 %collective-permute-start.3 = (bf16[256,1024]{1,0:T(8,128)(2,1)S(1)}, bf16[256,1024]{1,0:T(8,128)(2,1)S(1)}, u32[]{:S(2)}, u32[]{:S(2)}) collective-permute-start(bf16[256,1024]{1,0:T(8,128)(2,1)S(1)} %get-tuple-element.49), channel_id=1, source_target_pairs={{0,31},{1,0},{2,1},{3,2},{4,3},{5,4},{6,5},{7,6},{8,7},{9,8},{10,9... | collective-permute-start | bytes 1572872 | tf_op jit(solution)/shard_map/ppermute | solution.py:34
  57.5 3.0 %all-gather.1 = bf16[16,128,128]{2,1,0:T(8,128)(2,1)S(1)} all-gather(bf16[8,128,128]{2,1,0:T(8,128)(2,1)S(1)} %get-tuple-element.51), channel_id=3, replica_groups={{0,32},{64,96},{128,160},{192,224},{256,288},{320,352},{384,416},{448,4..., dimensions={0}, use_global_device_ids=true | all-gather | bytes 786432 | tf_op jit(solution)/shard_map/all_gather | solution.py:484
  60.5 10.0 %all_to_all.11.landed_ref = bf16[8,128,128]{2,1,0:T(8,128)(2,1)S(1)} all-to-all(bf16[8,128,128]{2,1,0:T(8,128)(2,1)S(1)} %shard_map.117), channel_id=1, replica_groups={{0,64,128,192,256,320,384,448},{32,96,160,224,288,352,416,480},{1,65,12..., dimensions={0} | all-to-all | bytes 524288 | tf_op jit(solution)/shard_map/all_to_all | solution.py:495
  70.6 0.0 collective-permute-done.2.first_ref
  70.6 0.1 collective-permute-done.3.second_ref
  70.7 0.9 %shard_map.118 = (bf16[256,1024]{1,0:T(8,128)(2,1)}, bf16[64,256]{1,0:T(8,128)(2,1)}) custom-call(f32[256,1024]{1,0:T(8,128)S(1)} %get-tuple-element.47.own_ref, bf16[256,1024]{1,0:T(8,128)(2,1)S(1)} %collective-permute-done.2.first_ref, bf16[256,1024]{1,0:T(8,128)(2,1)S(1)} %collective-permute-done.3.second_ref, bf16[8,128,128]{2,1,0:T(8,128)(2,1)S(1)} %all_to_all.11.landed_ref), custom_call_target="tpu_custom_call" | custom-call | flops 1048576 | bytes 3145728 | tf_op jit(solution)/shard_map/pallas_call | solution.py:497
  (1 shorter events, 0.0 us)
Async XLA Ops:
  0.6 19.7 %collective-permute-start = (bf16[256,1024]{1,0:T(8,128)(2,1)}, bf16[256,1024]{1,0:T(8,128)(2,1)S(1)}, u32[]{:S(2)}, u32[]{:S(2)}) collective-permute-start(bf16[256,1024]{1,0:T(8,128)(2,1)} %bitcast.12), channel_id=1, source_target_pairs={{0,31},{1,0},{2,1},{3,2},{4,3},{5,4},{6,5},{7,6},{8,7},{9,8},{10,9... | collective-permute-start | bytes 1572872 | tf_op jit(solution)/shard_map/ppermute | solution.py:34
  5.0 21.8 %collective-permute-start.1 = (bf16[256,1024]{1,0:T(8,128)(2,1)}, bf16[256,1024]{1,0:T(8,128)(2,1)S(1)}, u32[]{:S(2)}, u32[]{:S(2)}) collective-permute-start(bf16[256,1024]{1,0:T(8,128)(2,1)} %bitcast.13), channel_id=1, source_target_pairs={{0,1},{1,2},{2,3},{3,4},{4,5},{5,6},{6,7},{7,8},{8,9},{9,10},{10,1... | collective-permute-start | bytes 1572872 | tf_op jit(solution)/shard_map/ppermute | solution.py:34
  50.3 20.2 %collective-permute-start.2 = (bf16[256,1024]{1,0:T(8,128)(2,1)S(1)}, bf16[256,1024]{1,0:T(8,128)(2,1)S(1)}, u32[]{:S(2)}, u32[]{:S(2)}) collective-permute-start(bf16[256,1024]{1,0:T(8,128)(2,1)S(1)} %get-tuple-element.48), channel_id=1, source_target_pairs={{0,1},{1,2},{2,3},{3,4},{4,5},{5,6},{6,7},{7,8},{8,9},{9,10},{10,1... | collective-permute-start | bytes 1572872 | tf_op jit(solution)/shard_map/ppermute | solution.py:34
  55.6 15.1 %collective-permute-start.3 = (bf16[256,1024]{1,0:T(8,128)(2,1)S(1)}, bf16[256,1024]{1,0:T(8,128)(2,1)S(1)}, u32[]{:S(2)}, u32[]{:S(2)}) collective-permute-start(bf16[256,1024]{1,0:T(8,128)(2,1)S(1)} %get-tuple-element.49), channel_id=1, source_target_pairs={{0,31},{1,0},{2,1},{3,2},{4,3},{5,4},{6,5},{7,6},{8,7},{9,8},{10,9... | collective-permute-start | bytes 1572872 | tf_op jit(solution)/shard_map/ppermute | solution.py:34
